TPU v7x, 128 devices: a whole 4x4x4 slice. The times are simulated.
128 devices in a mesh: dp: 32 (over x_hi, y, z), vocab: 4 (over x_lo, core).
Axes of the slice: x: 4 (x_hi: 2, x_lo: 2; x = x_hi * 2 + x_lo), y: 4, z: 4, core: 2. Of those that a mesh axis runs over, the one named last changes fastest.
Arguments:
- token_ids: int32 [2, 8192], P(None, ('dp', 'vocab')), may hold values from 0 to 50264
- box_coords: int32 [4, 2, 8192], P(None, None, ('dp', 'vocab')), may hold values from 0 to 1023
- intersection_flags: int32 [2, 8192], P(None, ('dp', 'vocab')), may hold values from 0 to 1, as said below
- masked_rows: int32 [2, 1024], P(None, ('dp', 'vocab')), may hold values from 0 to 63, as said below
- masked_labels: int32 [2, 1024], P(None, ('dp', 'vocab')), may hold values from 0 to 50264
- word_table: float32 [768, 50304], P('dp', 'vocab'), may hold values from -0.21650635 to 0.21650635
- word_table_momentum: float32 [768, 50304], P('dp', 'vocab'), may hold values from -1.5258789e-05 to 1.5258789e-05
- word_table_average: float32 [768, 50304], P('dp', 'vocab'), may hold values from -0.4375 to 0.4375
- position_table: float32 [640, 960], P(('dp', 'vocab')), may hold values from -0.4375 to 0.4375
- position_table_momentum: float32 [640, 960], P(('dp', 'vocab')), may hold values from -0.0004272461 to 0.0004272461
- position_table_average: float32 [640, 960], P(('dp', 'vocab')), may hold values from -0.4375 to 0.4375
- box_table: float32 [4, 1024, 128], P(None, ('dp', 'vocab')), may hold values from -0.4375 to 0.4375
- box_table_momentum: float32 [4, 1024, 128], P(None, ('dp', 'vocab')), may hold values from -1.5258789e-05 to 1.5258789e-05
- box_table_average: float32 [4, 1024, 128], P(None, ('dp', 'vocab')), may hold values from -0.4375 to 0.4375
- text_weights: float32 [768, 6144], P(None, ('dp', 'vocab')), may hold values from -0.109375 to 0.109375
- text_weights_momentum: float32 [768, 6144], P(None, ('dp', 'vocab')), may hold values from -1.5258789e-05 to 1.5258789e-05
- text_weights_average: float32 [768, 6144], P(None, ('dp', 'vocab')), may hold values from -0.109375 to 0.109375
- text_down: float32 [3072, 768], P(('dp', 'vocab')), may hold values from -0.109375 to 0.109375
- text_down_momentum: float32 [3072, 768], P(('dp', 'vocab')), may hold values from -1.5258789e-05 to 1.5258789e-05
- text_down_average: float32 [3072, 768], P(('dp', 'vocab')), may hold values from -0.109375 to 0.109375
- layout_weights: float32 [192, 1536], P(None, ('dp', 'vocab')), may hold values from -0.21875 to 0.21875
- layout_weights_momentum: float32 [192, 1536], P(None, ('dp', 'vocab')), may hold values from -1.5258789e-05 to 1.5258789e-05
- layout_weights_average: float32 [192, 1536], P(None, ('dp', 'vocab')), may hold values from -0.21875 to 0.21875
- layout_down: float32 [2, 768, 192], P(None, ('dp', 'vocab')), may hold values from -0.21875 to 0.21875
- layout_down_momentum: float32 [2, 768, 192], P(None, ('dp', 'vocab')), may hold values from -1.5258789e-05 to 1.5258789e-05
- layout_down_average: float32 [2, 768, 192], P(None, ('dp', 'vocab')), may hold values from -0.21875 to 0.21875
- head_dense: float32 [960, 768], P(None, ('dp', 'vocab')), may hold values from -0.1875 to 0.1875
- head_dense_momentum: float32 [960, 768], P(None, ('dp', 'vocab')), may hold values from -1.5258789e-05 to 1.5258789e-05
- head_dense_average: float32 [960, 768], P(None, ('dp', 'vocab')), may hold values from -0.1875 to 0.1875
- norm_vectors: float32 [15744], P(('dp', 'vocab')), may hold values from -1 to 2.4
- norm_vectors_momentum: float32 [15744], P(('dp', 'vocab')), may hold values from -7.6293945e-05 to 7.6293945e-05
- norm_vectors_average: float32 [15744], P(('dp', 'vocab')), may hold values from 0.5 to 1.5
Outputs:
- word_table_next: float32 [768, 50304], P('dp', 'vocab')
- word_table_momentum_next: float32 [768, 50304], P('dp', 'vocab')
- word_table_average_next: float32 [768, 50304], P('dp', 'vocab')
- position_table_next: float32 [640, 960], P(('dp', 'vocab'))
- position_table_momentum_next: float32 [640, 960], P(('dp', 'vocab'))
- position_table_average_next: float32 [640, 960], P(('dp', 'vocab'))
- box_table_next: float32 [4, 1024, 128], P(None, ('dp', 'vocab'))
- box_table_momentum_next: float32 [4, 1024, 128], P(None, ('dp', 'vocab'))
- box_table_average_next: float32 [4, 1024, 128], P(None, ('dp', 'vocab'))
- text_weights_next: float32 [768, 6144], P(None, ('dp', 'vocab'))
- text_weights_momentum_next: float32 [768, 6144], P(None, ('dp', 'vocab'))
- text_weights_average_next: float32 [768, 6144], P(None, ('dp', 'vocab'))
- text_down_next: float32 [3072, 768], P(('dp', 'vocab'))
- text_down_momentum_next: float32 [3072, 768], P(('dp', 'vocab'))
- text_down_average_next: float32 [3072, 768], P(('dp', 'vocab'))
- layout_weights_next: float32 [192, 1536], P(None, ('dp', 'vocab'))
- layout_weights_momentum_next: float32 [192, 1536], P(None, ('dp', 'vocab'))
- layout_weights_average_next: float32 [192, 1536], P(None, ('dp', 'vocab'))
- layout_down_next: float32 [2, 768, 192], P(None, ('dp', 'vocab'))
- layout_down_momentum_next: float32 [2, 768, 192], P(None, ('dp', 'vocab'))
- layout_down_average_next: float32 [2, 768, 192], P(None, ('dp', 'vocab'))
- head_dense_next: float32 [960, 768], P(None, ('dp', 'vocab'))
- head_dense_momentum_next: float32 [960, 768], P(None, ('dp', 'vocab'))
- head_dense_average_next: float32 [960, 768], P(None, ('dp', 'vocab'))
- norm_vectors_next: float32 [15744], P(('dp', 'vocab'))
- norm_vectors_momentum_next: float32 [15744], P(('dp', 'vocab'))
- norm_vectors_average_next: float32 [15744], P(('dp', 'vocab'))
- loss_sum: float32 [], replicated
- masked_count: float32 [], replicated
- grad_norm: float32 [], replicated
Inputs may be any that keep to these rules, and one draw needn't show every extreme that they name: `intersection_flags`: 1 marks a token that a later block of its document already holds; slots at such tokens are not counted. `masked_rows`: in a micro-batch, the 8 entries of one device are distinct rows of that device's block of 64 tokens.
All inputs are finite; a program needn't handle non-finite values.
Results may differ from a plain program's by a relative error of at most 0.017.
Values may be sent and summed in bfloat16 or wider, within the bound.
A program may use at most 320 MiB of HBM per device.

v0:
```python
import functools

import jax
import jax.numpy as jnp
from jax import lax
from jax.experimental import pallas as pl
from jax.experimental.pallas import tpu as pltpu
from jax.sharding import PartitionSpec as P

AXES = ("dp", "vocab")
MESH = pl.DeviceIdType.MESH
LONG = pl.CostEstimate(flops=60_000_000_000, bytes_accessed=200_000_000, transcendentals=0)
ORDERS = (("z", "y", "x"), ("y", "x", "z"), ("x", "z", "y"))


def my_place():
    dp = lax.axis_index("dp")
    vocab = lax.axis_index("vocab")
    return {
        "x": (dp // 16) * 2 + vocab // 2,
        "y": (dp // 4) % 4,
        "z": dp % 4,
        "c": vocab % 2,
    }


def moved(place, dim, step):
    other = dict(place)
    other[dim] = (1 - place["c"]) if dim == "c" else (place[dim] + step + 4) % 4
    return other


def device_of(place):
    return (
        (place["x"] // 2) * 16 + place["y"] * 4 + place["z"],
        (place["x"] % 2) * 2 + place["c"],
    )


def greet(place, steps=(1, 3)):
    barrier = pltpu.get_barrier_semaphore()
    peers = [moved(place, dim, step) for dim in "xyz" for step in steps]
    peers.append(moved(place, "c", 1))
    for peer in peers:
        pl.semaphore_signal(barrier, inc=1, device_id=device_of(peer), device_id_type=MESH)
    pl.semaphore_wait(barrier, len(peers))


def remote(src, dst, send, recv, place):
    return pltpu.make_async_remote_copy(
        src_ref=src,
        dst_ref=dst,
        send_sem=send,
        recv_sem=recv,
        device_id=device_of(place),
        device_id_type=MESH,
    )


def lanes_at(ref, lanes):
    return slice(None) if lanes is None else pl.ds(*lanes)


def block_view(ref, place, dims, lanes, core=None):
    high, low = (pl.ds(0, 2), pl.ds(0, 2)) if "x" in dims else (place["x"] // 2, place["x"] % 2)
    mid = pl.ds(0, 4) if "y" in dims else place["y"]
    deep = pl.ds(0, 4) if "z" in dims else place["z"]
    where = (high, mid, deep, low)
    if core is not None:
        where += (core,)
    return ref.at[where + (slice(None), lanes_at(ref, lanes))]


def halves(lanes, number):
    if lanes is None or lanes[1] < 256:
        return (lanes, False) if number % 2 == 0 else (False, lanes)
    half = lanes[1] // 256 * 128
    return (lanes[0], half), (lanes[0] + half, lanes[1] - half)


def gather_kernel(pieces, count, *refs):
    ins, outs = refs[:count], refs[count : 2 * count]
    own_sem, core_sems, ring_send, ring_recv, pass_send, pass_recv = refs[2 * count :]
    place = my_place()
    sibling = moved(place, "c", 1)
    greet(place)

    def spot(number, origin, dims, lanes):
        return block_view(outs[number], origin, dims, lanes, place["c"])

    copies, crosses = [], []
    for number in range(count):
        here = block_view(outs[number], place, "", None, place["c"])
        copy = pltpu.make_async_copy(ins[number], here, own_sem.at[number])
        copy.start()
        copies.append(copy)
        cross = remote(ins[number], here, core_sems.at[0, number], core_sems.at[1, number], sibling)
        cross.start()
        crosses.append(cross)
    rings, passes = {}, []

    def send(phase, piece, way, src, dst, target):
        copy = remote(
            src, dst, ring_send.at[phase, way, piece], ring_recv.at[phase, way, piece], target
        )
        copy.start()
        rings[(phase, way, piece)] = copy

    def hand_over(phase, piece, way, where):
        copy = remote(
            where, where, pass_send.at[phase, way, piece], pass_recv.at[phase, way, piece], sibling
        )
        copy.start()
        passes.append(copy)

    def begin(phase, piece):
        number, lanes, order = pieces[piece]
        dim, dims = ORDERS[order][phase], ORDERS[order][:phase]
        where = spot(number, place, dims, lanes)
        src = ins[number].at[:, lanes_at(ins[number], lanes)] if phase == 0 else where
        for way, step in ((0, 1), (1, -1)):
            send(phase, piece, way, src, where, moved(place, dim, step))

    for piece in range(len(pieces)):
        begin(0, piece)
    for copy in copies:
        copy.wait()
    for phase in range(3):
        for piece, (number, lanes, order) in enumerate(pieces):
            dim, dims = ORDERS[order][phase], ORDERS[order][:phase]
            parts = halves(lanes, piece)
            for way, step in ((0, 1), (1, -1)):
                rings[(phase, way, piece)].wait_recv()
                origin = moved(place, dim, -step)
                if parts[way] is not False:
                    onward = spot(number, origin, dims, parts[way])
                    send(phase, piece, 2 + way, onward, onward, moved(place, dim, step))
                hand_over(phase, piece, way, spot(number, origin, dims, lanes))
        for piece, (number, lanes, order) in enumerate(pieces):
            dim, dims = ORDERS[order][phase], ORDERS[order][:phase]
            parts = halves(lanes, piece)
            for way in range(2):
                if parts[way] is not False:
                    rings[(phase, 2 + way, piece)].wait_recv()
            if phase < 2:
                begin(phase + 1, piece)
            hand_over(phase, piece, 2, spot(number, moved(place, dim, 2), dims, lanes))
    for copy in rings.values():
        copy.wait_send()
    for copy in crosses + passes:
        copy.wait()


def gather_all(arrays, pieces, collective_id):
    count, total = len(arrays), len(pieces)
    outs = pl.pallas_call(
        functools.partial(gather_kernel, pieces, count),
        out_shape=[jax.ShapeDtypeStruct((2, 4, 4, 2, 2) + a.shape, a.dtype) for a in arrays],
        in_specs=[pl.BlockSpec(memory_space=pl.ANY)] * count,
        out_specs=[pl.BlockSpec(memory_space=pl.ANY)] * count,
        scratch_shapes=[
            pltpu.SemaphoreType.DMA((count,)),
            pltpu.SemaphoreType.DMA((2, count)),
            pltpu.SemaphoreType.DMA((3, 4, total)),
            pltpu.SemaphoreType.DMA((3, 4, total)),
            pltpu.SemaphoreType.DMA((3, 3, total)),
            pltpu.SemaphoreType.DMA((3, 3, total)),
        ],
        cost_estimate=LONG,
        compiler_params=pltpu.CompilerParams(collective_id=collective_id, has_side_effects=True),
    )(*arrays)
    return [o.reshape((128,) + a.shape) for o, a in zip(outs, arrays)]


def open_shape(dims):
    shape = ()
    if "x" in dims:
        shape += (2,)
    if "y" in dims:
        shape += (4,)
    if "z" in dims:
        shape += (4,)
    if "x" in dims:
        shape += (2,)
    return shape


def chunks_of(dims, place):
    high, mid, deep, low = place["x"] // 2, place["y"], place["z"], place["x"] % 2
    every = slice(None)
    if dims == "":
        return 1, lambda flat: ((high, mid, deep, low), ())
    inner = (every if "y" in dims else mid, every if "z" in dims else deep)
    if "x" in dims and "y" in dims and "z" in dims:
        return 8, lambda flat: ((flat // 4, flat % 4, every, every), (flat // 4, flat % 4))
    if "x" in dims:
        return 2, lambda flat: ((flat,) + inner + (every,), (flat,))
    if "y" in dims and "z" in dims:
        return 4, lambda flat: ((high, flat, every, low), (flat,))
    return 1, lambda flat: ((high,) + inner + (low,), ())


def reduce_kernel(sources, pieces, count, *refs):
    total = len(pieces)
    ins = refs[: len(sources)]
    refs = refs[len(sources) :]
    outs, square_ref, refs = refs[:count], refs[count], refs[count + 1 :]
    accs, crosses, refs = refs[:count], refs[count : 2 * count], refs[2 * count :]
    slots = refs[: 12 * total]
    own_sem, core_sems, ring_send, ring_recv = refs[12 * total :]
    place = my_place()
    sibling = moved(place, "c", 1)
    greet(place)

    def slot(phase, way, piece):
        return slots[(phase * 4 + way) * total + piece]

    def add(number, lanes, at, dims, others):
        acc = accs[number]

        count, chunk = chunks_of(dims, at)

        def body(flat, carry):
            block, inner = chunk(flat)
            where = block + (slice(None), lanes_at(acc, lanes))
            parts = [
                other[inner] if index is None else other[block + index] for other, index in others
            ]
            if len(parts) == 1:
                acc[where] = acc[where] + parts[0]
            else:
                wide = [part.astype(jnp.float32) for part in [acc[where]] + parts]
                acc[where] = sum(wide).astype(acc.dtype)
            return carry

        if count == 1:
            body(0, 0)
        else:
            lax.fori_loop(0, count, body, 0)

    started = []
    first = {}
    for piece, (number, lanes, order) in enumerate(pieces):
        for index, (owner, high, mids) in enumerate(sources):
            if owner != number:
                continue
            copies = []
            for core, target in ((sibling["c"], "cross"), (place["c"], "own")):
                where = (slice(None), slice(None), slice(None), slice(None), core)
                src = ins[index].at[where + (slice(None), lanes_at(ins[index], lanes))]
                at = (
                    pl.ds(*high),
                    pl.ds(*mids),
                    slice(None),
                    slice(None),
                    slice(None),
                    lanes_at(accs[number], lanes),
                )
                if target == "cross":
                    copy = remote(
                        src,
                        crosses[number].at[at],
                        core_sems.at[0, piece, index],
                        core_sems.at[1, piece, index],
                        sibling,
                    )
                else:
                    copy = pltpu.make_async_copy(src, accs[number].at[at], own_sem.at[piece, index])
                copy.start()
                copies.append(copy)
            started.append(copies[0])
            first.setdefault(piece, []).append(copies)
    rings = {}

    def send(phase, way, piece, src, step):
        number, lanes, order = pieces[piece]
        copy = remote(
            src,
            slot(phase, way, piece),
            ring_send.at[phase, way, piece],
            ring_recv.at[phase, way, piece],
            moved(place, ORDERS[order][phase], step),
        )
        copy.start()
        rings[(phase, way, piece)] = copy
        started.append(copy)

    def begin(phase, piece):
        number, lanes, order = pieces[piece]
        dim, rest = ORDERS[order][phase], ORDERS[order][phase + 1 :]
        parts = halves(lanes, piece)
        for way, step in ((0, 1), (1, -1)):
            if parts[way] is not False:
                there = moved(place, dim, 2)
                send(phase, way, piece, block_view(accs[number], there, rest, parts[way]), step)

    for piece, (number, lanes, order) in enumerate(pieces):
        for cross, own in first[piece]:
            own.wait()
            cross.wait_recv()
        add(number, lanes, place, "xyz", [(crosses[number], (slice(None), lanes_at(accs[number], lanes)))])
        begin(0, piece)
    for phase in range(3):
        for piece, (number, lanes, order) in enumerate(pieces):
            dim, rest = ORDERS[order][phase], ORDERS[order][phase + 1 :]
            parts = halves(lanes, piece)
            for way, step in ((0, 1), (1, -1)):
                there = moved(place, dim, step)
                if parts[way] is not False:
                    rings[(phase, way, piece)].wait_recv()
                    add(number, parts[way], there, rest, [(slot(phase, way, piece), None)])
                send(phase, 2 + way, piece, block_view(accs[number], there, rest, lanes), step)
        for piece, (number, lanes, order) in enumerate(pieces):
            rest = ORDERS[order][phase + 1 :]
            for way in range(2):
                rings[(phase, 2 + way, piece)].wait_recv()
            others = [slot(phase, 2 + way, piece) for way in range(2)]
            if phase < 2:
                add(number, lanes, place, rest, [(other, None) for other in others])
                begin(phase + 1, piece)
            else:
                block = (place["x"] // 2, place["y"], place["z"], place["x"] % 2)
                where = (slice(None), lanes_at(accs[number], lanes))
                value = accs[number][block + where].astype(jnp.float32)
                for other in others:
                    value = value + other[...].astype(jnp.float32)
                outs[number][where] = value
    total_square = jnp.zeros((1, 1), jnp.float32)
    for number in range(count):
        value = outs[number][...]
        total_square = total_square + jnp.sum(
            jnp.sum(value * value, 1, keepdims=True), 0, keepdims=True
        )
    square_ref[...] = jnp.broadcast_to(total_square, square_ref.shape)
    for copy in started:
        copy.wait_send()


def reduce_all(arrays, sources, pieces, collective_id):
    shapes = {}
    views = []
    for array, (owner, high, mids) in zip(arrays, sources):
        shapes[owner] = array.shape[1:]
        views.append(array.reshape((high[1], mids[1], 4, 2, 2) + array.shape[1:]))
    count, total = len(shapes), len(pieces)
    dtype = arrays[0].dtype
    scratch = [pltpu.VMEM((2, 4, 4, 2) + shapes[n], dtype) for n in range(count)] * 2
    for phase in range(3):
        for way in range(4):
            for piece, (number, lanes, order) in enumerate(pieces):
                rest = ORDERS[order][phase + 1 :]
                rows, width = shapes[number]
                part = halves(lanes, piece)[way] if way < 2 else lanes
                if part is False:
                    scratch.append(pltpu.VMEM((8, 128), dtype))
                else:
                    wide = width if part is None else part[1]
                    scratch.append(pltpu.VMEM(open_shape(rest) + (rows, wide), dtype))
    scratch += [
        pltpu.SemaphoreType.DMA((total, len(arrays))),
        pltpu.SemaphoreType.DMA((2, total, len(arrays))),
        pltpu.SemaphoreType.DMA((3, 4, total)),
        pltpu.SemaphoreType.DMA((3, 4, total)),
    ]
    return pl.pallas_call(
        functools.partial(reduce_kernel, sources, pieces, count),
        out_shape=[
            jax.ShapeDtypeStruct(shape, jnp.float32)
            for shape in [shapes[n] for n in range(count)] + [(16, 128)]
        ],
        in_specs=[pl.BlockSpec(memory_space=pl.ANY)] * len(arrays),
        out_specs=[pl.BlockSpec(memory_space=pltpu.VMEM)] * (count + 1),
        scratch_shapes=scratch,
        cost_estimate=LONG,
        compiler_params=pltpu.CompilerParams(
            collective_id=collective_id, has_side_effects=True, vmem_limit_bytes=56 * 1024 * 1024
        ),
    )(*views)


def blocks_in(dims):
    total = 1
    for size in open_shape(dims):
        total *= size
    return total


def view(ref, place, open_dims, rows):
    start, count = rows
    if "x" in open_dims:
        high, low = pl.ds(0, 2), pl.ds(0, 2)
    else:
        high, low = place["x"] // 2, place["x"] % 2
    mid = pl.ds(0, 4) if "y" in open_dims else place["y"]
    deep = pl.ds(0, 4) if "z" in open_dims else place["z"]
    core = pl.ds(0, 2) if "c" in open_dims else place["c"]
    return ref.at[high, mid, deep, low, core, pl.ds(start, count), :]


def slot_gather_kernel(pieces, count, *refs):
    ins, outs = refs[:count], refs[count : 2 * count]
    own_sem, core_send, core_recv, ring_send, ring_recv, pass_send, pass_recv = refs[2 * count :]
    place = my_place()
    sibling = moved(place, "c", 1)
    greet(place, (1, 2, 3))


    closing = []
    locals_ = []
    for number in range(count):
        whole = (0, ins[number].shape[0])
        copy = pltpu.make_async_copy(ins[number], view(outs[number], place, "", whole), own_sem.at[number])
        copy.start()
        locals_.append(copy)
        cross = remote(ins[number], view(outs[number], place, "", whole),
                       core_send.at[number], core_recv.at[number], sibling)
        cross.start()
        closing.append(cross)
    started = {}
    forwarded = []

    def land(phase):
        for split, pieces_of in enumerate(pieces):
            order = ORDERS[split]
            dim = order[phase]
            for step in (1, 2, 3):
                origin = moved(place, dim, -step)
                for index, (number, rows) in pieces_of:
                    started[(phase, split, step, index)].wait_recv()
                    spot = view(outs[number], origin, order[:phase], rows)
                    onward = remote(spot, spot, pass_send.at[phase, step - 1, index],
                                    pass_recv.at[phase, step - 1, index], sibling)
                    onward.start()
                    forwarded.append(onward)

    for phase in range(3):
        if phase:
            land(phase - 1)
        for split, pieces_of in enumerate(pieces):
            order = ORDERS[split]
            dim = order[phase]
            for step in (1, 2, 3):
                target = moved(place, dim, step)
                for index, (number, rows) in pieces_of:
                    spot = view(outs[number], place, order[:phase], rows)
                    src = ins[number].at[pl.ds(*rows), :] if phase == 0 else spot
                    copy = remote(src, spot, ring_send.at[phase, step - 1, index],
                                  ring_recv.at[phase, step - 1, index], target)
                    copy.start()
                    started[(phase, split, step, index)] = copy
        if phase == 0:
            for copy in locals_:
                copy.wait()
    land(2)
    for copy in started.values():
        copy.wait_send()
    for copy in forwarded + closing:
        copy.wait()


def number_pieces(splits):
    index = 0
    result = []
    for split in splits:
        rows = []
        for piece in split:
            rows.append((index, piece))
            index += 1
        result.append(rows)
    return result, index


def gather_slots(arrays, splits, collective_id):
    pieces, total = number_pieces(splits)
    count = len(arrays)
    outs = pl.pallas_call(
        functools.partial(slot_gather_kernel, pieces, count),
        out_shape=[jax.ShapeDtypeStruct((2, 4, 4, 2, 2) + a.shape, a.dtype) for a in arrays],
        in_specs=[pl.BlockSpec(memory_space=pl.ANY)] * count,
        out_specs=[pl.BlockSpec(memory_space=pl.ANY)] * count,
        scratch_shapes=[
            pltpu.SemaphoreType.DMA((count,)),
            pltpu.SemaphoreType.DMA((count,)),
            pltpu.SemaphoreType.DMA((count,)),
            pltpu.SemaphoreType.DMA((3, 3, total)),
            pltpu.SemaphoreType.DMA((3, 3, total)),
            pltpu.SemaphoreType.DMA((3, 3, total)),
            pltpu.SemaphoreType.DMA((3, 3, total)),
        ],
        compiler_params=pltpu.CompilerParams(collective_id=collective_id, has_side_effects=True),
    )(*arrays)
    return [o.reshape((128,) + a.shape) for o, a in zip(outs, arrays)]


def block_at(ref, place, dims, rows, lead=()):
    start, count = rows
    high, low = (pl.ds(0, 2), pl.ds(0, 2)) if "x" in dims else (place["x"] // 2, place["x"] % 2)
    mid = pl.ds(0, 4) if "y" in dims else place["y"]
    deep = pl.ds(0, 4) if "z" in dims else place["z"]
    return ref.at[high, mid, deep, low, pl.ds(start, count), :]


def spot_of(flat, dims, place):
    spot = {"xh": place["x"] // 2, "y": place["y"], "z": place["z"], "xl": place["x"] % 2}
    if "x" in dims:
        spot["xl"] = flat % 2
        flat = flat // 2
    if "z" in dims:
        spot["z"] = flat % 4
        flat = flat // 4
    if "y" in dims:
        spot["y"] = flat % 4
        flat = flat // 4
    if "x" in dims:
        spot["xh"] = flat
    return spot


def open_index(spot, dims):
    index = ()
    if "x" in dims:
        index += (spot["xh"],)
    if "y" in dims:
        index += (spot["y"],)
    if "z" in dims:
        index += (spot["z"],)
    if "x" in dims:
        index += (spot["xl"],)
    return index


def slot_reduce_kernel(pieces, count, total, *refs):
    ins, outs = refs[:count], refs[count : 2 * count]
    refs = refs[2 * count :]
    accs, crosses = refs[:count], refs[count : 2 * count]
    rings = [refs[2 * count + phase * total : 2 * count + (phase + 1) * total] for phase in range(3)]
    own_sem, core_send, core_recv, ring_send, ring_recv = refs[2 * count + 3 * total :]
    place = my_place()
    sibling = moved(place, "c", 1)
    greet(place, (1, 2, 3))


    def add_into(number, rows, place, dims, others):
        start, length = rows
        acc = accs[number]

        def body(flat, carry):
            spot = spot_of(flat, dims, place)
            where = (spot["xh"], spot["y"], spot["z"], spot["xl"], pl.ds(start, length), slice(None))
            value = acc[where].astype(jnp.float32)
            for other in others:
                value = value + other(spot)
            acc[where] = value.astype(acc.dtype)
            return carry

        lax.fori_loop(0, blocks_in(dims), body, 0)

    crossing = {}
    for split, pieces_of in enumerate(pieces):
        for index, (number, rows) in pieces_of:
            cross = remote(
                view(ins[number], sibling, "xyz", rows),
                block_at(crosses[number], place, "xyz", rows),
                core_send.at[index], core_recv.at[index], sibling,
            )
            cross.start()
            own = pltpu.make_async_copy(
                view(ins[number], place, "xyz", rows),
                block_at(accs[number], place, "xyz", rows),
                own_sem.at[index],
            )
            own.start()
            crossing[index] = (cross, own)
    sends = []
    rounds = {}

    def launch(phase, split, pieces_of):
        order = ORDERS[split]
        dim = order[phase]
        rest = "".join(order[phase + 1 :])
        for step in (1, 2, 3):
            there = moved(place, dim, step)
            target = there
            for index, (number, rows) in pieces_of:
                copy = remote(
                    block_at(accs[number], there, rest, rows),
                    rings[phase][index].at[step - 1],
                    ring_send.at[phase, step - 1, index],
                    ring_recv.at[phase, step - 1, index],
                    target,
                )
                copy.start()
                rounds[(phase, step, index)] = copy

    for split, pieces_of in enumerate(pieces):
        for index, (number, rows) in pieces_of:
            cross, own = crossing[index]
            own.wait()
            cross.wait_recv()
            start, length = rows

            def other(spot, number=number, start=start, length=length):
                return crosses[number][spot["xh"], spot["y"], spot["z"], spot["xl"], pl.ds(start, length), :].astype(jnp.float32)

            add_into(number, rows, place, "xyz", [other])
        launch(0, split, pieces_of)
    for phase in range(3):
        for split, pieces_of in enumerate(pieces):
            order = ORDERS[split]
            rest = "".join(order[phase + 1 :])
            for index, (number, rows) in pieces_of:
                others = []
                for step in (1, 2, 3):
                    rounds[(phase, step, index)].wait_recv()

                    def other(spot, step=step, index=index, rest=rest):
                        return rings[phase][index][(step - 1,) + open_index(spot, rest)].astype(jnp.float32)

                    others.append(other)
                if phase < 2:
                    add_into(number, rows, place, rest, others)
                else:
                    start, length = rows
                    spot = spot_of(0, "", place)
                    value = accs[number][spot["xh"], spot["y"], spot["z"], spot["xl"], pl.ds(start, length), :].astype(jnp.float32)
                    for item in others:
                        value = value + item(spot)
                    outs[number][pl.ds(start, length), :] = value
            if phase < 2:
                launch(phase + 1, split, pieces_of)
    for cross, own in crossing.values():
        cross.wait_send()
    for copy in rounds.values():
        copy.wait_send()


def reduce_slots(arrays, splits, collective_id):
    pieces, total = number_pieces(splits)
    count = len(arrays)
    shapes = [a.shape[1:] for a in arrays]
    dtype = arrays[0].dtype
    arrays = [a.reshape((2, 4, 4, 2, 2) + s) for a, s in zip(arrays, shapes)]
    scratch = [pltpu.VMEM((2, 4, 4, 2) + s, dtype) for s in shapes] * 2
    for phase in range(3):
        for split, pieces_of in enumerate(pieces):
            rest = "".join(ORDERS[split][phase + 1 :])
            for index, (number, rows) in pieces_of:
                scratch.append(pltpu.VMEM((3,) + open_shape(rest) + (rows[1], shapes[number][1]), dtype))
    scratch += [
        pltpu.SemaphoreType.DMA((total,)),
        pltpu.SemaphoreType.DMA((total,)),
        pltpu.SemaphoreType.DMA((total,)),
        pltpu.SemaphoreType.DMA((3, 3, total)),
        pltpu.SemaphoreType.DMA((3, 3, total)),
    ]
    return pl.pallas_call(
        functools.partial(slot_reduce_kernel, pieces, count, total),
        out_shape=[jax.ShapeDtypeStruct(s, jnp.float32) for s in shapes],
        in_specs=[pl.BlockSpec(memory_space=pl.ANY)] * count,
        out_specs=[pl.BlockSpec(memory_space=pltpu.VMEM)] * count,
        scratch_shapes=scratch,
        compiler_params=pltpu.CompilerParams(
            collective_id=collective_id, has_side_effects=True, vmem_limit_bytes=56 * 1024 * 1024
        ),
    )(*arrays)


def merge_parts(parts):
    top = parts[0][0]
    for part in parts[1:]:
        top = jnp.maximum(top, part[0])
    total = 0.0
    target = 0.0
    for part in parts:
        total = total + part[1] * jnp.exp(part[0] - top)
        target = target + part[2]
    return top, total, target


def stats_kernel(in_ref, out_ref, core_slots, ring_slots, core_sems, ring_send, ring_recv):
    place = my_place()
    greet(place, (1, 2, 3))

    def parts_of(ref, index):
        return tuple(ref[index, pl.ds(16 * row, 16), :] for row in range(3))

    def put(ref, index, parts):
        for row in range(3):
            ref[index, pl.ds(16 * row, 16), :] = parts[row]

    put(core_slots, place["c"], tuple(in_ref[pl.ds(16 * row, 16), :] for row in range(3)))
    cross = pltpu.make_async_remote_copy(
        src_ref=core_slots.at[place["c"]],
        dst_ref=core_slots.at[place["c"]],
        send_sem=core_sems.at[0],
        recv_sem=core_sems.at[1],
        device_id=device_of(moved(place, "c", 1)),
        device_id_type=pl.DeviceIdType.MESH,
    )
    cross.start()
    cross.wait()
    merged = merge_parts([parts_of(core_slots, number) for number in range(2)])
    for phase, dim in enumerate("xyz"):
        slots = ring_slots.at[phase]
        put(slots, place[dim], merged)
        copies = []
        for step in (1, 2, 3):
            copy = pltpu.make_async_remote_copy(
                src_ref=slots.at[place[dim]],
                dst_ref=slots.at[place[dim]],
                send_sem=ring_send.at[phase, step - 1],
                recv_sem=ring_recv.at[phase, step - 1],
                device_id=device_of(moved(place, dim, step)),
                device_id_type=pl.DeviceIdType.MESH,
            )
            copy.start()
            copies.append(copy)
        for copy in copies:
            copy.wait()
        merged = merge_parts([parts_of(slots, number) for number in range(4)])
    for row in range(3):
        out_ref[pl.ds(16 * row, 16), :] = merged[row]


def merge_stats(stats, collective_id):
    return pl.pallas_call(
        stats_kernel,
        out_shape=jax.ShapeDtypeStruct((48, 128), jnp.float32),
        in_specs=[pl.BlockSpec(memory_space=pltpu.VMEM)],
        out_specs=pl.BlockSpec(memory_space=pltpu.VMEM),
        scratch_shapes=[
            pltpu.VMEM((2, 48, 128), jnp.float32),
            pltpu.VMEM((3, 4, 48, 128), jnp.float32),
            pltpu.SemaphoreType.DMA((2,)),
            pltpu.SemaphoreType.DMA((3, 3)),
            pltpu.SemaphoreType.DMA((3, 3)),
        ],
        compiler_params=pltpu.CompilerParams(collective_id=collective_id, has_side_effects=True),
    )(stats)


MOMENTUM = 0.9
AVERAGE_KEEP = 0.9
RATE = 1500.0
CLIP = 0.05
LOW = jnp.bfloat16
SPAN_LOW = 256
HEAD_BLOCK = 512
TOKEN_BLOCK = 1024


def pick_kernel(levels, rows, table_ref, high_ref, low_ref, out_ref):
    low = low_ref[...]
    high = high_ref[...]
    count = low.shape[1]
    hot = (lax.broadcasted_iota(jnp.int32, (SPAN_LOW, count), 0) == low).astype(LOW)
    total = jnp.zeros((rows, count), jnp.float32)
    group = 5
    for first in range(0, levels, group):
        found = jnp.dot(
            table_ref[pl.ds(first * rows, group * rows), :], hot, preferred_element_type=jnp.float32
        )
        for level in range(group):
            total = total + jnp.where(
                high == first + level, found[level * rows : (level + 1) * rows], 0.0
            )
    value = total.astype(LOW)
    for piece in range(count // 128):
        out_ref[piece] = value[:, piece * 128 : (piece + 1) * 128]


def pick_columns(table_levels, high, low, rows):
    levels = table_levels.shape[0] // rows
    tokens = high.shape[1]
    return pl.pallas_call(
        functools.partial(pick_kernel, levels, rows),
        grid=(tokens // TOKEN_BLOCK,),
        out_shape=jax.ShapeDtypeStruct((tokens // 128, rows, 128), LOW),
        in_specs=[
            pl.BlockSpec(table_levels.shape, lambda step: (0, 0)),
            pl.BlockSpec((1, TOKEN_BLOCK), lambda step: (0, step)),
            pl.BlockSpec((1, TOKEN_BLOCK), lambda step: (0, step)),
        ],
        out_specs=pl.BlockSpec((TOKEN_BLOCK // 128, rows, 128), lambda step: (step, 0, 0)),
        compiler_params=pltpu.CompilerParams(vmem_limit_bytes=32 * 1024 * 1024),
    )(table_levels, high, low)


def spread_kernel(levels, rows, grad_ref, high_ref, low_ref, out_ref, spread_ref):
    step = pl.program_id(0)

    @pl.when(step == 0)
    def _():
        out_ref[...] = jnp.zeros_like(out_ref)

    low = low_ref[...]
    high = high_ref[...]
    count = low.shape[1]
    hot = (lax.broadcasted_iota(jnp.int32, (SPAN_LOW, count), 0) == low).astype(LOW)
    grad = jnp.concatenate([grad_ref[piece] for piece in range(count // 128)], 1).astype(jnp.float32)
    pair = 2
    for first in range(0, levels, pair):
        spread_ref[pl.ds(first * rows, pair * rows), :] = jnp.concatenate(
            [jnp.where(high == first + level, grad, 0.0) for level in range(pair)], 0
        ).astype(LOW)
    group = 10 * rows
    for first in range(0, levels * rows, group):
        out_ref[pl.ds(first, group), :] += lax.dot_general(
            spread_ref[pl.ds(first, group), :],
            hot,
            (((1,), (1,)), ((), ())),
            preferred_element_type=jnp.float32,
        )


def spread_columns(grads, high, low, levels):
    rows = grads.shape[1]
    tokens = high.shape[1]
    return pl.pallas_call(
        functools.partial(spread_kernel, levels, rows),
        grid=(tokens // TOKEN_BLOCK,),
        out_shape=jax.ShapeDtypeStruct((levels * rows, SPAN_LOW), jnp.float32),
        in_specs=[
            pl.BlockSpec((TOKEN_BLOCK // 128, rows, 128), lambda step: (step, 0, 0)),
            pl.BlockSpec((1, TOKEN_BLOCK), lambda step: (0, step)),
            pl.BlockSpec((1, TOKEN_BLOCK), lambda step: (0, step)),
        ],
        out_specs=pl.BlockSpec((levels * rows, SPAN_LOW), lambda step: (0, 0)),
        scratch_shapes=[pltpu.VMEM((levels * rows, TOKEN_BLOCK), LOW)],
        compiler_params=pltpu.CompilerParams(vmem_limit_bytes=32 * 1024 * 1024),
    )(grads, high, low)


HEADS = 12
NORM_EPSILON = 1e-05
ROOT_HALF = 0.5**0.5
PEAK = 0.3989422804014327
WIDTHS = (768, 192)
HEAD_SIZES = (64, 16)
SCALES = (0.125, 0.25)
QUERY_LANES = ((0, 768), (768, 192))
NEGATIVE = -1e30


def plain_product(left, right):
    return jnp.dot(left, right, preferred_element_type=jnp.float32)


def rows_product(left, right):
    return lax.dot_general(
        left, right, (((0,), (0,)), ((), ())), preferred_element_type=jnp.float32
    )


def cols_product(left, right):
    return lax.dot_general(
        left, right, (((1,), (1,)), ((), ())), preferred_element_type=jnp.float32
    )


def exact_product(left, right):
    return jnp.dot(
        left, right, precision=lax.Precision.HIGHEST, preferred_element_type=jnp.float32
    )


def total_rows(values):
    return jnp.sum(values.astype(jnp.float32), 0, keepdims=True)


def normalised(values):
    centred = values - jnp.mean(values, -1, keepdims=True)
    scale = lax.rsqrt(jnp.mean(centred * centred, -1, keepdims=True) + NORM_EPSILON)
    return centred * scale, scale


def norm_apply(values, gain, bias):
    return normalised(values)[0] * gain + bias


def norm_back(values, gain, grad):
    unit, scale = normalised(values)
    inner = grad * gain
    result = scale * (
        inner
        - jnp.mean(inner, -1, keepdims=True)
        - unit * jnp.mean(inner * unit, -1, keepdims=True)
    )
    return result, total_rows(grad * unit), total_rows(grad)


def gelu_value(values):
    return 0.5 * values * (1.0 + lax.erf(values * ROOT_HALF))


def gelu_slope(values):
    return 0.5 * (1.0 + lax.erf(values * ROOT_HALF)) + values * PEAK * jnp.exp(
        -0.5 * values * values
    )


def row_of(ref, row):
    return ref[row : row + 1, :]


def hidden_bias(ref):
    return jnp.concatenate([row_of(ref, row) for row in range(7, 11)], 1)


def head_of(rows, stream):
    lanes = lax.broadcasted_iota(jnp.int32, (rows, WIDTHS[stream]), 1)
    return lanes // HEAD_SIZES[stream]


def stack_heads(values, stream):
    heads = head_of(values.shape[0], stream)
    zero = jnp.zeros_like(values)
    return jnp.concatenate([jnp.where(heads == h, values, zero) for h in range(HEADS)], 0)


def fold_heads(values, stream):
    rows = values.shape[0] // HEADS
    heads = head_of(rows, stream)
    total = jnp.zeros((rows, values.shape[1]), jnp.float32)
    for h in range(HEADS):
        total = total + jnp.where(heads == h, values[h * rows : (h + 1) * rows], 0.0)
    return total


def lane_heads(stream):
    rows = lax.broadcasted_iota(jnp.int32, (128, WIDTHS[stream]), 0)
    return (rows == head_of(128, stream)).astype(jnp.float32)


def head_lanes(stream):
    rows = lax.broadcasted_iota(jnp.int32, (WIDTHS[stream], 128), 0) // HEAD_SIZES[stream]
    return (rows == lax.broadcasted_iota(jnp.int32, (WIDTHS[stream], 128), 1)).astype(jnp.float32)


def stack_columns(values):
    return jnp.concatenate([values[:, h : h + 1] for h in range(HEADS)], 0)


def one_micro_batch(rows):
    row = lax.broadcasted_iota(jnp.int32, (rows, 128), 0)
    key = lax.broadcasted_iota(jnp.int32, (rows, 128), 1)
    return (row // 8) % 2 == key // 64


def coupled_scores(stacks, key_refs):
    return sum(
        cols_product(stacks[n], key_refs[n][...]) * SCALES[n] for n in range(2)
    )


def open_kernel(
    found_ref, position_ref, index_ref, box_ref, proj_ref, qkv_ref, layout_ref,
    text_vec, layout_vec, slot_ref,
    text_sum_ref, layout_sum_ref, spatial_ref, key_text, value_text, key_layout, value_layout,
    query_ref, slot_text, slot_layout,
):
    found = found_ref[...].astype(jnp.float32).reshape(32, 4, 24, 128)
    embedded = (found[:, 0] + found[:, 1] + found[:, 2] + found[:, 3]).reshape(768, 128).T
    place = position_ref[...]
    place = jnp.concatenate([place, place], 0)
    text_sum = embedded + place[:, :768]
    text_sum_ref[...] = text_sum
    tables = (0, 1, 0, 1, 2, 3)
    number = lax.broadcasted_iota(jnp.int32, (128, 1024), 1)
    for k in range(6):
        hot = (number == index_ref[:, k : k + 1]).astype(LOW)
        rows = box_ref[pl.ds(1024 * tables[k], 1024), :]
        spatial_ref[:, pl.ds(128 * k, 128)] = plain_product(hot, rows).astype(LOW)
    layout_sum = place[:, 768:] + plain_product(spatial_ref[...], proj_ref[...])
    layout_sum_ref[...] = layout_sum
    query_ref[...] = jnp.zeros_like(query_ref)
    qkv = qkv_ref[...].reshape(2304, 768)
    weights = (qkv, layout_ref[pl.ds(0, 576), :])
    sums, vecs = (text_sum, layout_sum), (text_vec, layout_vec)
    keys, values, slots = (key_text, key_layout), (value_text, value_layout), (slot_text, slot_layout)
    for n in range(2):
        width, weight, vec = WIDTHS[n], weights[n], vecs[n]
        normed = norm_apply(sums[n], row_of(vec, 0), row_of(vec, 1))
        low = normed.astype(LOW)
        keys[n][...] = cols_product(low, weight[width : 2 * width]).astype(LOW)
        values[n][...] = (cols_product(low, weight[2 * width :]) + row_of(vec, 3)).astype(LOW)
        slot = exact_product(slot_ref[...], normed)
        slots[n][...] = slot
        start, size = QUERY_LANES[n]
        query_ref[:, pl.ds(start, size)] = (
            cols_product(slot.astype(LOW), weight[:width]) + row_of(vec, 2)
        ).astype(LOW)


def score_kernel(query_ref, key_text, value_text, key_layout, value_layout, out_ref):
    stacks = [
        stack_heads(query_ref[:, pl.ds(*QUERY_LANES[n])], n) for n in range(2)
    ]
    mask = one_micro_batch(64 * HEADS)
    scores = jnp.where(mask, coupled_scores(stacks, (key_text, key_layout)), NEGATIVE)
    top = jnp.max(scores, -1, keepdims=True)
    powers = jnp.where(mask, jnp.exp(scores - top), 0.0)
    total = jnp.sum(powers, -1, keepdims=True)
    low = powers.astype(LOW)
    out_ref[:, pl.ds(768, 256)] = jnp.zeros((64, 256), jnp.float32)
    for n, values in enumerate((value_text, value_layout)):
        out_ref[:, pl.ds(*QUERY_LANES[n])] = fold_heads(plain_product(low, values[...]), n)
    lane = lax.broadcasted_iota(jnp.int32, (64, 128), 1)
    tops = jnp.zeros((64, 128), jnp.float32)
    totals = jnp.ones((64, 128), jnp.float32)
    for h in range(HEADS):
        tops = jnp.where(lane == h, top[64 * h : 64 * h + 64], tops)
        totals = jnp.where(lane == h, total[64 * h : 64 * h + 64], totals)
    out_ref[:, pl.ds(1024, 128)] = tops
    out_ref[:, pl.ds(1152, 128)] = totals


def close_kernel(
    parts_ref, slot_text, slot_layout, out_w, up_w, down_w, layout_ref, layout_down,
    text_vec, layout_vec, head_ref, head_vec,
    att_text, att_layout, log_ref, mid_text, mid_layout, pre_text, pre_layout,
    end_text, end_layout, joined_ref, dense_ref, pick0, pick1, pick2,
):
    tops = [parts_ref[j, :, pl.ds(1024, 128)] for j in range(4)]
    top = jnp.maximum(jnp.maximum(tops[0], tops[1]), jnp.maximum(tops[2], tops[3]))
    shares = [jnp.exp(item - top) for item in tops]
    total = sum(shares[j] * parts_ref[j, :, pl.ds(1152, 128)] for j in range(4))
    log_ref[...] = top + jnp.log(total)
    shares = [item / total for item in shares]
    joined_ref[...] = jnp.zeros_like(joined_ref)
    streams = (
        (slot_text, text_vec, out_w, up_w, down_w, att_text, mid_text, pre_text, end_text),
        (slot_layout, layout_vec, layout_ref, layout_ref, layout_down, att_layout, mid_layout,
         pre_layout, end_layout),
    )
    for n, (slot, vec, out_r, up_r, down_r, att_r, mid_r, pre_r, end_r) in enumerate(streams):
        width = WIDTHS[n]
        spread = lane_heads(n)
        att = sum(
            parts_ref[j, :, pl.ds(*QUERY_LANES[n])] * exact_product(shares[j], spread)
            for j in range(4)
        )
        att_r[...] = att
        if n == 0:
            out_m, up_m = out_r[...].reshape(768, 768), up_r[...].reshape(3072, 768)
        else:
            out_m, up_m = out_r[pl.ds(576, 192), :], up_r[pl.ds(768, 768), :]
        mid = slot[...] + (cols_product(att.astype(LOW), out_m) + row_of(vec, 4))
        mid_r[...] = mid
        first = norm_apply(mid, row_of(vec, 5), row_of(vec, 6))
        pre = cols_product(first.astype(LOW), up_m) + hidden_bias(vec)
        pre_r[...] = pre
        end = first + (
            plain_product(gelu_value(pre).astype(LOW), down_r[...]) + row_of(vec, 11)
        )
        end_r[...] = end
        joined_ref[:, pl.ds(*QUERY_LANES[n])] = norm_apply(
            end, row_of(vec, 12), row_of(vec, 13)
        ).astype(LOW)
    dense = cols_product(joined_ref[:, pl.ds(0, 960)], head_ref[...]) + row_of(head_vec, 0)
    dense_ref[...] = dense
    picked = norm_apply(gelu_value(dense), row_of(head_vec, 1), row_of(head_vec, 2)).astype(LOW)
    for k, ref in enumerate((pick0, pick1, pick2)):
        ref[...] = picked[:, 256 * k : 256 * k + 256]


def close_back_kernel(
    grad0, grad1, grad2, dense_ref, joined_ref, att_text, att_layout, log_ref, mid_text, mid_layout,
    pre_text, pre_layout, end_text, end_layout, out_w, up_w, down_w, layout_ref, layout_down,
    text_vec, layout_vec, head_ref, head_vec,
    back_ref, d_mid_text, d_mid_layout, d_head, d_out, d_up, d_down, d_layout, d_layout_down,
    d_text_vec, d_layout_vec, d_head_vec,
):
    d_picked = jnp.concatenate([grad0[...], grad1[...], grad2[...]], 1)
    dense = dense_ref[...]
    d_active, d_gain, d_shift = norm_back(gelu_value(dense), row_of(head_vec, 1), d_picked)
    d_dense = (d_active * gelu_slope(dense)).astype(LOW)
    d_head_vec[0:1, :] = total_rows(d_dense)
    d_head_vec[1:2, :] = d_gain
    d_head_vec[2:3, :] = d_shift
    d_head[...] = rows_product(d_dense, joined_ref[:, pl.ds(0, 960)]).astype(LOW)
    d_joined = plain_product(d_dense, head_ref[...])
    back_ref[:, pl.ds(768, 256)] = jnp.zeros((16, 256), jnp.float32)
    delta = jnp.zeros((16, 128), jnp.float32)
    streams = (
        (text_vec, out_w, up_w, down_w, att_text, mid_text, pre_text, end_text,
         d_mid_text, d_out, d_up, d_down, d_text_vec),
        (layout_vec, layout_ref, layout_ref, layout_down, att_layout, mid_layout, pre_layout,
         end_layout, d_mid_layout, d_layout, d_layout, d_layout_down, d_layout_vec),
    )
    for n, (vec, out_r, up_r, down_r, att_r, mid_r, pre_r, end_r, d_mid_r, d_out_r, d_up_r,
            d_down_r, d_vec) in enumerate(streams):
        width = WIDTHS[n]
        if n == 0:
            out_m, up_m = out_r[...].reshape(768, 768), up_r[...].reshape(3072, 768)
        else:
            out_m, up_m = out_r[pl.ds(576, 192), :], up_r[pl.ds(768, 768), :]
        d_end, d_gain2, d_shift2 = norm_back(
            end_r[...], row_of(vec, 12), d_joined[:, QUERY_LANES[n][0] : sum(QUERY_LANES[n])]
        )
        d_branch2 = d_end.astype(LOW)
        mid, pre = mid_r[...], pre_r[...]
        low = gelu_value(pre).astype(LOW)
        d_pre = (cols_product(d_branch2, down_r[...]) * gelu_slope(pre)).astype(LOW)
        first_low = norm_apply(mid, row_of(vec, 5), row_of(vec, 6)).astype(LOW)
        for k in range(4):
            part = slice(width * k, width * (k + 1))
            d_down_r[pl.ds(width * k, width), :] = rows_product(low[:, part], d_branch2).astype(LOW)
            up_at = pl.ds(width * k, width) if n == 0 else pl.ds(192 + width * k, width)
            d_up_r[up_at, :] = rows_product(d_pre[:, part], first_low).astype(LOW)
            d_vec[7 + k : 8 + k, :] = total_rows(d_pre[:, part])
        d_first = d_end + plain_product(d_pre, up_m)
        d_mid, d_gain1, d_shift1 = norm_back(mid, row_of(vec, 5), d_first)
        d_mid_r[...] = d_mid
        d_branch1 = d_mid.astype(LOW)
        att = att_r[...]
        d_out_r[pl.ds(0, width), :] = rows_product(d_branch1, att.astype(LOW)).astype(LOW)
        d_att = plain_product(d_branch1, out_m).astype(LOW).astype(jnp.float32)
        back_ref[:, pl.ds(*QUERY_LANES[n])] = d_att
        delta = delta + exact_product(d_att * att, head_lanes(n))
        d_vec[0:4, :] = jnp.zeros((4, width), jnp.float32)
        for row, value in (
            (4, total_rows(d_branch1)),
            (5, d_gain1),
            (6, d_shift1),
            (11, total_rows(d_branch2)),
            (12, d_gain2),
            (13, d_shift2),
        ):
            d_vec[row : row + 1, :] = value
    back_ref[:, pl.ds(1024, 128)] = log_ref[...]
    back_ref[:, pl.ds(1152, 128)] = delta


def score_back_kernel(
    back_ref, query_ref, key_text, value_text, key_layout, value_layout,
    d_query, d_key_text, d_value_text, d_key_layout, d_value_layout,
):
    keys, values = (key_text, key_layout), (value_text, value_layout)
    stacks = [stack_heads(query_ref[:, pl.ds(*QUERY_LANES[n])], n) for n in range(2)]
    grads = [stack_heads(back_ref[:, pl.ds(*QUERY_LANES[n])], n).astype(LOW) for n in range(2)]
    logs = stack_columns(back_ref[:, pl.ds(1024, 128)])
    delta = stack_columns(back_ref[:, pl.ds(1152, 128)])
    mask = one_micro_batch(64 * HEADS)
    probs = jnp.where(mask, jnp.exp(jnp.where(mask, coupled_scores(stacks, keys) - logs, 0.0)), 0.0)
    d_probs = sum(cols_product(grads[n], values[n][...]) for n in range(2))
    d_scores = (probs * (d_probs - delta)).astype(LOW)
    low = probs.astype(LOW)
    d_query[:, pl.ds(768, 256)] = jnp.zeros((64, 256), jnp.float32)
    d_keys, d_values = (d_key_text, d_key_layout), (d_value_text, d_value_layout)
    for n in range(2):
        d_query[:, pl.ds(*QUERY_LANES[n])] = (
            fold_heads(plain_product(d_scores, keys[n][...]), n) * SCALES[n]
        )
        d_keys[n][...] = (rows_product(d_scores, stacks[n]) * SCALES[n]).astype(LOW)
        d_values[n][...] = rows_product(low, grads[n]).astype(LOW)


def open_back_kernel(
    parts_ref, d_key_text, d_value_text, d_key_layout, d_value_layout, d_mid_text, d_mid_layout,
    text_sum, layout_sum, slot_text, slot_layout, qkv_ref, layout_ref, proj_ref, spatial_ref,
    index_ref, text_vec, layout_vec, slot_turned,
    d_query_w, d_kv_w, d_layout, d_embedded, d_position, d_box, d_proj, d_text_vec, d_layout_vec,
):
    qkv = qkv_ref[...].reshape(2304, 768)
    streams = (
        (qkv, d_key_text, d_value_text, d_mid_text, text_sum, slot_text, text_vec, d_text_vec),
        (layout_ref[pl.ds(0, 576), :], d_key_layout, d_value_layout, d_mid_layout, layout_sum,
         slot_layout, layout_vec, d_layout_vec),
    )
    lows = []
    for n, (weight, d_key_r, d_value_r, d_mid_r, sum_r, slot_r, vec, d_vec) in enumerate(streams):
        width = WIDTHS[n]
        lanes = pl.ds(*QUERY_LANES[n])
        d_query = sum(parts_ref[j, :, lanes] for j in range(4)).astype(LOW)
        d_key, d_value = d_key_r[...], d_value_r[...]
        d_slot = d_mid_r[...] + plain_product(d_query, weight[:width])
        d_normed = (
            plain_product(d_key, weight[width : 2 * width])
            + plain_product(d_value, weight[2 * width :])
            + exact_product(slot_turned[...], d_slot)
        )
        sums = sum_r[...]
        low = norm_apply(sums, row_of(vec, 0), row_of(vec, 1)).astype(LOW)
        d_sum, d_gain, d_shift = norm_back(sums, row_of(vec, 0), d_normed)
        d_vec[...] = jnp.zeros_like(d_vec)
        for row, value in ((0, d_gain), (1, d_shift), (2, total_rows(d_query)), (3, total_rows(d_value))):
            d_vec[row : row + 1, :] = value
        slot_low = slot_r[...].astype(LOW)
        grads = (rows_product(d_query, slot_low), rows_product(d_key, low), rows_product(d_value, low))
        if n == 0:
            d_query_w[...] = grads[0].astype(LOW)
            d_kv_w[pl.ds(0, 768), :] = grads[1].astype(LOW)
            d_kv_w[pl.ds(768, 768), :] = grads[2].astype(LOW)
        else:
            for k in range(3):
                d_layout[pl.ds(192 * k, 192), :] = grads[k].astype(LOW)
        d_low = d_sum.astype(LOW)
        lows.append(d_low)
        wide = d_low.astype(jnp.float32)
        d_position[:, lanes] = wide[:64] + wide[64:]
        if n == 0:
            d_embedded[...] = wide.T.astype(LOW)
    d_spatial = cols_product(lows[1], proj_ref[...]).astype(LOW)
    d_proj[...] = rows_product(spatial_ref[...], lows[1]).astype(LOW)
    number = lax.broadcasted_iota(jnp.int32, (128, 1024), 1)
    for table, users in enumerate(((0, 2), (1, 3), (4,), (5,))):
        total = 0.0
        for k in users:
            hot = (number == index_ref[:, k : k + 1]).astype(LOW)
            total = total + rows_product(hot, d_spatial[:, 128 * k : 128 * k + 128])
        d_box[pl.ds(1024 * table, 1024), :] = total.astype(LOW)


def local_call(kernel, inputs, outputs, name):
    specs, arrays = [], []

    def spec(shape, index):
        return pl.BlockSpec(shape, lambda step: index, pipeline_mode=pl.Buffered(1))

    for item in inputs:
        array, shape, index = item if isinstance(item, tuple) else (item, item.shape, None)
        specs.append(spec(shape, index or (0,) * len(shape)))
        arrays.append(array)
    return pl.pallas_call(
        kernel,
        name=name,
        grid=(1,),
        out_shape=[jax.ShapeDtypeStruct(shape, dtype) for shape, dtype in outputs],
        in_specs=specs,
        out_specs=[spec(shape, (0,) * len(shape)) for shape, dtype in outputs],
        compiler_params=pltpu.CompilerParams(vmem_limit_bytes=56 * 1024 * 1024),
    )(*arrays)


def thirds(number):
    return [(number, (256 * k, 256), k) for k in range(3)]


GATHER_PIECES = thirds(0) + thirds(1) + [(2, None, 0), (3, None, 2), (4, None, 1), (5, None, 2)]
REDUCE_PIECES = (
    thirds(0)
    + thirds(1)
    + [(2, None, 0), (3, None, 2), (4, None, 1), (5, None, 1), (6, None, 2), (7, None, 2), (8, None, 0)]
)
WHOLE = ((0, 2), (0, 4))
REDUCE_SOURCES = [
    (0, (0, 1), (0, 1)),
    (0, (0, 1), (1, 2)),
    (0, (0, 1), (3, 1)),
    (0, (1, 1), (0, 4)),
] + [(number,) + WHOLE for number in range(1, 9)]
SLOT_SPLITS = [[(0, (0, 16))], [(1, (0, 16))], [(2, (0, 16))]]


def fetch(masters):
    word, position, box, text, down, layout, layout_down, head, vector = [
        m.astype(LOW) for m in masters
    ]
    misc = jnp.concatenate(
        [
            layout.T,
            layout_down[0],
            layout_down[1],
            jnp.pad(vector, (0, 192 - vector.shape[0]))[None],
        ],
        0,
    )
    text, down, head, position, misc, box = gather_all(
        [text.T, down, head.T, position, misc, box.reshape(32, 128)], GATHER_PIECES, 2
    )
    return dict(
        text=text,
        down=down.reshape(3072, 768),
        head=head.reshape(768, 960),
        box=box.reshape(128, 4, 8, 128).transpose(1, 0, 2, 3).reshape(4096, 128),
        layout=misc[:, :12].reshape(1536, 192),
        layout_down=misc[:, 12:18].reshape(768, 192),
        box_proj=misc[:, 18:24].reshape(768, 192),
        position=position.reshape(640, 960),
        vector=misc[:, 24, :123].reshape(15744),
    )


def reduce_weights(grads):
    shards = reduce_all(
        [
            grads["query"].reshape(16, 48, 768),
            grads["key_value"].reshape(32, 48, 768),
            grads["out"].reshape(16, 48, 768),
            grads["up"].reshape(64, 48, 768),
            grads["down"].reshape(128, 24, 768),
            grads["head"].reshape(128, 6, 960),
            grads["position"].reshape(128, 5, 960),
            grads["layout"].reshape(128, 12, 192),
            grads["layout_down"].reshape(128, 6, 192),
            grads["box_proj"].reshape(128, 6, 192),
            grads["box"].reshape(4, 128, 8, 128).transpose(1, 0, 2, 3).reshape(128, 32, 128),
            grads["vector"].reshape(128, 1, 123),
        ],
        REDUCE_SOURCES,
        REDUCE_PIECES,
        6,
    )
    text, down, head, position, layout, layout_down, box_proj, box, vector, square = shards
    return square, [
        position,
        box.reshape(4, 8, 128),
        text.T,
        down,
        layout.T,
        jnp.stack([layout_down, box_proj]),
        head.T,
        vector[0],
    ]


def on_device(
    token_ids,
    box_coords,
    intersection_flags,
    masked_rows,
    masked_labels,
    *weights,
):
    triples = [tuple(weights[3 * n : 3 * n + 3]) for n in range(9)]
    masters = [entry[0] for entry in triples]
    word_table = masters[0]
    dp = lax.axis_index("dp")
    vocab = lax.axis_index("vocab")
    shard_width = word_table.shape[1]
    table_rows = word_table.shape[0]
    levels = -(-shard_width // SPAN_LOW)

    row_hot = masked_rows[:, :, None] == jnp.arange(64)[None, None, :]
    counted = jnp.sum(jnp.where(row_hot & (intersection_flags == 0)[:, None, :], 1, 0), 2)
    slot_hot = jnp.concatenate(
        [
            jnp.pad(row_hot[0], ((0, 0), (0, 64))),
            jnp.pad(row_hot[1], ((0, 0), (64, 0))),
        ],
        0,
    )
    slot_hot_wide = slot_hot.astype(jnp.float32)
    f32 = jnp.float32

    notes = jnp.concatenate(
        [
            token_ids.reshape(1, 128),
            jnp.concatenate(
                [masked_labels.reshape(1, 16), counted.reshape(1, 16), jnp.zeros((1, 96), jnp.int32)], 1
            ),
        ],
        0,
    )
    notes_all = lax.all_to_all(
        jnp.broadcast_to(notes[None], (128,) + notes.shape), AXES, 0, 0, tiled=True
    )
    ids_all = notes_all[:, 0, :].reshape(1, 16384)
    labels_all = notes_all[:, 1, :16].reshape(2048)
    counted_all = notes_all[:, 1, 16:32].reshape(2048).astype(jnp.float32)
    total_count = jnp.sum(counted_all)

    local_ids = ids_all - vocab * shard_width
    ids_high = local_ids >> 8
    ids_low = local_ids & 255
    table_low = word_table.astype(LOW)
    table_levels = (
        jnp.pad(table_low, ((0, 0), (0, levels * SPAN_LOW - shard_width)))
        .reshape(table_rows, levels, SPAN_LOW)
        .transpose(1, 0, 2)
        .reshape(levels * table_rows, SPAN_LOW)
    )
    found = pick_columns(table_levels, ids_high, ids_low, table_rows)
    found, masters = lax.optimization_barrier((found, masters))
    found = lax.all_to_all(found, AXES, 0, 0, tiled=True)

    table_blocks = (
        jnp.pad(table_low, ((0, 0), (0, 32 * HEAD_BLOCK - shard_width)))
        .reshape(table_rows, 32, HEAD_BLOCK)
        .transpose(1, 0, 2)
    )
    table_head = lax.all_to_all(table_blocks, "dp", 0, 0, tiled=True).reshape(768, HEAD_BLOCK)

    full = fetch(masters)
    vector = full["vector"].astype(jnp.float32)
    text_vec = vector[:10752].reshape(14, 768)
    layout_vec = vector[10752:13440].reshape(14, 192)
    head_vec = vector[13440:].reshape(3, 768)
    position_own = lax.dynamic_slice_in_dim(full["position"], vocab * 64, 64, 0).astype(f32)
    boxes = box_coords.reshape(4, 128)
    box_index = jnp.stack(
        [
            boxes[0],
            boxes[1],
            boxes[2],
            boxes[3],
            jnp.abs(boxes[3] - boxes[1]),
            jnp.abs(boxes[2] - boxes[0]),
            boxes[0],
            boxes[0],
        ],
        1,
    )
    qkv = (full["text"], (48, 48, 768), (0, 0, 0))
    out_w = (full["text"], (16, 48, 768), (3, 0, 0))
    up_w = (full["text"], (64, 48, 768), (1, 0, 0))
    text_sum, layout_sum, spatial, *kv, query, slot_text, slot_layout = local_call(
        open_kernel,
        [
            found,
            position_own,
            box_index,
            full["box"],
            full["box_proj"],
            qkv,
            full["layout"],
            text_vec,
            layout_vec,
            slot_hot_wide,
        ],
        [
            ((128, 768), f32),
            ((128, 192), f32),
            ((128, 768), LOW),
            ((128, 768), LOW),
            ((128, 768), LOW),
            ((128, 192), LOW),
            ((128, 192), LOW),
            ((16, 1024), LOW),
            ((16, 768), f32),
            ((16, 192), f32),
        ],
        "open_streams",
    )
    query_all = lax.all_gather(query, "vocab", axis=0, tiled=True)
    (partial,) = local_call(score_kernel, [query_all, *kv], [((64, 1280), f32)], "partial_attention")
    partial = lax.all_to_all(partial.reshape(4, 16, 1280), "vocab", 0, 0, tiled=True)
    weights_close = [out_w, up_w, full["down"], full["layout"], full["layout_down"]]
    vectors_close = [text_vec, layout_vec, full["head"], head_vec]
    (att_text, att_layout, log_total, mid_text, mid_layout, pre_text, pre_layout, end_text,
     end_layout, joined, dense, *picked) = local_call(
        close_kernel,
        [partial, slot_text, slot_layout] + weights_close + vectors_close,
        [
            ((16, 768), f32),
            ((16, 192), f32),
            ((16, 128), f32),
            ((16, 768), f32),
            ((16, 192), f32),
            ((16, 3072), f32),
            ((16, 768), f32),
            ((16, 768), f32),
            ((16, 192), f32),
            ((16, 1024), LOW),
            ((16, 768), f32),
            ((16, 256), LOW),
            ((16, 256), LOW),
            ((16, 256), LOW),
        ],
        "close_streams",
    )
    picked_all = gather_slots(picked, SLOT_SPLITS, 3)
    picked_all = jnp.concatenate([p.reshape(2048, 256) for p in picked_all], 1)
    column = lax.broadcasted_iota(jnp.int32, (1, HEAD_BLOCK), 1)
    valid = column < shard_width - dp * HEAD_BLOCK
    logits = jnp.where(valid, plain_product(picked_all, table_head), -1e30)
    row_max = jnp.max(logits, 1)
    row_sum = jnp.sum(jnp.where(valid, jnp.exp(logits - row_max[:, None]), 0.0), 1)
    label_hot = valid & (
        (labels_all - vocab * shard_width - dp * HEAD_BLOCK)[:, None] == column
    )
    target = jnp.sum(jnp.where(label_hot, logits, 0.0), 1)
    stats = jnp.concatenate(
        [row_max.reshape(16, 128), row_sum.reshape(16, 128), target.reshape(16, 128)], 0
    )
    stats = merge_stats(stats, 4)
    row_log = (stats[:16] + jnp.log(stats[16:32])).reshape(2048)
    loss_total = jnp.sum(counted_all * (row_log - stats[32:].reshape(2048)))
    d_logits = (
        (counted_all / total_count)[:, None]
        * (
            jnp.where(valid, jnp.exp(logits - row_log[:, None]), 0.0)
            - label_hot.astype(jnp.float32)
        )
    ).astype(LOW)
    d_picked_part = cols_product(d_logits, table_head).astype(LOW)
    d_picked = reduce_slots(
        [d_picked_part[:, 256 * k : 256 * (k + 1)].reshape(128, 16, 256) for k in range(3)],
        SLOT_SPLITS,
        5,
    )
    table_head_grad = rows_product(picked_all, d_logits).astype(LOW).reshape(32, 24, HEAD_BLOCK)
    table_head_grad = lax.all_to_all(table_head_grad, "dp", 0, 0, tiled=True)

    (back, d_mid_text, d_mid_layout, d_head, d_out, d_up, d_down, d_layout_close, d_layout_down,
     d_text_vec, d_layout_vec, d_head_vec) = local_call(
        close_back_kernel,
        list(d_picked)
        + [dense, joined, att_text, att_layout, log_total, mid_text, mid_layout, pre_text]
        + [pre_layout, end_text, end_layout]
        + weights_close
        + vectors_close,
        [
            ((16, 1280), f32),
            ((16, 768), f32),
            ((16, 192), f32),
            ((768, 960), LOW),
            ((768, 768), LOW),
            ((3072, 768), LOW),
            ((3072, 768), LOW),
            ((960, 192), LOW),
            ((768, 192), LOW),
            ((14, 768), f32),
            ((14, 192), f32),
            ((3, 768), f32),
        ],
        "close_streams_back",
    )
    back = lax.all_gather(back, "vocab", axis=0, tiled=True)
    d_query, *d_kv = local_call(
        score_back_kernel,
        [back, query_all, *kv],
        [
            ((64, 1024), f32),
            ((128, 768), LOW),
            ((128, 768), LOW),
            ((128, 192), LOW),
            ((128, 192), LOW),
        ],
        "attention_back",
    )
    d_query = lax.all_to_all(d_query.reshape(4, 16, 1024), "vocab", 0, 0, tiled=True)
    (d_query_w, d_kv_w, d_layout_open, d_embedded, d_position, d_box, d_proj, d_text_open,
     d_layout_vec_open) = local_call(
        open_back_kernel,
        [d_query, *d_kv, d_mid_text, d_mid_layout, text_sum, layout_sum, slot_text, slot_layout]
        + [qkv, full["layout"], full["box_proj"], spatial, box_index, text_vec, layout_vec]
        + [slot_hot_wide.T],
        [
            ((768, 768), LOW),
            ((1536, 768), LOW),
            ((576, 192), LOW),
            ((768, 128), LOW),
            ((64, 960), f32),
            ((4096, 128), LOW),
            ((768, 192), LOW),
            ((14, 768), f32),
            ((14, 192), f32),
        ],
        "open_streams_back",
    )
    d_text_blocks = jnp.broadcast_to(
        d_embedded.reshape(32, 1, 24, 128), (32, 4, 24, 128)
    ).reshape(128, 24, 128)
    d_text_all = lax.all_to_all(d_text_blocks, AXES, 0, 0, tiled=True)
    table_grad = (
        spread_columns(d_text_all, ids_high, ids_low, levels)
        .reshape(levels, table_rows, SPAN_LOW)
        .transpose(1, 0, 2)
        .reshape(table_rows, levels * SPAN_LOW)[:, :shard_width]
    )
    table_grad = table_grad + table_head_grad.transpose(1, 0, 2).reshape(
        table_rows, 32 * HEAD_BLOCK
    )[:, :shard_width].astype(jnp.float32)

    d_positions = lax.dynamic_update_slice_in_dim(
        jnp.zeros((640, 960), LOW), d_position.astype(LOW), vocab * 64, 0
    )
    square, shards = reduce_weights(
        dict(
            query=d_query_w,
            key_value=d_kv_w,
            out=d_out,
            up=d_up,
            down=d_down,
            head=d_head,
            box=d_box,
            layout=jnp.concatenate([d_layout_open, d_layout_close], 0),
            layout_down=d_layout_down,
            box_proj=d_proj,
            position=d_positions,
            vector=jnp.concatenate(
                [
                    (d_text_vec + d_text_open).reshape(10752),
                    (d_layout_vec + d_layout_vec_open).reshape(2688),
                    d_head_vec.reshape(2304),
                ]
            ).astype(LOW),
        )
    )
    all_grads = [table_grad] + shards
    norm_stats = jnp.concatenate(
        [
            jnp.zeros((16, 128), f32),
            square + jnp.sum(table_grad * table_grad),
            jnp.zeros((16, 128), f32),
        ],
        0,
    )
    grad_norm = jnp.sqrt(merge_stats(norm_stats, 7)[16, 0])
    factor = jnp.minimum(1.0, CLIP / grad_norm)
    results = []
    for (master, momentum, average), grad in zip(triples, all_grads):
        clipped = factor * grad
        momentum_next = MOMENTUM * momentum + clipped
        master_next = master - RATE * (clipped + MOMENTUM * momentum_next)
        average_next = AVERAGE_KEEP * average + (1.0 - AVERAGE_KEEP) * master_next
        results += [master_next, momentum_next, average_next]
    return tuple(results + [loss_total, total_count, grad_norm])


TOKEN_SPEC = P(None, AXES)
WEIGHT_SPECS = (
    P("dp", "vocab"),
    P(AXES, None),
    P(None, AXES, None),
    P(None, AXES),
    P(AXES, None),
    P(None, AXES),
    P(None, AXES, None),
    P(None, AXES),
    P(AXES),
)


def solution(mesh):
    weight_specs = tuple(spec for spec in WEIGHT_SPECS for _ in range(3))
    in_specs = (TOKEN_SPEC, P(None, None, AXES), TOKEN_SPEC, TOKEN_SPEC, TOKEN_SPEC) + weight_specs
    out_specs = weight_specs + (P(), P(), P())
    return jax.shard_map(
        on_device, mesh=mesh, in_specs=in_specs, out_specs=out_specs, check_vma=False
    )
```

profile of v0, /device:TPU:0, one launch (start us, length us, event | category | flops | bytes accessed | tf_op | source)
XLA Modules:
  0.0 471.8 jit_solution(2631536010979895459)
XLA Ops:
  4.6 11.1 %all-to-all-start = ((s32[128,2,128]{2,1,0:T(2,128)}), s32[128,2,128]{2,1,0:T(2,128)S(1)}, u32[]{:S(2)}, u32[]{:S(2)}) async-start(s32[128,2,128]{2,1,0:T(2,128)} %broadcast_in_dim.63), calls=%async_computation | async-start | bytes 262144 | tf_op jit(solution)/shard_map/all_to_all | solution.py:1356
  21.0 4.2 all-to-all-done
  25.3 15.9 %shard_map.535 = bf16[128,24,128]{2,1,0:T(8,128)(2,1)} custom-call(bf16[1200,256]{1,0:T(8,128)(2,1)S(1)} %bitcast.123, s32[1,16384]{1,0:T(1,128)S(1)} %get-tuple-element.380.high_ref, s32[1,16384]{1,0:T(1,128)S(1)} %get-tuple-element.379.low_ref), custom_call_target="tpu_custom_call" | custom-call | tf_op jit(solution)/shard_map/pallas_call | solution.py:775
  42.5 5.6 %all-to-all-start.1 = ((bf16[128,24,128]{2,1,0:T(8,128)(2,1)}), bf16[128,24,128]{2,1,0:T(8,128)(2,1)S(1)}, u32[]{:S(2)}, u32[]{:S(2)}) async-start(bf16[128,24,128]{2,1,0:T(8,128)(2,1)} %shard_map.535), calls=%async_computation.1 | async-start | bytes 1572864 | tf_op jit(solution)/shard_map/all_to_all | solution.py:1376
  51.9 64.5 %shard_map.536 = (bf16[2,4,4,2,2,48,768]{6,5,4,3,2,1,0:T(8,128)(2,1)}, bf16[2,4,4,2,2,24,768]{6,5,4,3,2,1,0:T(8,128)(2,1)}, bf16[2,4,4,2,2,6,960]{6,5,4,3,2,1,0:...) custom-call(bf16[48,768]{1,0:T(8,128)(2,1)} %convert_bitcast_fusion., ...), custom_call_target="tpu_custom_call" | custom-call | flops 60000002048 | bytes 200000000 | tf_op jit(solution)/shard_map/pallas_call | solution.py:156
  131.8 5.8 %open_streams.1 = (f32[128,768]{1,0:T(8,128)}, f32[128,192]{1,0:T(8,128)}, bf16[128,768]{1,0:T(8,128)(2,1)}, bf16[128,768]{1,0:T(8,128)(2,1)}, bf16[128,768]{1,0...) custom-call(bf16[128,24,128]{2,1,0:T(8,128)(2,1)} %copy-done.8, ...), custom_call_target="tpu_custom_call" | custom-call | tf_op jit(solution)/shard_map/open_streams/pallas_call | solution.py:1225
  137.6 6.4 %all_gather.6.query_ref = bf16[64,1024]{1,0:T(8,128)(2,1)} all-gather(bf16[16,1024]{1,0:T(8,128)(2,1)} %get-tuple-element.124), channel_id=1, replica_groups=mesh['dp'=32,'vocab'=4] {'vocab'}, dimensions={0}, use_global_device_ids=true | all-gather | bytes 163840 | tf_op jit(solution)/shard_map/all_gather | solution.py:1436
  153.0 5.2 %all-to-all-done.2.parts_ref = f32[4,16,1280]{2,1,0:T(8,128)} async-done(((f32[4,16,1280]{2,1,0:T(8,128)}), f32[4,16,1280]{2,1,0:T(8,128)}, u32[]{:S(2)}, u32[]{:S(2)}) %all-to-all-start.2) | async-done | bytes 327712 | tf_op jit(solution)/shard_map/all_to_all | solution.py:1438
  158.1 7.8 %all-to-all-start.3 = ((bf16[32,24,512]{2,1,0:T(8,128)(2,1)}), bf16[32,24,512]{2,1,0:T(8,128)(2,1)}, u32[]{:S(2)}, u32[]{:S(2)}) async-start(bf16[32,24,512]{2,1,0:T(8,128)(2,1)} %copy.159), calls=%async_computation.3 | async-start | bytes 1572864 | tf_op jit(solution)/shard_map/all_to_all | solution.py:1383
  170.6 10.4 %close_streams.1 = (f32[16,768]{1,0:T(8,128)}, f32[16,192]{1,0:T(8,128)}, f32[16,128]{1,0:T(8,128)}, f32[16,768]{1,0:T(8,128)}, f32[16,192]{1,0:T(8,128)}, /*ind...) custom-call(f32[4,16,1280]{2,1,0:T(8,128)} %all-to-all-done.2.parts_, ...), custom_call_target="tpu_custom_call" | custom-call | tf_op jit(solution)/shard_map/close_streams/pallas_call | solution.py:1225
  181.0 23.7 %shard_map.537 = (bf16[2,4,4,2,2,16,256]{6,5,4,3,2,1,0:T(8,128)(2,1)}, bf16[2,4,4,2,2,16,256]{6,5,4,3,2,1,0:T(8,128)(2,1)}, bf16[2,4,4,2,2,16,256]{6,5,4,3,2,1,0:T(8,128)(2,1)}) custom-call(bf16[16,256]{1,0:T(8,128)(2,1)} %get-tuple-element.133.refs_0_, bf16[16,256]{1,0:T(8,128)(2,1)} %get-tuple-element.134.refs_1_, bf16[16,256]{1,0:T(8,128)(2,1)} %get-tuple-element.135.refs_2_), custom_call_target="tpu_custom_call" | custom-call | tf_op jit(solution)/shard_map/pallas_call | solution.py:476
  213.3 16.6 %shard_map.538 = f32[48,128]{1,0:T(8,128)} custom-call(f32[48,128]{1,0:T(8,128)} %pad_maximum_fusion.5.in_ref), custom_call_target="tpu_custom_call" | custom-call | tf_op jit(solution)/shard_map/pallas_call | solution.py:726
  232.1 5.8 %convolution_convert_fusion = bf16[2048,768]{1,0:T(8,128)(2,1)S(1)} fusion(bf16[768,512]{1,0:T(8,128)(2,1)} %bitcast.23, f32[2048,512]{0,1:T(8,128)} %copy-done.5, f32[2048]{0:T(1024)S(1)} %get-tuple-element.383, s32[2048]{0:T(1024)S(1)} %sub.138, f32[2048]{0:T(1024)S(1)} %div.18, pred[512]{0:T(512)(128)(4,1)S(1)} %iota_compare_fusion.2), kind=kOutput, calls=%fused_computation.6 | convolution fusion | flops 1621622784 | bytes 8151552 | tf_op jit(solution)/shard_map/dot_general | solution.py:856
  239.6 35.1 %shard_map.539 = (f32[16,256]{1,0:T(8,128)}, f32[16,256]{1,0:T(8,128)}, f32[16,256]{1,0:T(8,128)}) custom-call(bf16[2,4,4,2,2,16,256]{6,5,4,3,2,1,0:T(8,128)(2,1)} %bitcast.138, bf16[2,4,4,2,2,16,256]{6,5,4,3,2,1,0:T(8,128)(2,1)} %bitcast.137, bf16[2,4,4,2,2,16,256]{6,5,4,3,2,1,0:T(8,128)(2,1)} %bitcast.136), custom_call_target="tpu_custom_call" | custom-call | tf_op jit(solution)/shard_map/pallas_call | solution.py:656
  274.7 14.7 %close_streams_back.1 = (f32[16,1280]{1,0:T(8,128)}, f32[16,768]{1,0:T(8,128)}, f32[16,192]{1,0:T(8,128)}, bf16[768,960]{1,0:T(8,128)(2,1)}, bf16[768,768]{1,0:T...) custom-call(f32[16,256]{1,0:T(8,128)} %get-tuple-element.139.grad0, ...), custom_call_target="tpu_custom_call" | custom-call | tf_op jit(solution)/shard_map/close_streams_back/pallas_call | solution.py:1225
  289.5 6.6 %all_gather.7.back_ref = f32[64,1280]{1,0:T(8,128)} all-gather(f32[16,1280]{1,0:T(8,128)} %get-tuple-element.153), channel_id=1, replica_groups=mesh['dp'=32,'vocab'=4] {'vocab'}, dimensions={0}, use_global_device_ids=true | all-gather | bytes 409600 | tf_op jit(solution)/shard_map/all_gather | solution.py:1520
  303.6 6.3 %convolution_convert_fusion.1 = bf16[768,512]{1,0:T(8,128)(2,1)} fusion(bf16[2048,256]{1,0:T(8,128)(2,1)} %bitcast.172, bf16[2048,256]{1,0:T(8,128)(2,1)} %bitcast.170, bf16[2048,256]{1,0:T(8,128)(2,1)S(1)} %bitcast.168, f32[2048,512]{0,1:T(8,128)} %copy-done.5, f32[2048]{0:T(1024)S(1)} %get-tuple-element.383, s32[2048]{0:T(1024)S(1)} %sub.138, ...), kind=kOutput, calls=%fused_computation.8 | convolution fusion | flops 1629880320 | bytes 8151552 | tf_op jit(solution)/shard_map/dot_general | solution.py:850
  312.5 6.8 %all-to-all-start.6 = ((bf16[32,24,512]{2,1,0:T(8,128)(2,1)}), bf16[32,24,512]{2,1,0:T(8,128)(2,1)S(1)}, u32[]{:S(2)}, u32[]{:S(2)}) async-start(bf16[32,24,512]{2,1,0:T(8,128)(2,1)} %bitcast.45), calls=%async_computation.6 | async-start | bytes 1572864 | tf_op jit(solution)/shard_map/all_to_all | solution.py:1494
  319.4 7.3 %open_streams_back.1 = (bf16[768,768]{1,0:T(8,128)(2,1)}, bf16[1536,768]{1,0:T(8,128)(2,1)}, bf16[576,192]{1,0:T(8,128)(2,1)}, bf16[768,128]{1,0:T(8,128)(2,1)},...) custom-call(f32[4,16,1024]{2,1,0:T(8,128)} %copy-done.12, ...), custom_call_target="tpu_custom_call" | custom-call | tf_op jit(solution)/shard_map/open_streams_back/pallas_call | solution.py:1225
  336.3 10.6 %all-to-all-start.5 = ((bf16[128,24,128]{2,1,0:T(8,128)(2,1)}), bf16[128,24,128]{2,1,0:T(8,128)(2,1)S(1)}, u32[]{:S(2)}, u32[]{:S(2)}) async-start(bf16[128,24,128]{2,1,0:T(8,128)(2,1)} %bitcast.42), calls=%async_computation.5 | async-start | bytes 1572864 | tf_op jit(solution)/shard_map/all_to_all | solution.py:1556
  347.0 77.0 %shard_map.540 = (f32[48,768]{1,0:T(8,128)}, f32[24,768]{1,0:T(8,128)}, f32[6,960]{1,0:T(8,128)}, f32[5,960]{1,0:T(8,128)}, f32[12,192]{1,0:T(8,128)}, /*index=5...) custom-call(bf16[1,1,4,2,2,48,768]{6,5,4,3,2,1,0:T(8,128)(2,1)} %bitcast.166, ...), custom_call_target="tpu_custom_call" | custom-call | flops 60000002048 | bytes 200000000 | tf_op jit(solution)/shard_map/pallas_call | solution.py:365
  424.2 14.5 %shard_map.541 = f32[1200,256]{1,0:T(8,128)S(1)} custom-call(bf16[128,24,128]{2,1,0:T(8,128)(2,1)S(1)} %all-to-all-done.5.grad_ref, s32[1,16384]{1,0:T(1,128)S(1)} %copy-done.3, s32[1,16384]{1,0:T(1,128)S(1)} %copy-done.1), custom_call_target="tpu_custom_call" | custom-call | tf_op jit(solution)/shard_map/pallas_call | solution.py:819
  441.1 16.2 %shard_map.542 = f32[48,128]{1,0:T(8,128)} custom-call(f32[48,128]{1,0:T(8,128)} %pad_maximum_fusion.6.in_ref), custom_call_target="tpu_custom_call" | custom-call | tf_op jit(solution)/shard_map/pallas_call | solution.py:726
  461.4 4.1 multiply_add_fusion
  (255 shorter events, 85.3 us)
Async XLA Ops:
  4.6 20.5 %all-to-all-start = ((s32[128,2,128]{2,1,0:T(2,128)}), s32[128,2,128]{2,1,0:T(2,128)S(1)}, u32[]{:S(2)}, u32[]{:S(2)}) async-start(s32[128,2,128]{2,1,0:T(2,128)} %broadcast_in_dim.63), calls=%async_computation | async-start | bytes 262144 | tf_op jit(solution)/shard_map/all_to_all | solution.py:1356
  19.0 29.0 %copy-start.17 = (f32[768,48]{0,1:T(8,128)S(1)}, f32[768,48]{0,1:T(8,128)}, u32[]{:S(2)}) copy-start(f32[768,48]{0,1:T(8,128)} %param.46) | copy-start | bytes 442372
  19.0 29.7 %copy-start.22 = (f32[24,768]{1,0:T(8,128)S(1)}, f32[24,768]{1,0:T(8,128)}, u32[]{:S(2)}) copy-start(f32[24,768]{1,0:T(8,128)} %param.49) | copy-start | bytes 221188
  19.0 30.3 %copy-start.30 = (f32[960,6]{0,1:T(8,128)S(1)}, f32[960,6]{0,1:T(8,128)}, u32[]{:S(2)}) copy-start(f32[960,6]{0,1:T(8,128)} %param.58) | copy-start | bytes 69124
  19.0 30.9 %copy-start.28 = (f32[5,960]{1,0:T(8,128)S(1)}, f32[5,960]{1,0:T(8,128)}, u32[]{:S(2)}) copy-start(f32[5,960]{1,0:T(8,128)} %param.40) | copy-start | bytes 57604
  19.1 31.5 %copy-start.64 = (f32[123]{0:T(128)S(1)}, f32[123]{0:T(128)}, u32[]{:S(2)}) copy-start(f32[123]{0:T(128)} %param.61) | copy-start | bytes 1480
  19.1 31.5 %copy-start.40 = (f32[2,6,192]{2,0,1:T(2,128)S(1)}, f32[2,6,192]{2,0,1:T(2,128)}, u32[]{:S(2)}) copy-start(f32[2,6,192]{2,0,1:T(2,128)} %param.55) | copy-start | bytes 27652
  19.1 31.5 %copy-start.38 = (f32[192,12]{0,1:T(8,128)S(1)}, f32[192,12]{0,1:T(8,128)}, u32[]{:S(2)}) copy-start(f32[192,12]{0,1:T(8,128)} %param.52) | copy-start | bytes 27652
  19.1 31.5 %copy-start.36 = (f32[4,8,128]{2,1,0:T(8,128)S(1)}, f32[4,8,128]{2,1,0:T(8,128)}, u32[]{:S(2)}) copy-start(f32[4,8,128]{2,1,0:T(8,128)} %param.43) | copy-start | bytes 49156
  42.5 88.5 %all-to-all-start.1 = ((bf16[128,24,128]{2,1,0:T(8,128)(2,1)}), bf16[128,24,128]{2,1,0:T(8,128)(2,1)S(1)}, u32[]{:S(2)}, u32[]{:S(2)}) async-start(bf16[128,24,128]{2,1,0:T(8,128)(2,1)} %shard_map.535), calls=%async_computation.1 | async-start | bytes 1572864 | tf_op jit(solution)/shard_map/all_to_all | solution.py:1376
  147.2 10.9 %all-to-all-start.2 = ((f32[4,16,1280]{2,1,0:T(8,128)}), f32[4,16,1280]{2,1,0:T(8,128)}, u32[]{:S(2)}, u32[]{:S(2)}) async-start(f32[4,16,1280]{2,1,0:T(8,128)} %bitcast.148), calls=%async_computation.2 | async-start | bytes 655360 | tf_op jit(solution)/shard_map/all_to_all | solution.py:1438
  158.1 46.6 %all-to-all-start.3 = ((bf16[32,24,512]{2,1,0:T(8,128)(2,1)}), bf16[32,24,512]{2,1,0:T(8,128)(2,1)}, u32[]{:S(2)}, u32[]{:S(2)}) async-start(bf16[32,24,512]{2,1,0:T(8,128)(2,1)} %copy.159), calls=%async_computation.3 | async-start | bytes 1572864 | tf_op jit(solution)/shard_map/all_to_all | solution.py:1383
  300.1 12.4 %all-to-all-start.4 = ((f32[4,16,1024]{2,1,0:T(8,128)}), f32[4,16,1024]{2,1,0:T(8,128)S(1)}, u32[]{:S(2)}, u32[]{:S(2)}) async-start(f32[4,16,1024]{2,1,0:T(8,128)} %bitcast.155), calls=%async_computation.4 | async-start | bytes 524288 | tf_op jit(solution)/shard_map/all_to_all | solution.py:1533
  312.5 22.6 %all-to-all-start.6 = ((bf16[32,24,512]{2,1,0:T(8,128)(2,1)}), bf16[32,24,512]{2,1,0:T(8,128)(2,1)S(1)}, u32[]{:S(2)}, u32[]{:S(2)}) async-start(bf16[32,24,512]{2,1,0:T(8,128)(2,1)} %bitcast.45), calls=%async_computation.6 | async-start | bytes 1572864 | tf_op jit(solution)/shard_map/all_to_all | solution.py:1494
  336.3 87.9 %all-to-all-start.5 = ((bf16[128,24,128]{2,1,0:T(8,128)(2,1)}), bf16[128,24,128]{2,1,0:T(8,128)(2,1)S(1)}, u32[]{:S(2)}, u32[]{:S(2)}) async-start(bf16[128,24,128]{2,1,0:T(8,128)(2,1)} %bitcast.42), calls=%async_computation.5 | async-start | bytes 1572864 | tf_op jit(solution)/shard_map/all_to_all | solution.py:1556
  347.0 77.1 %copy-start.7 = (bf16[32,24,512]{2,1,0:T(8,128)(2,1)S(1)}, bf16[32,24,512]{2,1,0:T(8,128)(2,1)}, u32[]{:S(2)}) copy-start(bf16[32,24,512]{2,1,0:T(8,128)(2,1)} %copy-done.6) | copy-start | bytes 2359300
  347.0 77.3 %copy-start.1 = (s32[1,16384]{1,0:T(1,128)S(1)}, s32[1,16384]{1,0:T(1,128)}, u32[]{:S(2)}) copy-start(s32[1,16384]{1,0:T(1,128)} %copy-done) | copy-start | bytes 196612
  347.0 77.3 %copy-start.3 = (s32[1,16384]{1,0:T(1,128)S(1)}, s32[1,16384]{1,0:T(1,128)}, u32[]{:S(2)}) copy-start(s32[1,16384]{1,0:T(1,128)} %copy-done.2) | copy-start | bytes 196612
  424.1 35.0 %copy-start.41 = (f32[2,6,192]{2,0,1:T(2,128)S(1)}, f32[2,6,192]{2,0,1:T(2,128)}, u32[]{:S(2)}) copy-start(f32[2,6,192]{2,0,1:T(2,128)} %param.55) | copy-start | bytes 27652
  424.2 35.0 %copy-start.58 = (f32[2,6,192]{2,0,1:T(2,128)S(1)}, f32[2,6,192]{2,0,1:T(2,128)}, u32[]{:S(2)}) copy-start(f32[2,6,192]{2,0,1:T(2,128)} %param.57) | copy-start | bytes 27652
  424.2 35.0 %copy-start.59 = (f32[2,6,192]{2,0,1:T(2,128)S(1)}, f32[2,6,192]{2,0,1:T(2,128)}, u32[]{:S(2)}) copy-start(f32[2,6,192]{2,0,1:T(2,128)} %param.56) | copy-start | bytes 27652
  424.2 35.0 %copy-start.61 = (f32[6,192]{1,0:T(8,128)S(1)}, f32[6,192]{1,0:T(8,128)}, u32[]{:S(2)}) copy-start(f32[6,192]{1,0:T(8,128)} %get-tuple-element.188) | copy-start | bytes 13828
  424.2 35.0 %copy-start.62 = (f32[6,192]{1,0:T(8,128)S(1)}, f32[6,192]{1,0:T(8,128)}, u32[]{:S(2)}) copy-start(f32[6,192]{1,0:T(8,128)} %get-tuple-element.189) | copy-start | bytes 13828
  424.2 36.9 %copy-start.4 = (f32[24,12576]{1,0:T(8,128)S(1)}, f32[24,12576]{1,0:T(8,128)}, u32[]{:S(2)}) copy-start(f32[24,12576]{1,0:T(8,128)} %param.37) | copy-start | bytes 3621892
  (53 other events, 349.4 us)
where the time goes:
time: 481 us; the launch traced here: 472 us
  Pallas kernels  309 us (64%)
  starting transfers between devices  49.5 us (10%)
  local copies, waits for them, and re-layouts  41 us (9%)
  other arithmetic  29.8 us (6%)
  matrix products  15.8 us (3%)
  blocking collectives  13 us (3%)
  waiting for transfers between devices  9.36 us (2%)
    pallas_call x1, Pallas kernels, reduce_all(): pl.pallas_call(functools.partial(reduce_kernel, sources, pieces, count),...  77 us
    pallas_call x1, Pallas kernels, gather_all(): pl.pallas_call(functools.partial(gather_kernel, pieces, count), out_shape...  64.5 us
    pallas_call x6, Pallas kernels, local_call(): pl.pallas_call(kernel, name=name, grid=(1,), out_shape=[jax.ShapeDtypeStr...  45.5 us
    pallas_call x1, Pallas kernels, reduce_slots(): pl.pallas_call(functools.partial(slot_reduce_kernel, pieces, count, total...  35.1 us
    pallas_call x2, Pallas kernels, merge_stats(): pl.pallas_call(stats_kernel, out_shape=jax.ShapeDtypeStruct((48, 128), jn...  32.8 us
    pallas_call x1, Pallas kernels, gather_slots(): pl.pallas_call(functools.partial(slot_gather_kernel, pieces, count), out_...  23.7 us
    pallas_call x1, Pallas kernels, pick_columns(): pl.pallas_call(functools.partial(pick_kernel, levels, rows), grid=(tokens...  15.9 us
    pallas_call x1, Pallas kernels, spread_columns(): pl.pallas_call(functools.partial(spread_kernel, levels, rows), grid=(toke...  14.5 us
  transfers between devices with their start and end apart: 7, of which 2 were waited for; matrix products, arithmetic and copies ran while one was open for 10% of the time, Pallas kernels for 39%

commit v1 on v0

--- a/solution.py
+++ b/solution.py
@@ -378,293 +378,6 @@
     )(*views)
 
 
-def blocks_in(dims):
-    total = 1
-    for size in open_shape(dims):
-        total *= size
-    return total
-
-
-def view(ref, place, open_dims, rows):
-    start, count = rows
-    if "x" in open_dims:
-        high, low = pl.ds(0, 2), pl.ds(0, 2)
-    else:
-        high, low = place["x"] // 2, place["x"] % 2
-    mid = pl.ds(0, 4) if "y" in open_dims else place["y"]
-    deep = pl.ds(0, 4) if "z" in open_dims else place["z"]
-    core = pl.ds(0, 2) if "c" in open_dims else place["c"]
-    return ref.at[high, mid, deep, low, core, pl.ds(start, count), :]
-
-
-def slot_gather_kernel(pieces, count, *refs):
-    ins, outs = refs[:count], refs[count : 2 * count]
-    own_sem, core_send, core_recv, ring_send, ring_recv, pass_send, pass_recv = refs[2 * count :]
-    place = my_place()
-    sibling = moved(place, "c", 1)
-    greet(place, (1, 2, 3))
-
-
-    closing = []
-    locals_ = []
-    for number in range(count):
-        whole = (0, ins[number].shape[0])
-        copy = pltpu.make_async_copy(ins[number], view(outs[number], place, "", whole), own_sem.at[number])
-        copy.start()
-        locals_.append(copy)
-        cross = remote(ins[number], view(outs[number], place, "", whole),
-                       core_send.at[number], core_recv.at[number], sibling)
-        cross.start()
-        closing.append(cross)
-    started = {}
-    forwarded = []
-
-    def land(phase):
-        for split, pieces_of in enumerate(pieces):
-            order = ORDERS[split]
-            dim = order[phase]
-            for step in (1, 2, 3):
-                origin = moved(place, dim, -step)
-                for index, (number, rows) in pieces_of:
-                    started[(phase, split, step, index)].wait_recv()
-                    spot = view(outs[number], origin, order[:phase], rows)
-                    onward = remote(spot, spot, pass_send.at[phase, step - 1, index],
-                                    pass_recv.at[phase, step - 1, index], sibling)
-                    onward.start()
-                    forwarded.append(onward)
-
-    for phase in range(3):
-        if phase:
-            land(phase - 1)
-        for split, pieces_of in enumerate(pieces):
-            order = ORDERS[split]
-            dim = order[phase]
-            for step in (1, 2, 3):
-                target = moved(place, dim, step)
-                for index, (number, rows) in pieces_of:
-                    spot = view(outs[number], place, order[:phase], rows)
-                    src = ins[number].at[pl.ds(*rows), :] if phase == 0 else spot
-                    copy = remote(src, spot, ring_send.at[phase, step - 1, index],
-                                  ring_recv.at[phase, step - 1, index], target)
-                    copy.start()
-                    started[(phase, split, step, index)] = copy
-        if phase == 0:
-            for copy in locals_:
-                copy.wait()
-    land(2)
-    for copy in started.values():
-        copy.wait_send()
-    for copy in forwarded + closing:
-        copy.wait()
-
-
-def number_pieces(splits):
-    index = 0
-    result = []
-    for split in splits:
-        rows = []
-        for piece in split:
-            rows.append((index, piece))
-            index += 1
-        result.append(rows)
-    return result, index
-
-
-def gather_slots(arrays, splits, collective_id):
-    pieces, total = number_pieces(splits)
-    count = len(arrays)
-    outs = pl.pallas_call(
-        functools.partial(slot_gather_kernel, pieces, count),
-        out_shape=[jax.ShapeDtypeStruct((2, 4, 4, 2, 2) + a.shape, a.dtype) for a in arrays],
-        in_specs=[pl.BlockSpec(memory_space=pl.ANY)] * count,
-        out_specs=[pl.BlockSpec(memory_space=pl.ANY)] * count,
-        scratch_shapes=[
-            pltpu.SemaphoreType.DMA((count,)),
-            pltpu.SemaphoreType.DMA((count,)),
-            pltpu.SemaphoreType.DMA((count,)),
-            pltpu.SemaphoreType.DMA((3, 3, total)),
-            pltpu.SemaphoreType.DMA((3, 3, total)),
-            pltpu.SemaphoreType.DMA((3, 3, total)),
-            pltpu.SemaphoreType.DMA((3, 3, total)),
-        ],
-        compiler_params=pltpu.CompilerParams(collective_id=collective_id, has_side_effects=True),
-    )(*arrays)
-    return [o.reshape((128,) + a.shape) for o, a in zip(outs, arrays)]
-
-
-def block_at(ref, place, dims, rows, lead=()):
-    start, count = rows
-    high, low = (pl.ds(0, 2), pl.ds(0, 2)) if "x" in dims else (place["x"] // 2, place["x"] % 2)
-    mid = pl.ds(0, 4) if "y" in dims else place["y"]
-    deep = pl.ds(0, 4) if "z" in dims else place["z"]
-    return ref.at[high, mid, deep, low, pl.ds(start, count), :]
-
-
-def spot_of(flat, dims, place):
-    spot = {"xh": place["x"] // 2, "y": place["y"], "z": place["z"], "xl": place["x"] % 2}
-    if "x" in dims:
-        spot["xl"] = flat % 2
-        flat = flat // 2
-    if "z" in dims:
-        spot["z"] = flat % 4
-        flat = flat // 4
-    if "y" in dims:
-        spot["y"] = flat % 4
-        flat = flat // 4
-    if "x" in dims:
-        spot["xh"] = flat
-    return spot
-
-
-def open_index(spot, dims):
-    index = ()
-    if "x" in dims:
-        index += (spot["xh"],)
-    if "y" in dims:
-        index += (spot["y"],)
-    if "z" in dims:
-        index += (spot["z"],)
-    if "x" in dims:
-        index += (spot["xl"],)
-    return index
-
-
-def slot_reduce_kernel(pieces, count, total, *refs):
-    ins, outs = refs[:count], refs[count : 2 * count]
-    refs = refs[2 * count :]
-    accs, crosses = refs[:count], refs[count : 2 * count]
-    rings = [refs[2 * count + phase * total : 2 * count + (phase + 1) * total] for phase in range(3)]
-    own_sem, core_send, core_recv, ring_send, ring_recv = refs[2 * count + 3 * total :]
-    place = my_place()
-    sibling = moved(place, "c", 1)
-    greet(place, (1, 2, 3))
-
-
-    def add_into(number, rows, place, dims, others):
-        start, length = rows
-        acc = accs[number]
-
-        def body(flat, carry):
-            spot = spot_of(flat, dims, place)
-            where = (spot["xh"], spot["y"], spot["z"], spot["xl"], pl.ds(start, length), slice(None))
-            value = acc[where].astype(jnp.float32)
-            for other in others:
-                value = value + other(spot)
-            acc[where] = value.astype(acc.dtype)
-            return carry
-
-        lax.fori_loop(0, blocks_in(dims), body, 0)
-
-    crossing = {}
-    for split, pieces_of in enumerate(pieces):
-        for index, (number, rows) in pieces_of:
-            cross = remote(
-                view(ins[number], sibling, "xyz", rows),
-                block_at(crosses[number], place, "xyz", rows),
-                core_send.at[index], core_recv.at[index], sibling,
-            )
-            cross.start()
-            own = pltpu.make_async_copy(
-                view(ins[number], place, "xyz", rows),
-                block_at(accs[number], place, "xyz", rows),
-                own_sem.at[index],
-            )
-            own.start()
-            crossing[index] = (cross, own)
-    sends = []
-    rounds = {}
-
-    def launch(phase, split, pieces_of):
-        order = ORDERS[split]
-        dim = order[phase]
-        rest = "".join(order[phase + 1 :])
-        for step in (1, 2, 3):
-            there = moved(place, dim, step)
-            target = there
-            for index, (number, rows) in pieces_of:
-                copy = remote(
-                    block_at(accs[number], there, rest, rows),
-                    rings[phase][index].at[step - 1],
-                    ring_send.at[phase, step - 1, index],
-                    ring_recv.at[phase, step - 1, index],
-                    target,
-                )
-                copy.start()
-                rounds[(phase, step, index)] = copy
-
-    for split, pieces_of in enumerate(pieces):
-        for index, (number, rows) in pieces_of:
-            cross, own = crossing[index]
-            own.wait()
-            cross.wait_recv()
-            start, length = rows
-
-            def other(spot, number=number, start=start, length=length):
-                return crosses[number][spot["xh"], spot["y"], spot["z"], spot["xl"], pl.ds(start, length), :].astype(jnp.float32)
-
-            add_into(number, rows, place, "xyz", [other])
-        launch(0, split, pieces_of)
-    for phase in range(3):
-        for split, pieces_of in enumerate(pieces):
-            order = ORDERS[split]
-            rest = "".join(order[phase + 1 :])
-            for index, (number, rows) in pieces_of:
-                others = []
-                for step in (1, 2, 3):
-                    rounds[(phase, step, index)].wait_recv()
-
-                    def other(spot, step=step, index=index, rest=rest):
-                        return rings[phase][index][(step - 1,) + open_index(spot, rest)].astype(jnp.float32)
-
-                    others.append(other)
-                if phase < 2:
-                    add_into(number, rows, place, rest, others)
-                else:
-                    start, length = rows
-                    spot = spot_of(0, "", place)
-                    value = accs[number][spot["xh"], spot["y"], spot["z"], spot["xl"], pl.ds(start, length), :].astype(jnp.float32)
-                    for item in others:
-                        value = value + item(spot)
-                    outs[number][pl.ds(start, length), :] = value
-            if phase < 2:
-                launch(phase + 1, split, pieces_of)
-    for cross, own in crossing.values():
-        cross.wait_send()
-    for copy in rounds.values():
-        copy.wait_send()
-
-
-def reduce_slots(arrays, splits, collective_id):
-    pieces, total = number_pieces(splits)
-    count = len(arrays)
-    shapes = [a.shape[1:] for a in arrays]
-    dtype = arrays[0].dtype
-    arrays = [a.reshape((2, 4, 4, 2, 2) + s) for a, s in zip(arrays, shapes)]
-    scratch = [pltpu.VMEM((2, 4, 4, 2) + s, dtype) for s in shapes] * 2
-    for phase in range(3):
-        for split, pieces_of in enumerate(pieces):
-            rest = "".join(ORDERS[split][phase + 1 :])
-            for index, (number, rows) in pieces_of:
-                scratch.append(pltpu.VMEM((3,) + open_shape(rest) + (rows[1], shapes[number][1]), dtype))
-    scratch += [
-        pltpu.SemaphoreType.DMA((total,)),
-        pltpu.SemaphoreType.DMA((total,)),
-        pltpu.SemaphoreType.DMA((total,)),
-        pltpu.SemaphoreType.DMA((3, 3, total)),
-        pltpu.SemaphoreType.DMA((3, 3, total)),
-    ]
-    return pl.pallas_call(
-        functools.partial(slot_reduce_kernel, pieces, count, total),
-        out_shape=[jax.ShapeDtypeStruct(s, jnp.float32) for s in shapes],
-        in_specs=[pl.BlockSpec(memory_space=pl.ANY)] * count,
-        out_specs=[pl.BlockSpec(memory_space=pltpu.VMEM)] * count,
-        scratch_shapes=scratch,
-        compiler_params=pltpu.CompilerParams(
-            collective_id=collective_id, has_side_effects=True, vmem_limit_bytes=56 * 1024 * 1024
-        ),
-    )(*arrays)
-
-
 def merge_parts(parts):
     top = parts[0][0]
     for part in parts[1:]:
@@ -745,7 +458,6 @@
 CLIP = 0.05
 LOW = jnp.bfloat16
 SPAN_LOW = 256
-HEAD_BLOCK = 512
 TOKEN_BLOCK = 1024
 
 
@@ -1019,7 +731,7 @@
     parts_ref, slot_text, slot_layout, out_w, up_w, down_w, layout_ref, layout_down,
     text_vec, layout_vec, head_ref, head_vec,
     att_text, att_layout, log_ref, mid_text, mid_layout, pre_text, pre_layout,
-    end_text, end_layout, joined_ref, dense_ref, pick0, pick1, pick2,
+    end_text, end_layout, joined_ref, dense_ref, pick_ref,
 ):
     tops = [parts_ref[j, :, pl.ds(1024, 128)] for j in range(4)]
     top = jnp.maximum(jnp.maximum(tops[0], tops[1]), jnp.maximum(tops[2], tops[3]))
@@ -1059,21 +771,20 @@
         ).astype(LOW)
     dense = cols_product(joined_ref[:, pl.ds(0, 960)], head_ref[...]) + row_of(head_vec, 0)
     dense_ref[...] = dense
-    picked = norm_apply(gelu_value(dense), row_of(head_vec, 1), row_of(head_vec, 2)).astype(LOW)
-    for k, ref in enumerate((pick0, pick1, pick2)):
-        ref[...] = picked[:, 256 * k : 256 * k + 256]
+    pick_ref[...] = norm_apply(
+        gelu_value(dense), row_of(head_vec, 1), row_of(head_vec, 2)
+    ).astype(LOW)
 
 
 def close_back_kernel(
-    grad0, grad1, grad2, dense_ref, joined_ref, att_text, att_layout, log_ref, mid_text, mid_layout,
+    grad_ref, dense_ref, joined_ref, att_text, att_layout, log_ref, mid_text, mid_layout,
     pre_text, pre_layout, end_text, end_layout, out_w, up_w, down_w, layout_ref, layout_down,
     text_vec, layout_vec, head_ref, head_vec,
     back_ref, d_mid_text, d_mid_layout, d_head, d_out, d_up, d_down, d_layout, d_layout_down,
     d_text_vec, d_layout_vec, d_head_vec,
 ):
-    d_picked = jnp.concatenate([grad0[...], grad1[...], grad2[...]], 1)
     dense = dense_ref[...]
-    d_active, d_gain, d_shift = norm_back(gelu_value(dense), row_of(head_vec, 1), d_picked)
+    d_active, d_gain, d_shift = norm_back(gelu_value(dense), row_of(head_vec, 1), grad_ref[...])
     d_dense = (d_active * gelu_slope(dense)).astype(LOW)
     d_head_vec[0:1, :] = total_rows(d_dense)
     d_head_vec[1:2, :] = d_gain
@@ -1233,6 +944,274 @@
     )(*arrays)
 
 
+PLANES = (("y", "z"), ("x", "z"), ("x", "y"))
+LINES = ("x", "y", "z")
+HEAD_BLOCK = 512
+PLANE_STEPS = [(a, b) for a in range(4) for b in range(4) if (a, b) != (0, 0)]
+
+
+def plane_peer(place, plane, a, b):
+    return moved(moved(place, plane[0], a), plane[1], b)
+
+
+def head_peers(place):
+    peers = [
+        plane_peer(place, plane, a, b)
+        for plane in PLANES
+        for a, b in PLANE_STEPS
+        if (a and b) or plane == ("y", "z")
+    ]
+    peers += [moved(place, "x", step) for step in (1, 2, 3)]
+    peers += [moved(moved(place, "x", step), "c", 1) for step in range(4)]
+    return peers
+
+
+def merge_logs(logs):
+    top = logs[0]
+    for item in logs[1:]:
+        top = jnp.maximum(top, item)
+    total = jnp.exp(logs[0] - top)
+    for item in logs[1:]:
+        total = total + jnp.exp(item - top)
+    return top + jnp.log(total)
+
+
+def head_kernel(
+    limit_width, pick_ref, table_ref, label_ref, weight_ref, count_ref,
+    grad_ref, d_table_ref, loss_ref,
+    picked, table, logits, d_logits, part, acc, cross, near, far, line_in, plane_in, own_sem,
+    plane_send, plane_recv, line_send, line_recv, pass_send, pass_recv,
+    near_send, near_recv, far_send, far_recv, core_send, core_recv,
+    back_send, back_recv, last_send, last_recv,
+):
+    place = my_place()
+    sibling = moved(place, "c", 1)
+    barrier = pltpu.get_barrier_semaphore()
+    peers = head_peers(place)
+    for peer in peers:
+        pl.semaphore_signal(barrier, inc=1, device_id=device_of(peer), device_id_type=MESH)
+    own = pltpu.make_async_copy(
+        pick_ref, block_view(picked, place, "", None, place["c"]), own_sem
+    )
+    own.start()
+    pl.semaphore_wait(barrier, len(peers))
+    sends = []
+
+    def go(copy):
+        copy.start()
+        sends.append(copy)
+        return copy
+
+    def third(k):
+        return (256 * k, 256)
+
+    flights = {}
+    for k in range(3):
+        here = block_view(picked, place, "", third(k), place["c"])
+        for a, b in PLANE_STEPS:
+            n = 4 * a + b - 1
+            flights[(k, n)] = go(
+                remote(
+                    pick_ref.at[:, pl.ds(*third(k))], here, plane_send.at[k, n],
+                    plane_recv.at[k, n], plane_peer(place, PLANES[k], a, b),
+                )
+            )
+    table[...] = table_ref[...].astype(jnp.float32).T.astype(LOW)
+    own.wait()
+    lines, passes = {}, []
+
+    def hand_over(k, n, where):
+        passes.append(go(remote(where, where, pass_send.at[k, n], pass_recv.at[k, n], sibling)))
+
+    for k in range(3):
+        for a, b in PLANE_STEPS:
+            flights[(k, 4 * a + b - 1)].wait_recv()
+        sheet = block_view(picked, place, PLANES[k], third(k), place["c"])
+        for step in (1, 2, 3):
+            lines[(k, step)] = go(
+                remote(
+                    sheet, sheet, line_send.at[k, step - 1], line_recv.at[k, step - 1],
+                    moved(place, LINES[k], step),
+                )
+            )
+        hand_over(k, 0, sheet)
+    for step in (1, 3, 2):
+        for k in range(3):
+            lines[(k, step)].wait_recv()
+            origin = moved(place, LINES[k], -step)
+            hand_over(k, step, block_view(picked, origin, PLANES[k], third(k), place["c"]))
+    for copy in passes:
+        copy.wait_recv()
+
+    limit = limit_width - lax.axis_index("dp") * HEAD_BLOCK
+    row = lax.broadcasted_iota(jnp.int32, (HEAD_BLOCK, 256), 0)
+    valid = row < limit
+    mine = place["x"] * 2 + place["c"]
+    for chunk in range(8):
+        high, mid = chunk // 4, chunk % 4
+        lanes = pl.ds(256 * chunk, 256)
+        values = cols_product(table[...], picked[high, mid].reshape(256, 768))
+        values = jnp.where(valid, values, NEGATIVE)
+        logits[:, lanes] = values
+        top = jnp.max(values, 0, keepdims=True)
+        total = jnp.sum(jnp.where(valid, jnp.exp(values - top), 0.0), 0, keepdims=True)
+        hot = valid & (row == label_ref[:, lanes])
+        near[mine, 0, :, lanes] = top + jnp.log(jnp.maximum(total, 1e-30))
+        near[mine, 1, :, lanes] = jnp.sum(jnp.where(hot, values, 0.0), 0, keepdims=True)
+    meets = []
+    for n in range(1, 8):
+        peer = moved(place, "x", n // 2)
+        if n % 2:
+            peer = moved(peer, "c", 1)
+        meets.append(
+            go(remote(near.at[mine], near.at[mine], near_send.at[n - 1], near_recv.at[n - 1], peer))
+        )
+    for copy in meets:
+        copy.wait_recv()
+    spot = place["y"] * 4 + place["z"]
+    far[spot, 0] = merge_logs([near[n, 0] for n in range(8)])
+    far[spot, 1] = sum(near[n, 1] for n in range(8))
+    meets = []
+    for a, b in PLANE_STEPS:
+        n = 4 * a + b - 1
+        peer = plane_peer(place, ("y", "z"), a, b)
+        meets.append(go(remote(far.at[spot], far.at[spot], far_send.at[n], far_recv.at[n], peer)))
+    for copy in meets:
+        copy.wait_recv()
+    log_total = merge_logs([far[n, 0] for n in range(16)])
+    target = sum(far[n, 1] for n in range(16))
+    loss = jnp.sum(count_ref[...] * (log_total - target), 1, keepdims=True)
+    loss_ref[...] = jnp.broadcast_to(loss, loss_ref.shape)
+
+    crossings = []
+    for chunk in range(8):
+        high, mid = chunk // 4, chunk % 4
+        lanes = pl.ds(256 * chunk, 256)
+        here = slice(256 * chunk, 256 * chunk + 256)
+        hot = (valid & (row == label_ref[:, lanes])).astype(jnp.float32)
+        powers = jnp.where(valid, jnp.exp(logits[:, lanes] - log_total[:, here]), 0.0)
+        low = (weight_ref[:, lanes] * (powers - hot)).astype(LOW)
+        d_logits[:, lanes] = low
+        part[high, mid] = rows_product(low, table[...]).astype(LOW).reshape(4, 2, 2, 16, 768)
+        crossings.append(
+            go(
+                remote(
+                    part.at[high, mid, :, :, sibling["c"]], cross.at[high, mid],
+                    core_send.at[chunk], core_recv.at[chunk], sibling,
+                )
+            )
+        )
+    for chunk in range(8):
+        high, mid = chunk // 4, chunk % 4
+        crossings[chunk].wait_recv()
+        acc[high, mid] = part[high, mid, :, :, place["c"]] + cross[high, mid]
+
+    legs = {}
+    for k in range(3):
+        for step in (1, 3, 2):
+            there = moved(place, LINES[k], step)
+            legs[(k, step)] = go(
+                remote(
+                    block_view(acc, there, PLANES[k], third(k)), line_in[k].at[step - 1],
+                    back_send.at[k, step - 1], back_recv.at[k, step - 1], there,
+                )
+            )
+    d_table = jnp.zeros((HEAD_BLOCK, 768), jnp.float32)
+    for chunk in range(8):
+        d_table = d_table + plain_product(
+            d_logits[:, pl.ds(256 * chunk, 256)], picked[chunk // 4, chunk % 4].reshape(256, 768)
+        )
+    d_table_ref[...] = d_table.T.astype(LOW)
+    ends = {}
+    for k in range(3):
+        for step in (1, 2, 3):
+            legs[(k, step)].wait_recv()
+        count, chunk_of = chunks_of("".join(PLANES[k]), place)
+        for flat in range(count):
+            block, inner = chunk_of(flat)
+            where = block + (slice(None), pl.ds(*third(k)))
+            total = acc[where].astype(jnp.float32)
+            for step in (1, 2, 3):
+                total = total + line_in[k][(step - 1,) + inner].astype(jnp.float32)
+            acc[where] = total.astype(LOW)
+        for a, b in PLANE_STEPS:
+            n = 4 * a + b - 1
+            there = plane_peer(place, PLANES[k], a, b)
+            ends[(k, n)] = go(
+                remote(
+                    block_view(acc, there, "", third(k)), plane_in.at[k, n],
+                    last_send.at[k, n], last_recv.at[k, n], there,
+                )
+            )
+    home = (place["x"] // 2, place["y"], place["z"], place["x"] % 2)
+    for k in range(3):
+        total = acc[home + (slice(None), pl.ds(*third(k)))].astype(jnp.float32)
+        for n in range(15):
+            ends[(k, n)].wait_recv()
+            total = total + plane_in[k, n].astype(jnp.float32)
+        grad_ref[:, pl.ds(*third(k))] = total
+    for copy in sends:
+        copy.wait_send()
+
+
+def head_step(picked, table, labels, weights, counts, width, collective_id):
+    sems = pltpu.SemaphoreType.DMA
+    everyone = (2, 4, 4, 2, 2, 16, 768)
+    half = (2, 4, 4, 2, 16, 768)
+    line_slots = [
+        pltpu.VMEM((3,) + open_shape("".join(PLANES[k])) + (16, 256), LOW) for k in range(3)
+    ]
+
+    def kernel(*refs):
+        head_kernel(width, *refs[:17], refs[17:20], *refs[20:])
+
+    return pl.pallas_call(
+        kernel,
+        out_shape=[
+            jax.ShapeDtypeStruct((16, 768), jnp.float32),
+            jax.ShapeDtypeStruct((768, HEAD_BLOCK), LOW),
+            jax.ShapeDtypeStruct((8, 128), jnp.float32),
+        ],
+        in_specs=[pl.BlockSpec(memory_space=pltpu.VMEM)] * 5,
+        out_specs=[pl.BlockSpec(memory_space=pltpu.VMEM)] * 3,
+        scratch_shapes=[
+            pltpu.VMEM(everyone, LOW),
+            pltpu.VMEM((HEAD_BLOCK, 768), LOW),
+            pltpu.VMEM((HEAD_BLOCK, 2048), jnp.float32),
+            pltpu.VMEM((HEAD_BLOCK, 2048), LOW),
+            pltpu.VMEM(everyone, LOW),
+            pltpu.VMEM(half, LOW),
+            pltpu.VMEM(half, LOW),
+            pltpu.VMEM((8, 2, 1, 2048), jnp.float32),
+            pltpu.VMEM((16, 2, 1, 2048), jnp.float32),
+        ]
+        + line_slots
+        + [
+            pltpu.VMEM((3, 15, 16, 256), LOW),
+            sems(()),
+            sems((3, 15)),
+            sems((3, 15)),
+            sems((3, 3)),
+            sems((3, 3)),
+            sems((3, 4)),
+            sems((3, 4)),
+            sems((7,)),
+            sems((7,)),
+            sems((15,)),
+            sems((15,)),
+            sems((8,)),
+            sems((8,)),
+            sems((3, 3)),
+            sems((3, 3)),
+            sems((3, 15)),
+            sems((3, 15)),
+        ],
+        compiler_params=pltpu.CompilerParams(
+            collective_id=collective_id, has_side_effects=True, vmem_limit_bytes=56 * 1024 * 1024
+        ),
+    )(picked, table, labels, weights, counts)
+
+
 def thirds(number):
     return [(number, (256 * k, 256), k) for k in range(3)]
 
@@ -1250,7 +1229,6 @@
     (0, (0, 1), (3, 1)),
     (0, (1, 1), (0, 4)),
 ] + [(number,) + WHOLE for number in range(1, 9)]
-SLOT_SPLITS = [[(0, (0, 16))], [(1, (0, 16))], [(2, (0, 16))]]
 
 
 def fetch(masters):
@@ -1439,7 +1417,7 @@
     weights_close = [out_w, up_w, full["down"], full["layout"], full["layout_down"]]
     vectors_close = [text_vec, layout_vec, full["head"], head_vec]
     (att_text, att_layout, log_total, mid_text, mid_layout, pre_text, pre_layout, end_text,
-     end_layout, joined, dense, *picked) = local_call(
+     end_layout, joined, dense, picked) = local_call(
         close_kernel,
         [partial, slot_text, slot_layout] + weights_close + vectors_close,
         [
@@ -1454,51 +1432,28 @@
             ((16, 192), f32),
             ((16, 1024), LOW),
             ((16, 768), f32),
-            ((16, 256), LOW),
-            ((16, 256), LOW),
-            ((16, 256), LOW),
+            ((16, 768), LOW),
         ],
         "close_streams",
     )
-    picked_all = gather_slots(picked, SLOT_SPLITS, 3)
-    picked_all = jnp.concatenate([p.reshape(2048, 256) for p in picked_all], 1)
-    column = lax.broadcasted_iota(jnp.int32, (1, HEAD_BLOCK), 1)
-    valid = column < shard_width - dp * HEAD_BLOCK
-    logits = jnp.where(valid, plain_product(picked_all, table_head), -1e30)
-    row_max = jnp.max(logits, 1)
-    row_sum = jnp.sum(jnp.where(valid, jnp.exp(logits - row_max[:, None]), 0.0), 1)
-    label_hot = valid & (
-        (labels_all - vocab * shard_width - dp * HEAD_BLOCK)[:, None] == column
-    )
-    target = jnp.sum(jnp.where(label_hot, logits, 0.0), 1)
-    stats = jnp.concatenate(
-        [row_max.reshape(16, 128), row_sum.reshape(16, 128), target.reshape(16, 128)], 0
-    )
-    stats = merge_stats(stats, 4)
-    row_log = (stats[:16] + jnp.log(stats[16:32])).reshape(2048)
-    loss_total = jnp.sum(counted_all * (row_log - stats[32:].reshape(2048)))
-    d_logits = (
-        (counted_all / total_count)[:, None]
-        * (
-            jnp.where(valid, jnp.exp(logits - row_log[:, None]), 0.0)
-            - label_hot.astype(jnp.float32)
-        )
-    ).astype(LOW)
-    d_picked_part = cols_product(d_logits, table_head).astype(LOW)
-    d_picked = reduce_slots(
-        [d_picked_part[:, 256 * k : 256 * (k + 1)].reshape(128, 16, 256) for k in range(3)],
-        SLOT_SPLITS,
-        5,
-    )
-    table_head_grad = rows_product(picked_all, d_logits).astype(LOW).reshape(32, 24, HEAD_BLOCK)
-    table_head_grad = lax.all_to_all(table_head_grad, "dp", 0, 0, tiled=True)
-
+    d_picked, table_head_grad, loss = head_step(
+        picked,
+        table_head,
+        (labels_all - vocab * shard_width - dp * HEAD_BLOCK)[None],
+        (counted_all / total_count)[None],
+        counted_all[None],
+        shard_width,
+        3,
+    )
+    loss_total = loss[0, 0]
+    table_head_grad = lax.all_to_all(
+        table_head_grad.reshape(32, 24, HEAD_BLOCK), "dp", 0, 0, tiled=True
+    )
     (back, d_mid_text, d_mid_layout, d_head, d_out, d_up, d_down, d_layout_close, d_layout_down,
      d_text_vec, d_layout_vec, d_head_vec) = local_call(
         close_back_kernel,
-        list(d_picked)
-        + [dense, joined, att_text, att_layout, log_total, mid_text, mid_layout, pre_text]
-        + [pre_layout, end_text, end_layout]
+        [d_picked, dense, joined, att_text, att_layout, log_total, mid_text, mid_layout]
+        + [pre_text, pre_layout, end_text, end_layout]
         + weights_close
         + vectors_close,
         [

time: 481 us -> 459 us (0.954); the launches traced: 472 us -> 456 us
  matrix products: 15.8 us -> 0 us
  blocking collectives: 13 us -> 25.6 us
  Pallas kernels: 309 us -> 297 us
    pallas_call x2 -> x1, Pallas kernels: 32.8 us -> 16.2 us  [merge_stats(): pl.pallas_call(stats_kernel, out_shape=jax.ShapeDtypeStruct((48, 128), jn...]
    dot_general x3 -> x0, matrix products: 15.8 us -> none  [the longest x1 6.29 us: rows_product(): lax.dot_general(left, right, (((0,), (0,)), ((), ())), preferred_element_...]
    all_gather x1, blocking collectives: 6.42 us -> 18.9 us  [on_device(): query_all = lax.all_gather(query, 'vocab', axis=0, tiled=True)]
    pallas_call x2 -> x1, Pallas kernels: 58.9 us -> 59.3 us  [head_step(): pl.pallas_call(kernel, out_shape=[jax.ShapeDtypeStruct((16, 768), jnp.flo...]
  transfers between devices with their start and end apart: 7 -> 7, of which waited for: 2 -> 3; matrix products, arithmetic and copies ran while one was open for 10% -> 10% of each run, Pallas kernels for 39% -> 36%
where the time goes in v1:
time: 459 us; the launch traced here: 456 us
  Pallas kernels  297 us (65%)
  starting transfers between devices  48 us (10%)
  local copies, waits for them, and re-layouts  43.4 us (9%)
  other arithmetic  27.4 us (6%)
  blocking collectives  25.6 us (6%)
  waiting for transfers between devices  11.3 us (2%)
    pallas_call x1, Pallas kernels, reduce_all(): pl.pallas_call(functools.partial(reduce_kernel, sources, pieces, count),...  77.1 us
    pallas_call x1, Pallas kernels, gather_all(): pl.pallas_call(functools.partial(gather_kernel, pieces, count), out_shape...  67.5 us
    pallas_call x1, Pallas kernels, head_step(): pl.pallas_call(kernel, out_shape=[jax.ShapeDtypeStruct((16, 768), jnp.flo...  59.3 us
    pallas_call x6, Pallas kernels, local_call(): pl.pallas_call(kernel, name=name, grid=(1,), out_shape=[jax.ShapeDtypeStr...  46.3 us
    all_gather x1, blocking collectives, on_device(): query_all = lax.all_gather(query, 'vocab', axis=0, tiled=True)  18.9 us
    pallas_call x1, Pallas kernels, merge_stats(): pl.pallas_call(stats_kernel, out_shape=jax.ShapeDtypeStruct((48, 128), jn...  16.2 us
    pallas_call x1, Pallas kernels, pick_columns(): pl.pallas_call(functools.partial(pick_kernel, levels, rows), grid=(tokens...  15.8 us
    pallas_call x1, Pallas kernels, spread_columns(): pl.pallas_call(functools.partial(spread_kernel, levels, rows), grid=(toke...  14.5 us
  transfers between devices with their start and end apart: 7, of which 3 were waited for; matrix products, arithmetic and copies ran while one was open for 10% of the time, Pallas kernels for 36%

profile of v1, /device:TPU:0, one launch (start us, length us, event | category | flops | bytes accessed | tf_op | source)
XLA Modules:
  0.0 456.1 jit_solution(5588295802282134267)
XLA Ops:
  4.6 11.1 %all-to-all-start = ((s32[128,2,128]{2,1,0:T(2,128)}), s32[128,2,128]{2,1,0:T(2,128)S(1)}, u32[]{:S(2)}, u32[]{:S(2)}) async-start(s32[128,2,128]{2,1,0:T(2,128)} %broadcast_in_dim.39), calls=%async_computation | async-start | bytes 262144 | tf_op jit(solution)/shard_map/all_to_all | solution.py:1334
  21.0 4.2 all-to-all-done
  25.3 15.8 %shard_map.535 = bf16[128,24,128]{2,1,0:T(8,128)(2,1)} custom-call(bf16[1200,256]{1,0:T(8,128)(2,1)S(1)} %bitcast.111, s32[1,16384]{1,0:T(1,128)S(1)} %get-tuple-element.363.high_ref, s32[1,16384]{1,0:T(1,128)S(1)} %get-tuple-element.362.low_ref), custom_call_target="tpu_custom_call" | custom-call | tf_op jit(solution)/shard_map/pallas_call | solution.py:487
  44.3 5.6 %all-to-all-start.1 = ((bf16[128,24,128]{2,1,0:T(8,128)(2,1)}), bf16[128,24,128]{2,1,0:T(8,128)(2,1)S(1)}, u32[]{:S(2)}, u32[]{:S(2)}) async-start(bf16[128,24,128]{2,1,0:T(8,128)(2,1)} %shard_map.535), calls=%async_computation.1 | async-start | bytes 1572864 | tf_op jit(solution)/shard_map/all_to_all | solution.py:1354
  50.5 67.5 %shard_map.536 = (bf16[2,4,4,2,2,48,768]{6,5,4,3,2,1,0:T(8,128)(2,1)}, bf16[2,4,4,2,2,24,768]{6,5,4,3,2,1,0:T(8,128)(2,1)}, bf16[2,4,4,2,2,6,960]{6,5,4,3,2,1,0:...) custom-call(bf16[48,768]{1,0:T(8,128)(2,1)} %convert_bitcast_fusion., ...), custom_call_target="tpu_custom_call" | custom-call | flops 60000002048 | bytes 200000000 | tf_op jit(solution)/shard_map/pallas_call | solution.py:156
  120.4 3.8 reshape_reshape.46
  135.5 5.8 %open_streams.1 = (f32[128,768]{1,0:T(8,128)}, f32[128,192]{1,0:T(8,128)}, bf16[128,768]{1,0:T(8,128)(2,1)}, bf16[128,768]{1,0:T(8,128)(2,1)}, bf16[128,768]{1,0...) custom-call(bf16[128,24,128]{2,1,0:T(8,128)(2,1)} %copy-done.6, ...), custom_call_target="tpu_custom_call" | custom-call | tf_op jit(solution)/shard_map/open_streams/pallas_call | solution.py:936
  141.3 18.9 %all_gather.6.query_ref = bf16[64,1024]{1,0:T(8,128)(2,1)} all-gather(bf16[16,1024]{1,0:T(8,128)(2,1)} %get-tuple-element.119), channel_id=1, replica_groups=mesh['dp'=32,'vocab'=4] {'vocab'}, dimensions={0}, use_global_device_ids=true | all-gather | bytes 163840 | tf_op jit(solution)/shard_map/all_gather | solution.py:1414
  163.4 3.5 all-to-all-start.2
  167.9 5.7 %all-to-all-done.2.parts_ref = f32[4,16,1280]{2,1,0:T(8,128)S(1)} async-done(((f32[4,16,1280]{2,1,0:T(8,128)}), f32[4,16,1280]{2,1,0:T(8,128)S(1)}, u32[]{:S(2)}, u32[]{:S(2)}) %all-to-all-start.2) | async-done | bytes 327712 | tf_op jit(solution)/shard_map/all_to_all | solution.py:1416
  174.3 7.9 %all-to-all-start.3 = ((bf16[32,24,512]{2,1,0:T(8,128)(2,1)}), bf16[32,24,512]{2,1,0:T(8,128)(2,1)S(1)}, u32[]{:S(2)}, u32[]{:S(2)}) async-start(bf16[32,24,512]{2,1,0:T(8,128)(2,1)} %bitcast.109), calls=%async_computation.3 | async-start | bytes 1572864 | tf_op jit(solution)/shard_map/all_to_all | solution.py:1361
  189.5 10.3 %close_streams.1 = (f32[16,768]{1,0:T(8,128)}, f32[16,192]{1,0:T(8,128)}, f32[16,128]{1,0:T(8,128)}, f32[16,768]{1,0:T(8,128)}, f32[16,192]{1,0:T(8,128)}, /*ind...) custom-call(f32[4,16,1280]{2,1,0:T(8,128)} %copy-done.10, ...), custom_call_target="tpu_custom_call" | custom-call | tf_op jit(solution)/shard_map/close_streams/pallas_call | solution.py:936
  200.7 59.3 %shard_map.537 = (f32[16,768]{1,0:T(8,128)}, bf16[768,512]{1,0:T(8,128)(2,1)}, f32[8,128]{1,0:T(8,128)}) custom-call(bf16[16,768]{1,0:T(8,128)(2,1)} %get-tuple-element.128.refs_0_, bf16[768,512]{1,0:T(8,128)(2,1)} %bitcast.126, s32[1,2048]{1,0:T(1,128)} %sub.104.refs_2_, f32[1,2048]{1,0:T(1,128)} %broadcast_divide_fusion.refs_3_, f32[1,2048]{1,0:T(1,128)} %copy-done.30), custom_call_target="tpu_custom_call" | custom-call | tf_op jit(solution)/shard_map/pallas_call | solution.py:1168
  260.0 15.5 %close_streams_back.1 = (f32[16,1280]{1,0:T(8,128)}, f32[16,768]{1,0:T(8,128)}, f32[16,192]{1,0:T(8,128)}, bf16[768,960]{1,0:T(8,128)(2,1)}, bf16[768,768]{1,0:T...) custom-call(f32[16,768]{1,0:T(8,128)} %get-tuple-element.129.grad_re, ...), custom_call_target="tpu_custom_call" | custom-call | tf_op jit(solution)/shard_map/close_streams_back/pallas_call | solution.py:936
  275.6 6.8 %all_gather.7.back_ref = f32[64,1280]{1,0:T(8,128)} all-gather(f32[16,1280]{1,0:T(8,128)} %get-tuple-element.141), channel_id=1, replica_groups=mesh['dp'=32,'vocab'=4] {'vocab'}, dimensions={0}, use_global_device_ids=true | all-gather | bytes 409600 | tf_op jit(solution)/shard_map/all_gather | solution.py:1475
  282.3 4.0 attention_back.1
  286.4 3.4 all-to-all-start.4
  295.8 6.3 %all-to-all-start.6 = ((bf16[32,24,512]{2,1,0:T(8,128)(2,1)}), bf16[32,24,512]{2,1,0:T(8,128)(2,1)S(1)}, u32[]{:S(2)}, u32[]{:S(2)}) async-start(bf16[32,24,512]{2,1,0:T(8,128)(2,1)} %bitcast.137), calls=%async_computation.6 | async-start | bytes 1572864 | tf_op jit(solution)/shard_map/all_to_all | solution.py:1449
  302.1 7.4 %open_streams_back.1 = (bf16[768,768]{1,0:T(8,128)(2,1)}, bf16[1536,768]{1,0:T(8,128)(2,1)}, bf16[576,192]{1,0:T(8,128)(2,1)}, bf16[768,128]{1,0:T(8,128)(2,1)},...) custom-call(f32[4,16,1024]{2,1,0:T(8,128)} %copy-done.11, ...), custom_call_target="tpu_custom_call" | custom-call | tf_op jit(solution)/shard_map/open_streams_back/pallas_call | solution.py:936
  320.7 10.3 %all-to-all-start.5 = ((bf16[128,24,128]{2,1,0:T(8,128)(2,1)}), bf16[128,24,128]{2,1,0:T(8,128)(2,1)S(1)}, u32[]{:S(2)}, u32[]{:S(2)}) async-start(bf16[128,24,128]{2,1,0:T(8,128)(2,1)} %bitcast.32), calls=%async_computation.5 | async-start | bytes 1572864 | tf_op jit(solution)/shard_map/all_to_all | solution.py:1511
  330.9 77.1 %shard_map.538 = (f32[48,768]{1,0:T(8,128)}, f32[24,768]{1,0:T(8,128)}, f32[6,960]{1,0:T(8,128)}, f32[5,960]{1,0:T(8,128)}, f32[12,192]{1,0:T(8,128)}, /*index=5...) custom-call(bf16[1,1,4,2,2,48,768]{6,5,4,3,2,1,0:T(8,128)(2,1)} %bitcast.147, ...), custom_call_target="tpu_custom_call" | custom-call | flops 60000002048 | bytes 200000000 | tf_op jit(solution)/shard_map/pallas_call | solution.py:365
  408.9 14.5 %shard_map.539 = f32[1200,256]{1,0:T(8,128)S(1)} custom-call(bf16[128,24,128]{2,1,0:T(8,128)(2,1)S(1)} %all-to-all-done.5.grad_ref, s32[1,16384]{1,0:T(1,128)S(1)} %copy-done.3, s32[1,16384]{1,0:T(1,128)S(1)} %copy-done.1), custom_call_target="tpu_custom_call" | custom-call | tf_op jit(solution)/shard_map/pallas_call | solution.py:531
  425.8 16.2 %shard_map.540 = f32[48,128]{1,0:T(8,128)} custom-call(f32[48,128]{1,0:T(8,128)} %pad_maximum_fusion.2.in_ref), custom_call_target="tpu_custom_call" | custom-call | tf_op jit(solution)/shard_map/pallas_call | solution.py:439
  446.0 4.0 multiply_add_fusion
  (236 shorter events, 67.7 us)
Async XLA Ops:
  4.6 20.5 %all-to-all-start = ((s32[128,2,128]{2,1,0:T(2,128)}), s32[128,2,128]{2,1,0:T(2,128)S(1)}, u32[]{:S(2)}, u32[]{:S(2)}) async-start(s32[128,2,128]{2,1,0:T(2,128)} %broadcast_in_dim.39), calls=%async_computation | async-start | bytes 262144 | tf_op jit(solution)/shard_map/all_to_all | solution.py:1334
  19.4 21.6 %copy-start.39 = (f32[2,6,192]{2,0,1:T(2,128)S(1)}, f32[2,6,192]{2,0,1:T(2,128)}, u32[]{:S(2)}) copy-start(f32[2,6,192]{2,0,1:T(2,128)} %param.55) | copy-start | bytes 27652
  19.5 21.7 %copy-start.35 = (f32[192,12]{0,1:T(8,128)S(1)}, f32[192,12]{0,1:T(8,128)}, u32[]{:S(2)}) copy-start(f32[192,12]{0,1:T(8,128)} %param.52) | copy-start | bytes 27652
  19.5 21.7 %copy-start.61 = (f32[123]{0:T(128)S(1)}, f32[123]{0:T(128)}, u32[]{:S(2)}) copy-start(f32[123]{0:T(128)} %param.61) | copy-start | bytes 1480
  19.5 21.7 %copy-start.13 = (f32[768,48]{0,1:T(8,128)S(1)}, f32[768,48]{0,1:T(8,128)}, u32[]{:S(2)}) copy-start(f32[768,48]{0,1:T(8,128)} %param.46) | copy-start | bytes 442372
  19.5 22.3 %copy-start.18 = (f32[24,768]{1,0:T(8,128)S(1)}, f32[24,768]{1,0:T(8,128)}, u32[]{:S(2)}) copy-start(f32[24,768]{1,0:T(8,128)} %param.49) | copy-start | bytes 221188
  19.5 22.9 %copy-start.26 = (f32[960,6]{0,1:T(8,128)S(1)}, f32[960,6]{0,1:T(8,128)}, u32[]{:S(2)}) copy-start(f32[960,6]{0,1:T(8,128)} %param.58) | copy-start | bytes 69124
  19.5 23.5 %copy-start.28 = (f32[5,960]{1,0:T(8,128)S(1)}, f32[5,960]{1,0:T(8,128)}, u32[]{:S(2)}) copy-start(f32[5,960]{1,0:T(8,128)} %param.40) | copy-start | bytes 57604
  19.5 24.1 %copy-start.37 = (f32[4,8,128]{2,1,0:T(8,128)S(1)}, f32[4,8,128]{2,1,0:T(8,128)}, u32[]{:S(2)}) copy-start(f32[4,8,128]{2,1,0:T(8,128)} %param.43) | copy-start | bytes 49156
  25.3 15.8 %copy-start = (s32[1,16384]{1,0:T(1,128)}, s32[1,16384]{1,0:T(1,128)S(1)}, u32[]{:S(2)}) copy-start(s32[1,16384]{1,0:T(1,128)S(1)} %get-tuple-element.362.low_ref) | copy-start | bytes 196612
  25.3 15.8 %copy-start.2 = (s32[1,16384]{1,0:T(1,128)}, s32[1,16384]{1,0:T(1,128)S(1)}, u32[]{:S(2)}) copy-start(s32[1,16384]{1,0:T(1,128)S(1)} %get-tuple-element.363.high_ref) | copy-start | bytes 196612
  44.3 90.4 %all-to-all-start.1 = ((bf16[128,24,128]{2,1,0:T(8,128)(2,1)}), bf16[128,24,128]{2,1,0:T(8,128)(2,1)S(1)}, u32[]{:S(2)}, u32[]{:S(2)}) async-start(bf16[128,24,128]{2,1,0:T(8,128)(2,1)} %shard_map.535), calls=%async_computation.1 | async-start | bytes 1572864 | tf_op jit(solution)/shard_map/all_to_all | solution.py:1354
  163.4 10.2 %all-to-all-start.2 = ((f32[4,16,1280]{2,1,0:T(8,128)}), f32[4,16,1280]{2,1,0:T(8,128)S(1)}, u32[]{:S(2)}, u32[]{:S(2)}) async-start(f32[4,16,1280]{2,1,0:T(8,128)} %bitcast.133), calls=%async_computation.2 | async-start | bytes 655360 | tf_op jit(solution)/shard_map/all_to_all | solution.py:1416
  166.9 15.9 %copy-start.8 = (bf16[128,6,192]{2,1,0:T(8,128)(2,1)S(1)}, bf16[128,6,192]{2,1,0:T(8,128)(2,1)}, u32[]{:S(2)}) copy-start(bf16[128,6,192]{2,1,0:T(8,128)(2,1)} %get-tuple-element.360) | copy-start | bytes 884740
  174.3 25.5 %all-to-all-start.3 = ((bf16[32,24,512]{2,1,0:T(8,128)(2,1)}), bf16[32,24,512]{2,1,0:T(8,128)(2,1)S(1)}, u32[]{:S(2)}, u32[]{:S(2)}) async-start(bf16[32,24,512]{2,1,0:T(8,128)(2,1)} %bitcast.109), calls=%async_computation.3 | async-start | bytes 1572864 | tf_op jit(solution)/shard_map/all_to_all | solution.py:1361
  286.4 9.4 %all-to-all-start.4 = ((f32[4,16,1024]{2,1,0:T(8,128)}), f32[4,16,1024]{2,1,0:T(8,128)S(1)}, u32[]{:S(2)}, u32[]{:S(2)}) async-start(f32[4,16,1024]{2,1,0:T(8,128)} %bitcast.139), calls=%async_computation.4 | async-start | bytes 524288 | tf_op jit(solution)/shard_map/all_to_all | solution.py:1488
  295.8 23.9 %all-to-all-start.6 = ((bf16[32,24,512]{2,1,0:T(8,128)(2,1)}), bf16[32,24,512]{2,1,0:T(8,128)(2,1)S(1)}, u32[]{:S(2)}, u32[]{:S(2)}) async-start(bf16[32,24,512]{2,1,0:T(8,128)(2,1)} %bitcast.137), calls=%async_computation.6 | async-start | bytes 1572864 | tf_op jit(solution)/shard_map/all_to_all | solution.py:1449
  320.7 87.5 %all-to-all-start.5 = ((bf16[128,24,128]{2,1,0:T(8,128)(2,1)}), bf16[128,24,128]{2,1,0:T(8,128)(2,1)S(1)}, u32[]{:S(2)}, u32[]{:S(2)}) async-start(bf16[128,24,128]{2,1,0:T(8,128)(2,1)} %bitcast.32), calls=%async_computation.5 | async-start | bytes 1572864 | tf_op jit(solution)/shard_map/all_to_all | solution.py:1511
  423.5 20.4 %copy-start.40 = (f32[2,6,192]{2,0,1:T(2,128)S(1)}, f32[2,6,192]{2,0,1:T(2,128)}, u32[]{:S(2)}) copy-start(f32[2,6,192]{2,0,1:T(2,128)} %param.55) | copy-start | bytes 27652
  423.5 20.4 %copy-start.55 = (f32[2,6,192]{2,0,1:T(2,128)S(1)}, f32[2,6,192]{2,0,1:T(2,128)}, u32[]{:S(2)}) copy-start(f32[2,6,192]{2,0,1:T(2,128)} %param.57) | copy-start | bytes 27652
  423.5 20.4 %copy-start.56 = (f32[2,6,192]{2,0,1:T(2,128)S(1)}, f32[2,6,192]{2,0,1:T(2,128)}, u32[]{:S(2)}) copy-start(f32[2,6,192]{2,0,1:T(2,128)} %param.56) | copy-start | bytes 27652
  423.5 20.4 %copy-start.58 = (f32[6,192]{1,0:T(8,128)S(1)}, f32[6,192]{1,0:T(8,128)}, u32[]{:S(2)}) copy-start(f32[6,192]{1,0:T(8,128)} %get-tuple-element.177) | copy-start | bytes 13828
  423.5 20.4 %copy-start.59 = (f32[6,192]{1,0:T(8,128)S(1)}, f32[6,192]{1,0:T(8,128)}, u32[]{:S(2)}) copy-start(f32[6,192]{1,0:T(8,128)} %get-tuple-element.178) | copy-start | bytes 13828
  423.6 22.2 %copy-start.4 = (f32[24,12576]{1,0:T(8,128)S(1)}, f32[24,12576]{1,0:T(8,128)}, u32[]{:S(2)}) copy-start(f32[24,12576]{1,0:T(8,128)} %param.37) | copy-start | bytes 3621892
  (49 other events, 263.0 us)

commit v2 on v1

--- a/solution.py
+++ b/solution.py
@@ -76,100 +76,6 @@
         return (lanes, False) if number % 2 == 0 else (False, lanes)
     half = lanes[1] // 256 * 128
     return (lanes[0], half), (lanes[0] + half, lanes[1] - half)
-
-
-def gather_kernel(pieces, count, *refs):
-    ins, outs = refs[:count], refs[count : 2 * count]
-    own_sem, core_sems, ring_send, ring_recv, pass_send, pass_recv = refs[2 * count :]
-    place = my_place()
-    sibling = moved(place, "c", 1)
-    greet(place)
-
-    def spot(number, origin, dims, lanes):
-        return block_view(outs[number], origin, dims, lanes, place["c"])
-
-    copies, crosses = [], []
-    for number in range(count):
-        here = block_view(outs[number], place, "", None, place["c"])
-        copy = pltpu.make_async_copy(ins[number], here, own_sem.at[number])
-        copy.start()
-        copies.append(copy)
-        cross = remote(ins[number], here, core_sems.at[0, number], core_sems.at[1, number], sibling)
-        cross.start()
-        crosses.append(cross)
-    rings, passes = {}, []
-
-    def send(phase, piece, way, src, dst, target):
-        copy = remote(
-            src, dst, ring_send.at[phase, way, piece], ring_recv.at[phase, way, piece], target
-        )
-        copy.start()
-        rings[(phase, way, piece)] = copy
-
-    def hand_over(phase, piece, way, where):
-        copy = remote(
-            where, where, pass_send.at[phase, way, piece], pass_recv.at[phase, way, piece], sibling
-        )
-        copy.start()
-        passes.append(copy)
-
-    def begin(phase, piece):
-        number, lanes, order = pieces[piece]
-        dim, dims = ORDERS[order][phase], ORDERS[order][:phase]
-        where = spot(number, place, dims, lanes)
-        src = ins[number].at[:, lanes_at(ins[number], lanes)] if phase == 0 else where
-        for way, step in ((0, 1), (1, -1)):
-            send(phase, piece, way, src, where, moved(place, dim, step))
-
-    for piece in range(len(pieces)):
-        begin(0, piece)
-    for copy in copies:
-        copy.wait()
-    for phase in range(3):
-        for piece, (number, lanes, order) in enumerate(pieces):
-            dim, dims = ORDERS[order][phase], ORDERS[order][:phase]
-            parts = halves(lanes, piece)
-            for way, step in ((0, 1), (1, -1)):
-                rings[(phase, way, piece)].wait_recv()
-                origin = moved(place, dim, -step)
-                if parts[way] is not False:
-                    onward = spot(number, origin, dims, parts[way])
-                    send(phase, piece, 2 + way, onward, onward, moved(place, dim, step))
-                hand_over(phase, piece, way, spot(number, origin, dims, lanes))
-        for piece, (number, lanes, order) in enumerate(pieces):
-            dim, dims = ORDERS[order][phase], ORDERS[order][:phase]
-            parts = halves(lanes, piece)
-            for way in range(2):
-                if parts[way] is not False:
-                    rings[(phase, 2 + way, piece)].wait_recv()
-            if phase < 2:
-                begin(phase + 1, piece)
-            hand_over(phase, piece, 2, spot(number, moved(place, dim, 2), dims, lanes))
-    for copy in rings.values():
-        copy.wait_send()
-    for copy in crosses + passes:
-        copy.wait()
-
-
-def gather_all(arrays, pieces, collective_id):
-    count, total = len(arrays), len(pieces)
-    outs = pl.pallas_call(
-        functools.partial(gather_kernel, pieces, count),
-        out_shape=[jax.ShapeDtypeStruct((2, 4, 4, 2, 2) + a.shape, a.dtype) for a in arrays],
-        in_specs=[pl.BlockSpec(memory_space=pl.ANY)] * count,
-        out_specs=[pl.BlockSpec(memory_space=pl.ANY)] * count,
-        scratch_shapes=[
-            pltpu.SemaphoreType.DMA((count,)),
-            pltpu.SemaphoreType.DMA((2, count)),
-            pltpu.SemaphoreType.DMA((3, 4, total)),
-            pltpu.SemaphoreType.DMA((3, 4, total)),
-            pltpu.SemaphoreType.DMA((3, 3, total)),
-            pltpu.SemaphoreType.DMA((3, 3, total)),
-        ],
-        cost_estimate=LONG,
-        compiler_params=pltpu.CompilerParams(collective_id=collective_id, has_side_effects=True),
-    )(*arrays)
-    return [o.reshape((128,) + a.shape) for o, a in zip(outs, arrays)]
 
 
 def open_shape(dims):
@@ -200,258 +106,6 @@
     return 1, lambda flat: ((high,) + inner + (low,), ())
 
 
-def reduce_kernel(sources, pieces, count, *refs):
-    total = len(pieces)
-    ins = refs[: len(sources)]
-    refs = refs[len(sources) :]
-    outs, square_ref, refs = refs[:count], refs[count], refs[count + 1 :]
-    accs, crosses, refs = refs[:count], refs[count : 2 * count], refs[2 * count :]
-    slots = refs[: 12 * total]
-    own_sem, core_sems, ring_send, ring_recv = refs[12 * total :]
-    place = my_place()
-    sibling = moved(place, "c", 1)
-    greet(place)
-
-    def slot(phase, way, piece):
-        return slots[(phase * 4 + way) * total + piece]
-
-    def add(number, lanes, at, dims, others):
-        acc = accs[number]
-
-        count, chunk = chunks_of(dims, at)
-
-        def body(flat, carry):
-            block, inner = chunk(flat)
-            where = block + (slice(None), lanes_at(acc, lanes))
-            parts = [
-                other[inner] if index is None else other[block + index] for other, index in others
-            ]
-            if len(parts) == 1:
-                acc[where] = acc[where] + parts[0]
-            else:
-                wide = [part.astype(jnp.float32) for part in [acc[where]] + parts]
-                acc[where] = sum(wide).astype(acc.dtype)
-            return carry
-
-        if count == 1:
-            body(0, 0)
-        else:
-            lax.fori_loop(0, count, body, 0)
-
-    started = []
-    first = {}
-    for piece, (number, lanes, order) in enumerate(pieces):
-        for index, (owner, high, mids) in enumerate(sources):
-            if owner != number:
-                continue
-            copies = []
-            for core, target in ((sibling["c"], "cross"), (place["c"], "own")):
-                where = (slice(None), slice(None), slice(None), slice(None), core)
-                src = ins[index].at[where + (slice(None), lanes_at(ins[index], lanes))]
-                at = (
-                    pl.ds(*high),
-                    pl.ds(*mids),
-                    slice(None),
-                    slice(None),
-                    slice(None),
-                    lanes_at(accs[number], lanes),
-                )
-                if target == "cross":
-                    copy = remote(
-                        src,
-                        crosses[number].at[at],
-                        core_sems.at[0, piece, index],
-                        core_sems.at[1, piece, index],
-                        sibling,
-                    )
-                else:
-                    copy = pltpu.make_async_copy(src, accs[number].at[at], own_sem.at[piece, index])
-                copy.start()
-                copies.append(copy)
-            started.append(copies[0])
-            first.setdefault(piece, []).append(copies)
-    rings = {}
-
-    def send(phase, way, piece, src, step):
-        number, lanes, order = pieces[piece]
-        copy = remote(
-            src,
-            slot(phase, way, piece),
-            ring_send.at[phase, way, piece],
-            ring_recv.at[phase, way, piece],
-            moved(place, ORDERS[order][phase], step),
-        )
-        copy.start()
-        rings[(phase, way, piece)] = copy
-        started.append(copy)
-
-    def begin(phase, piece):
-        number, lanes, order = pieces[piece]
-        dim, rest = ORDERS[order][phase], ORDERS[order][phase + 1 :]
-        parts = halves(lanes, piece)
-        for way, step in ((0, 1), (1, -1)):
-            if parts[way] is not False:
-                there = moved(place, dim, 2)
-                send(phase, way, piece, block_view(accs[number], there, rest, parts[way]), step)
-
-    for piece, (number, lanes, order) in enumerate(pieces):
-        for cross, own in first[piece]:
-            own.wait()
-            cross.wait_recv()
-        add(number, lanes, place, "xyz", [(crosses[number], (slice(None), lanes_at(accs[number], lanes)))])
-        begin(0, piece)
-    for phase in range(3):
-        for piece, (number, lanes, order) in enumerate(pieces):
-            dim, rest = ORDERS[order][phase], ORDERS[order][phase + 1 :]
-            parts = halves(lanes, piece)
-            for way, step in ((0, 1), (1, -1)):
-                there = moved(place, dim, step)
-                if parts[way] is not False:
-                    rings[(phase, way, piece)].wait_recv()
-                    add(number, parts[way], there, rest, [(slot(phase, way, piece), None)])
-                send(phase, 2 + way, piece, block_view(accs[number], there, rest, lanes), step)
-        for piece, (number, lanes, order) in enumerate(pieces):
-            rest = ORDERS[order][phase + 1 :]
-            for way in range(2):
-                rings[(phase, 2 + way, piece)].wait_recv()
-            others = [slot(phase, 2 + way, piece) for way in range(2)]
-            if phase < 2:
-                add(number, lanes, place, rest, [(other, None) for other in others])
-                begin(phase + 1, piece)
-            else:
-                block = (place["x"] // 2, place["y"], place["z"], place["x"] % 2)
-                where = (slice(None), lanes_at(accs[number], lanes))
-                value = accs[number][block + where].astype(jnp.float32)
-                for other in others:
-                    value = value + other[...].astype(jnp.float32)
-                outs[number][where] = value
-    total_square = jnp.zeros((1, 1), jnp.float32)
-    for number in range(count):
-        value = outs[number][...]
-        total_square = total_square + jnp.sum(
-            jnp.sum(value * value, 1, keepdims=True), 0, keepdims=True
-        )
-    square_ref[...] = jnp.broadcast_to(total_square, square_ref.shape)
-    for copy in started:
-        copy.wait_send()
-
-
-def reduce_all(arrays, sources, pieces, collective_id):
-    shapes = {}
-    views = []
-    for array, (owner, high, mids) in zip(arrays, sources):
-        shapes[owner] = array.shape[1:]
-        views.append(array.reshape((high[1], mids[1], 4, 2, 2) + array.shape[1:]))
-    count, total = len(shapes), len(pieces)
-    dtype = arrays[0].dtype
-    scratch = [pltpu.VMEM((2, 4, 4, 2) + shapes[n], dtype) for n in range(count)] * 2
-    for phase in range(3):
-        for way in range(4):
-            for piece, (number, lanes, order) in enumerate(pieces):
-                rest = ORDERS[order][phase + 1 :]
-                rows, width = shapes[number]
-                part = halves(lanes, piece)[way] if way < 2 else lanes
-                if part is False:
-                    scratch.append(pltpu.VMEM((8, 128), dtype))
-                else:
-                    wide = width if part is None else part[1]
-                    scratch.append(pltpu.VMEM(open_shape(rest) + (rows, wide), dtype))
-    scratch += [
-        pltpu.SemaphoreType.DMA((total, len(arrays))),
-        pltpu.SemaphoreType.DMA((2, total, len(arrays))),
-        pltpu.SemaphoreType.DMA((3, 4, total)),
-        pltpu.SemaphoreType.DMA((3, 4, total)),
-    ]
-    return pl.pallas_call(
-        functools.partial(reduce_kernel, sources, pieces, count),
-        out_shape=[
-            jax.ShapeDtypeStruct(shape, jnp.float32)
-            for shape in [shapes[n] for n in range(count)] + [(16, 128)]
-        ],
-        in_specs=[pl.BlockSpec(memory_space=pl.ANY)] * len(arrays),
-        out_specs=[pl.BlockSpec(memory_space=pltpu.VMEM)] * (count + 1),
-        scratch_shapes=scratch,
-        cost_estimate=LONG,
-        compiler_params=pltpu.CompilerParams(
-            collective_id=collective_id, has_side_effects=True, vmem_limit_bytes=56 * 1024 * 1024
-        ),
-    )(*views)
-
-
-def merge_parts(parts):
-    top = parts[0][0]
-    for part in parts[1:]:
-        top = jnp.maximum(top, part[0])
-    total = 0.0
-    target = 0.0
-    for part in parts:
-        total = total + part[1] * jnp.exp(part[0] - top)
-        target = target + part[2]
-    return top, total, target
-
-
-def stats_kernel(in_ref, out_ref, core_slots, ring_slots, core_sems, ring_send, ring_recv):
-    place = my_place()
-    greet(place, (1, 2, 3))
-
-    def parts_of(ref, index):
-        return tuple(ref[index, pl.ds(16 * row, 16), :] for row in range(3))
-
-    def put(ref, index, parts):
-        for row in range(3):
-            ref[index, pl.ds(16 * row, 16), :] = parts[row]
-
-    put(core_slots, place["c"], tuple(in_ref[pl.ds(16 * row, 16), :] for row in range(3)))
-    cross = pltpu.make_async_remote_copy(
-        src_ref=core_slots.at[place["c"]],
-        dst_ref=core_slots.at[place["c"]],
-        send_sem=core_sems.at[0],
-        recv_sem=core_sems.at[1],
-        device_id=device_of(moved(place, "c", 1)),
-        device_id_type=pl.DeviceIdType.MESH,
-    )
-    cross.start()
-    cross.wait()
-    merged = merge_parts([parts_of(core_slots, number) for number in range(2)])
-    for phase, dim in enumerate("xyz"):
-        slots = ring_slots.at[phase]
-        put(slots, place[dim], merged)
-        copies = []
-        for step in (1, 2, 3):
-            copy = pltpu.make_async_remote_copy(
-                src_ref=slots.at[place[dim]],
-                dst_ref=slots.at[place[dim]],
-                send_sem=ring_send.at[phase, step - 1],
-                recv_sem=ring_recv.at[phase, step - 1],
-                device_id=device_of(moved(place, dim, step)),
-                device_id_type=pl.DeviceIdType.MESH,
-            )
-            copy.start()
-            copies.append(copy)
-        for copy in copies:
-            copy.wait()
-        merged = merge_parts([parts_of(slots, number) for number in range(4)])
-    for row in range(3):
-        out_ref[pl.ds(16 * row, 16), :] = merged[row]
-
-
-def merge_stats(stats, collective_id):
-    return pl.pallas_call(
-        stats_kernel,
-        out_shape=jax.ShapeDtypeStruct((48, 128), jnp.float32),
-        in_specs=[pl.BlockSpec(memory_space=pltpu.VMEM)],
-        out_specs=pl.BlockSpec(memory_space=pltpu.VMEM),
-        scratch_shapes=[
-            pltpu.VMEM((2, 48, 128), jnp.float32),
-            pltpu.VMEM((3, 4, 48, 128), jnp.float32),
-            pltpu.SemaphoreType.DMA((2,)),
-            pltpu.SemaphoreType.DMA((3, 3)),
-            pltpu.SemaphoreType.DMA((3, 3)),
-        ],
-        compiler_params=pltpu.CompilerParams(collective_id=collective_id, has_side_effects=True),
-    )(stats)
-
-
 MOMENTUM = 0.9
 AVERAGE_KEEP = 0.9
 RATE = 1500.0
@@ -459,88 +113,6 @@
 LOW = jnp.bfloat16
 SPAN_LOW = 256
 TOKEN_BLOCK = 1024
-
-
-def pick_kernel(levels, rows, table_ref, high_ref, low_ref, out_ref):
-    low = low_ref[...]
-    high = high_ref[...]
-    count = low.shape[1]
-    hot = (lax.broadcasted_iota(jnp.int32, (SPAN_LOW, count), 0) == low).astype(LOW)
-    total = jnp.zeros((rows, count), jnp.float32)
-    group = 5
-    for first in range(0, levels, group):
-        found = jnp.dot(
-            table_ref[pl.ds(first * rows, group * rows), :], hot, preferred_element_type=jnp.float32
-        )
-        for level in range(group):
-            total = total + jnp.where(
-                high == first + level, found[level * rows : (level + 1) * rows], 0.0
-            )
-    value = total.astype(LOW)
-    for piece in range(count // 128):
-        out_ref[piece] = value[:, piece * 128 : (piece + 1) * 128]
-
-
-def pick_columns(table_levels, high, low, rows):
-    levels = table_levels.shape[0] // rows
-    tokens = high.shape[1]
-    return pl.pallas_call(
-        functools.partial(pick_kernel, levels, rows),
-        grid=(tokens // TOKEN_BLOCK,),
-        out_shape=jax.ShapeDtypeStruct((tokens // 128, rows, 128), LOW),
-        in_specs=[
-            pl.BlockSpec(table_levels.shape, lambda step: (0, 0)),
-            pl.BlockSpec((1, TOKEN_BLOCK), lambda step: (0, step)),
-            pl.BlockSpec((1, TOKEN_BLOCK), lambda step: (0, step)),
-        ],
-        out_specs=pl.BlockSpec((TOKEN_BLOCK // 128, rows, 128), lambda step: (step, 0, 0)),
-        compiler_params=pltpu.CompilerParams(vmem_limit_bytes=32 * 1024 * 1024),
-    )(table_levels, high, low)
-
-
-def spread_kernel(levels, rows, grad_ref, high_ref, low_ref, out_ref, spread_ref):
-    step = pl.program_id(0)
-
-    @pl.when(step == 0)
-    def _():
-        out_ref[...] = jnp.zeros_like(out_ref)
-
-    low = low_ref[...]
-    high = high_ref[...]
-    count = low.shape[1]
-    hot = (lax.broadcasted_iota(jnp.int32, (SPAN_LOW, count), 0) == low).astype(LOW)
-    grad = jnp.concatenate([grad_ref[piece] for piece in range(count // 128)], 1).astype(jnp.float32)
-    pair = 2
-    for first in range(0, levels, pair):
-        spread_ref[pl.ds(first * rows, pair * rows), :] = jnp.concatenate(
-            [jnp.where(high == first + level, grad, 0.0) for level in range(pair)], 0
-        ).astype(LOW)
-    group = 10 * rows
-    for first in range(0, levels * rows, group):
-        out_ref[pl.ds(first, group), :] += lax.dot_general(
-            spread_ref[pl.ds(first, group), :],
-            hot,
-            (((1,), (1,)), ((), ())),
-            preferred_element_type=jnp.float32,
-        )
-
-
-def spread_columns(grads, high, low, levels):
-    rows = grads.shape[1]
-    tokens = high.shape[1]
-    return pl.pallas_call(
-        functools.partial(spread_kernel, levels, rows),
-        grid=(tokens // TOKEN_BLOCK,),
-        out_shape=jax.ShapeDtypeStruct((levels * rows, SPAN_LOW), jnp.float32),
-        in_specs=[
-            pl.BlockSpec((TOKEN_BLOCK // 128, rows, 128), lambda step: (step, 0, 0)),
-            pl.BlockSpec((1, TOKEN_BLOCK), lambda step: (0, step)),
-            pl.BlockSpec((1, TOKEN_BLOCK), lambda step: (0, step)),
-        ],
-        out_specs=pl.BlockSpec((levels * rows, SPAN_LOW), lambda step: (0, 0)),
-        scratch_shapes=[pltpu.VMEM((levels * rows, TOKEN_BLOCK), LOW)],
-        compiler_params=pltpu.CompilerParams(vmem_limit_bytes=32 * 1024 * 1024),
-    )(grads, high, low)
 
 
 HEADS = 12
@@ -1212,11 +784,462 @@
     )(picked, table, labels, weights, counts)
 
 
+def device_at(number):
+    return number // 4, number % 4
+
+
+def start_kernel(
+    pieces, count, width, notes_ref, levels_ref, blocks_ref, *refs
+):
+    ins, refs = refs[:count], refs[count:]
+    notes_out, found_out, table_out = refs[:3]
+    outs, refs = refs[3 : 3 + count], refs[3 + count :]
+    notes_all, found, note_sems, found_sems, table_sems = refs[:5]
+    plane_send, plane_recv, ring_send, ring_recv, pass_send, pass_recv = refs[5:]
+    place = my_place()
+    sibling = moved(place, "c", 1)
+    me = lax.axis_index("dp") * 4 + lax.axis_index("vocab")
+    own_dp, own_vocab = device_at(me)
+    barrier = pltpu.get_barrier_semaphore()
+
+    def greet_one(step, carry):
+        pl.semaphore_signal(
+            barrier, inc=1, device_id=device_at((me + step) % 128), device_id_type=MESH
+        )
+        return carry
+
+    lax.fori_loop(1, 128, greet_one, 0)
+    pl.semaphore_wait(barrier, 127)
+
+    def to_device(src, dst, sems, device):
+        return pltpu.make_async_remote_copy(
+            src_ref=src, dst_ref=dst, send_sem=sems.at[0], recv_sem=sems.at[1],
+            device_id=device, device_id_type=MESH,
+        )
+
+    planes = []
+    for piece, (number, lanes, order) in enumerate(pieces):
+        here = block_view(outs[number], place, "", lanes, place["c"])
+        src = ins[number].at[:, lanes_at(ins[number], lanes)]
+        pltpu.make_async_copy(src, here, plane_recv.at[piece]).start()
+        for a, b in PLANE_STEPS:
+            copy = remote(
+                src, here, plane_send.at[piece, 4 * a + b - 1], plane_recv.at[piece],
+                plane_peer(place, PLANES[order], a, b),
+            )
+            copy.start()
+            planes.append(copy)
+    own_note = pltpu.make_async_copy(notes_ref, notes_all.at[me], note_sems.at[1])
+    own_note.start()
+
+    def send_note(step, carry):
+        to_device(notes_ref, notes_all.at[me], note_sems, device_at((me + step) % 128)).start()
+        return carry
+
+    lax.fori_loop(1, 128, send_note, 0)
+
+    pltpu.make_async_copy(
+        blocks_ref.at[own_dp], table_out.at[own_dp], table_sems.at[1]
+    ).start()
+
+    def send_block(step, carry):
+        other = (own_dp + step) % 32
+        to_device(
+            blocks_ref.at[other], table_out.at[own_dp], table_sems, (other, own_vocab)
+        ).start()
+        return carry
+
+    lax.fori_loop(1, 32, send_block, 0)
+
+    rows = found.shape[1]
+    levels = levels_ref.shape[0] // rows
+
+    def pick(step, carry):
+        block = (step + me // 8) % 16
+        ids = jnp.concatenate([notes_all[block * 8 + n, 0:1, :] for n in range(8)], 1)
+        local = ids - own_vocab * width
+        high = jnp.where((local >= 0) & (local < width), local >> 8, -1)
+        low = local & 255
+        hot = (lax.broadcasted_iota(jnp.int32, (SPAN_LOW, 1024), 0) == low).astype(LOW)
+        total = jnp.zeros((rows, 1024), jnp.float32)
+        group = 5
+        for first in range(0, levels, group):
+            values = jnp.dot(
+                levels_ref[pl.ds(first * rows, group * rows), :],
+                hot,
+                preferred_element_type=jnp.float32,
+            )
+            for level in range(group):
+                total = total + jnp.where(
+                    high == first + level, values[level * rows : (level + 1) * rows], 0.0
+                )
+        total = total.astype(LOW)
+        for n in range(8):
+            there = block * 8 + n
+            found[there] = total[:, 128 * n : 128 * n + 128]
+
+            @pl.when(there != me)
+            def _():
+                to_device(
+                    found.at[there], found_out.at[me], found_sems, device_at(there)
+                ).start()
+
+        return carry
+
+    rings, passes = {}, []
+
+    def spot(number, origin, dims, lanes):
+        return block_view(outs[number], origin, dims, lanes, place["c"])
+
+    def send(way, piece, src, target):
+        copy = remote(src, src, ring_send.at[way, piece], ring_recv.at[way, piece], target)
+        copy.start()
+        rings[(way, piece)] = copy
+
+    def hand_over(way, piece, where):
+        copy = remote(where, where, pass_send.at[way, piece], pass_recv.at[way, piece], sibling)
+        copy.start()
+        passes.append(copy)
+
+    for piece, (number, lanes, order) in enumerate(pieces):
+        sheet = spot(number, place, PLANES[order], lanes)
+        pltpu.make_async_copy(sheet, sheet, plane_recv.at[piece]).wait()
+        for way, step in ((0, 1), (1, -1)):
+            send(way, piece, sheet, moved(place, LINES[order], step))
+        hand_over(2, piece, sheet)
+    pltpu.make_async_copy(notes_all, notes_all, note_sems.at[1]).wait()
+    lax.fori_loop(0, 8, pick, 0)
+    for piece, (number, lanes, order) in enumerate(pieces):
+        dim, dims = LINES[order], PLANES[order]
+        parts = halves(lanes, piece)
+        for way, step in ((0, 1), (1, -1)):
+            rings[(way, piece)].wait_recv()
+            origin = moved(place, dim, -step)
+            if parts[way] is not False:
+                send(2 + way, piece, spot(number, origin, dims, parts[way]), moved(place, dim, step))
+            hand_over(way, piece, spot(number, origin, dims, lanes))
+    lax.fori_loop(8, 16, pick, 0)
+    own_found = pltpu.make_async_copy(found.at[me], found_out.at[me], found_sems.at[1])
+    own_found.start()
+    for piece, (number, lanes, order) in enumerate(pieces):
+        parts = halves(lanes, piece)
+        for way in range(2):
+            if parts[way] is not False:
+                rings[(2 + way, piece)].wait_recv()
+        far = moved(place, LINES[order], 2)
+        hand_over(3, piece, spot(number, far, PLANES[order], lanes))
+    notes_out[...] = notes_all[...]
+    pltpu.make_async_copy(found_out, found_out, found_sems.at[1]).wait()
+    pltpu.make_async_copy(table_out, table_out, table_sems.at[1]).wait()
+    for sems, ref, size in (
+        (note_sems, notes_all, 127), (found_sems, found, 127), (table_sems, blocks_ref, 31)
+    ):
+        sent = ref.at[pl.ds(0, size)]
+        pltpu.make_async_copy(sent, sent, sems.at[0]).wait()
+    for copy in planes + list(rings.values()):
+        copy.wait_send()
+    for copy in passes:
+        copy.wait()
+
+
+def start_step(notes, levels, blocks, arrays, pieces, width, collective_id):
+    count, total = len(arrays), len(pieces)
+    sems = pltpu.SemaphoreType.DMA
+    anywhere = pl.BlockSpec(memory_space=pl.ANY)
+    local = pl.BlockSpec(memory_space=pltpu.VMEM)
+    rows = blocks.shape[1]
+    notes_all, found, table, *outs = pl.pallas_call(
+        functools.partial(start_kernel, pieces, count, width),
+        out_shape=[
+            jax.ShapeDtypeStruct((128,) + notes.shape, jnp.int32),
+            jax.ShapeDtypeStruct((128, rows, 128), LOW),
+            jax.ShapeDtypeStruct(blocks.shape, LOW),
+        ]
+        + [jax.ShapeDtypeStruct((2, 4, 4, 2, 2) + a.shape, a.dtype) for a in arrays],
+        in_specs=[local, local, anywhere] + [anywhere] * count,
+        out_specs=[local, anywhere, anywhere] + [anywhere] * count,
+        scratch_shapes=[
+            pltpu.VMEM((128,) + notes.shape, jnp.int32),
+            pltpu.VMEM((128, rows, 128), LOW),
+            sems((2,)),
+            sems((2,)),
+            sems((2,)),
+            sems((total, 15)),
+            sems((total,)),
+            sems((4, total)),
+            sems((4, total)),
+            sems((4, total)),
+            sems((4, total)),
+        ],
+        cost_estimate=LONG,
+        compiler_params=pltpu.CompilerParams(
+            collective_id=collective_id, has_side_effects=True, vmem_limit_bytes=40 * 1024 * 1024
+        ),
+    )(notes, levels, blocks, *arrays)
+    return notes_all, found, table, [o.reshape((128,) + a.shape) for o, a in zip(outs, arrays)]
+
+
+def finish_kernel(sources, pieces, count, width, *refs):
+    total = len(pieces)
+    ins, refs = refs[: len(sources)], refs[len(sources) :]
+    text_ref, notes_ref, head_ref, refs = refs[0], refs[1], refs[2], refs[3:]
+    outs, table_ref, square_ref, refs = refs[:count], refs[count], refs[count + 1], refs[count + 2 :]
+    accs, crosses, refs = refs[:count], refs[count : 2 * count], refs[2 * count :]
+    slots, planes, refs = refs[: 4 * total], refs[4 * total : 5 * total], refs[5 * total :]
+    text_all, spread, near, far = refs[:4]
+    own_sem, core_sems, line_sems, plane_sems, text_sems, near_sems, far_sems = refs[4:]
+    place = my_place()
+    sibling = moved(place, "c", 1)
+    me = lax.axis_index("dp") * 4 + lax.axis_index("vocab")
+    own_dp, own_vocab = device_at(me)
+    barrier = pltpu.get_barrier_semaphore()
+
+    def greet_one(step, carry):
+        pl.semaphore_signal(
+            barrier, inc=1, device_id=device_at((me + step) % 128), device_id_type=MESH
+        )
+        return carry
+
+    lax.fori_loop(1, 128, greet_one, 0)
+    pl.semaphore_wait(barrier, 127)
+    started = []
+
+    def go(src, dst, sems, index, target):
+        copy = remote(src, dst, sems.at[(0,) + index], sems.at[(1,) + index], target)
+        copy.start()
+        started.append(copy)
+        return copy
+
+    def add(number, lanes, at, dims, others):
+        acc = accs[number]
+        count, chunk = chunks_of(dims, at)
+
+        def body(flat, carry):
+            block, inner = chunk(flat)
+            where = block + (slice(None), lanes_at(acc, lanes))
+            parts = [
+                other[inner] if index is None else other[block + index] for other, index in others
+            ]
+            if len(parts) == 1:
+                acc[where] = acc[where] + parts[0]
+            else:
+                wide = [part.astype(jnp.float32) for part in [acc[where]] + parts]
+                acc[where] = sum(wide).astype(acc.dtype)
+            return carry
+
+        if count == 1:
+            body(0, 0)
+        else:
+            lax.fori_loop(0, count, body, 0)
+
+    first, pair = {}, 0
+    for piece, (number, lanes, order) in enumerate(pieces):
+        for index, (owner, high, mids) in enumerate(sources):
+            if owner != number:
+                continue
+            every = slice(None)
+            run = lanes_at(accs[number], lanes)
+            at = (pl.ds(*high), pl.ds(*mids), every, every, every, run)
+            src = (every, every, every, every)
+            cross = go(
+                ins[index].at[src + (sibling["c"], every, run)], crosses[number].at[at],
+                core_sems, (pair,), sibling,
+            )
+            own = pltpu.make_async_copy(
+                ins[index].at[src + (place["c"], every, run)], accs[number].at[at], own_sem.at[pair]
+            )
+            own.start()
+            first.setdefault(piece, []).append((cross, own))
+            pair += 1
+
+    def text_copy(block, device):
+        return pltpu.make_async_remote_copy(
+            src_ref=text_ref.at[block], dst_ref=text_all.at[me], send_sem=text_sems.at[0],
+            recv_sem=text_sems.at[1], device_id=device, device_id_type=MESH,
+        )
+
+    pltpu.make_async_copy(text_ref.at[own_dp], text_all.at[me], text_sems.at[1]).start()
+
+    def send_text(step, carry):
+        there = (me + step) % 128
+        text_copy(there // 4, device_at(there)).start()
+        return carry
+
+    rings = {}
+
+    def send_opposite(piece):
+        number, lanes, order = pieces[piece]
+        parts = halves(lanes, piece)
+        there = moved(place, LINES[order], 2)
+        for way, step in ((0, 1), (1, -1)):
+            if parts[way] is not False:
+                rings[(way, piece)] = go(
+                    block_view(accs[number], there, PLANES[order], parts[way]),
+                    slots[way * total + piece], line_sems, (way, piece),
+                    moved(place, LINES[order], step),
+                )
+
+    for piece, (number, lanes, order) in enumerate(pieces):
+        for cross, own in first[piece]:
+            own.wait()
+            cross.wait_recv()
+        run = (slice(None), lanes_at(accs[number], lanes))
+        add(number, lanes, place, "xyz", [(crosses[number], run)])
+        send_opposite(piece)
+        if piece == 2:
+            lax.fori_loop(1, 128, send_text, 0)
+
+    rows = text_all.shape[1]
+    levels = head_ref.shape[0] // rows
+    table_ref[...] = head_ref[...]
+
+    def scatter(block, carry):
+        ids = jnp.concatenate([notes_ref[block * 8 + n, 0:1, :] for n in range(8)], 1)
+        local = ids - own_vocab * width
+        high = jnp.where((local >= 0) & (local < width), local >> 8, -1)
+        hot = (lax.broadcasted_iota(jnp.int32, (SPAN_LOW, 1024), 0) == (local & 255)).astype(LOW)
+        grad = jnp.concatenate([text_all[block * 8 + n] for n in range(8)], 1).astype(jnp.float32)
+        for level in range(0, levels, 2):
+            spread[pl.ds(level * rows, 2 * rows), :] = jnp.concatenate(
+                [jnp.where(high == level + n, grad, 0.0) for n in range(2)], 0
+            ).astype(LOW)
+        group = 10 * rows
+        for start in range(0, levels * rows, group):
+            table_ref[pl.ds(start, group), :] += cols_product(spread[pl.ds(start, group), :], hot)
+        return carry
+
+    for piece, (number, lanes, order) in enumerate(pieces):
+        parts = halves(lanes, piece)
+        for way, step in ((0, 1), (1, -1)):
+            there = moved(place, LINES[order], step)
+            if parts[way] is not False:
+                rings[(way, piece)].wait_recv()
+                add(number, parts[way], there, PLANES[order], [(slots[way * total + piece], None)])
+            rings[(2 + way, piece)] = go(
+                block_view(accs[number], there, PLANES[order], lanes),
+                slots[(2 + way) * total + piece], line_sems, (2 + way, piece), there,
+            )
+    whole = pltpu.make_async_copy(text_all, text_all, text_sems.at[1])
+    whole.wait()
+    lax.fori_loop(0, 10, scatter, 0)
+    for piece, (number, lanes, order) in enumerate(pieces):
+        for way in range(2):
+            rings[(2 + way, piece)].wait_recv()
+        add(
+            number, lanes, place, PLANES[order],
+            [(slots[(2 + way) * total + piece], None) for way in range(2)],
+        )
+        for a, b in PLANE_STEPS:
+            there = plane_peer(place, PLANES[order], a, b)
+            remote(
+                block_view(accs[number], there, "", lanes), planes[piece].at[4 * a + b - 1],
+                plane_sems.at[0, piece], plane_sems.at[1, piece], there,
+            ).start()
+    lax.fori_loop(10, 16, scatter, 0)
+    home = (place["x"] // 2, place["y"], place["z"], place["x"] % 2)
+    square = jnp.zeros((1, 1), jnp.float32)
+
+    def squared(value):
+        return jnp.sum(jnp.sum(value * value, 1, keepdims=True), 0, keepdims=True)
+
+    for piece, (number, lanes, order) in enumerate(pieces):
+        pltpu.make_async_copy(planes[piece], planes[piece], plane_sems.at[1, piece]).wait()
+        where = (slice(None), lanes_at(accs[number], lanes))
+        value = accs[number][home + where].astype(jnp.float32)
+        for n in range(15):
+            value = value + planes[piece][n].astype(jnp.float32)
+        outs[number][where] = value
+        square = square + squared(value)
+    square = square + squared(table_ref[...])
+
+    mine = place["x"] * 2 + place["c"]
+    near[mine] = jnp.broadcast_to(square, (8, 128))
+    meets = []
+    for n in range(1, 8):
+        peer = moved(place, "x", n // 2)
+        if n % 2:
+            peer = moved(peer, "c", 1)
+        meets.append(go(near.at[mine], near.at[mine], near_sems, (n - 1,), peer))
+    for copy in meets:
+        copy.wait_recv()
+    spot = place["y"] * 4 + place["z"]
+    far[spot] = sum(near[n] for n in range(8))
+    meets = []
+    for a, b in PLANE_STEPS:
+        peer = plane_peer(place, ("y", "z"), a, b)
+        meets.append(go(far.at[spot], far.at[spot], far_sems, (4 * a + b - 1,), peer))
+    for copy in meets:
+        copy.wait_recv()
+    square_ref[...] = sum(far[n] for n in range(16))
+    for piece in range(total):
+        pltpu.make_async_copy(planes[piece], planes[piece], plane_sems.at[0, piece]).wait()
+    sent = text_all.at[pl.ds(0, 127)]
+    pltpu.make_async_copy(sent, sent, text_sems.at[0]).wait()
+    for copy in started:
+        copy.wait_send()
+
+
+def finish_step(arrays, text, notes, head_levels, sources, pieces, width, collective_id):
+    shapes, views = {}, []
+    for array, (owner, high, mids) in zip(arrays, sources):
+        shapes[owner] = array.shape[1:]
+        views.append(array.reshape((high[1], mids[1], 4, 2, 2) + array.shape[1:]))
+    count, total = len(shapes), len(pieces)
+    pairs = sum(owner == piece[0] for piece in pieces for owner, high, mids in sources)
+    scratch = [pltpu.VMEM((2, 4, 4, 2) + shapes[n], LOW) for n in range(count)] * 2
+    widths = []
+    for piece, (number, lanes, order) in enumerate(pieces):
+        parts = halves(lanes, piece)
+        widths.append([shapes[number][1] if part is None else part for part in
+                       [p if p in (None, False) else p[1] for p in (*parts, lanes, lanes)]])
+    for way in range(4):
+        for piece, (number, lanes, order) in enumerate(pieces):
+            wide = widths[piece][way]
+            if wide is False:
+                scratch.append(pltpu.VMEM((8, 128), LOW))
+            else:
+                rest = open_shape("".join(PLANES[order]))
+                scratch.append(pltpu.VMEM(rest + (shapes[number][0], wide), LOW))
+    for piece, (number, lanes, order) in enumerate(pieces):
+        scratch.append(pltpu.VMEM((15, shapes[number][0], widths[piece][2]), LOW))
+    rows = text.shape[1]
+    sems = pltpu.SemaphoreType.DMA
+    scratch += [
+        pltpu.VMEM((128, rows, 128), LOW),
+        pltpu.VMEM((head_levels.shape[0], 1024), LOW),
+        pltpu.VMEM((8, 8, 128), jnp.float32),
+        pltpu.VMEM((16, 8, 128), jnp.float32),
+        sems((pairs,)),
+        sems((2, pairs)),
+        sems((2, 4, total)),
+        sems((2, total)),
+        sems((2,)),
+        sems((2, 7)),
+        sems((2, 15)),
+    ]
+    local = pl.BlockSpec(memory_space=pltpu.VMEM)
+    return pl.pallas_call(
+        functools.partial(finish_kernel, sources, pieces, count, width),
+        out_shape=[jax.ShapeDtypeStruct(shapes[n], jnp.float32) for n in range(count)]
+        + [
+            jax.ShapeDtypeStruct(head_levels.shape, jnp.float32),
+            jax.ShapeDtypeStruct((8, 128), jnp.float32),
+        ],
+        in_specs=[pl.BlockSpec(memory_space=pl.ANY)] * len(arrays) + [local] * 3,
+        out_specs=[local] * (count + 2),
+        scratch_shapes=scratch,
+        cost_estimate=LONG,
+        compiler_params=pltpu.CompilerParams(
+            collective_id=collective_id, has_side_effects=True, vmem_limit_bytes=60 * 1024 * 1024
+        ),
+    )(*views, text, notes, head_levels)
+
+
 def thirds(number):
     return [(number, (256 * k, 256), k) for k in range(3)]
 
 
-GATHER_PIECES = thirds(0) + thirds(1) + [(2, None, 0), (3, None, 2), (4, None, 1), (5, None, 2)]
+GATHER_PIECES = thirds(0) + thirds(1) + [(2, (0, 512), 0), (2, (512, 448), 2), (3, None, 1)]
 REDUCE_PIECES = (
     thirds(0)
     + thirds(1)
@@ -1231,37 +1254,50 @@
 ] + [(number,) + WHOLE for number in range(1, 9)]
 
 
-def fetch(masters):
+def pack(masters):
     word, position, box, text, down, layout, layout_down, head, vector = [
         m.astype(LOW) for m in masters
     ]
-    misc = jnp.concatenate(
+    box = box.reshape(2, 16, 128)
+    small = jnp.concatenate(
         [
-            layout.T,
-            layout_down[0],
-            layout_down[1],
-            jnp.pad(vector, (0, 192 - vector.shape[0]))[None],
+            jnp.concatenate([box[0], box[1]], 1),
+            jnp.pad(
+                jnp.concatenate(
+                    [
+                        layout.T,
+                        layout_down[0],
+                        layout_down[1],
+                        jnp.pad(vector, (0, 192 - vector.shape[0]))[None],
+                    ],
+                    0,
+                ),
+                ((0, 7), (0, 64)),
+            ),
         ],
         0,
     )
-    text, down, head, position, misc, box = gather_all(
-        [text.T, down, head.T, position, misc, box.reshape(32, 128)], GATHER_PIECES, 2
-    )
+    return [text.T, down, jnp.concatenate([head.T, position], 0), small]
+
+
+def unpack(gathered):
+    text, down, wide, small = gathered
+    box = small[:, :16].reshape(128, 2, 8, 2, 128).transpose(3, 1, 0, 2, 4)
     return dict(
         text=text,
         down=down.reshape(3072, 768),
-        head=head.reshape(768, 960),
-        box=box.reshape(128, 4, 8, 128).transpose(1, 0, 2, 3).reshape(4096, 128),
-        layout=misc[:, :12].reshape(1536, 192),
-        layout_down=misc[:, 12:18].reshape(768, 192),
-        box_proj=misc[:, 18:24].reshape(768, 192),
-        position=position.reshape(640, 960),
-        vector=misc[:, 24, :123].reshape(15744),
-    )
-
-
-def reduce_weights(grads):
-    shards = reduce_all(
+        head=wide[:, :6].reshape(768, 960),
+        box=box.reshape(4096, 128),
+        layout=small[:, 16:28, :192].reshape(1536, 192),
+        layout_down=small[:, 28:34, :192].reshape(768, 192),
+        box_proj=small[:, 34:40, :192].reshape(768, 192),
+        position=wide[:, 6:].reshape(640, 960),
+        vector=small[:, 40, :123].reshape(15744),
+    )
+
+
+def reduce_weights(grads, text, notes, head_levels, width):
+    shards = finish_step(
         [
             grads["query"].reshape(16, 48, 768),
             grads["key_value"].reshape(32, 48, 768),
@@ -1276,12 +1312,16 @@
             grads["box"].reshape(4, 128, 8, 128).transpose(1, 0, 2, 3).reshape(128, 32, 128),
             grads["vector"].reshape(128, 1, 123),
         ],
+        text,
+        notes,
+        head_levels,
         REDUCE_SOURCES,
         REDUCE_PIECES,
-        6,
-    )
-    text, down, head, position, layout, layout_down, box_proj, box, vector, square = shards
-    return square, [
+        width,
+        4,
+    )
+    text, down, head, position, layout, layout_down, box_proj, box, vector, table, square = shards
+    return table, square, [
         position,
         box.reshape(4, 8, 128),
         text.T,
@@ -1331,17 +1371,6 @@
         ],
         0,
     )
-    notes_all = lax.all_to_all(
-        jnp.broadcast_to(notes[None], (128,) + notes.shape), AXES, 0, 0, tiled=True
-    )
-    ids_all = notes_all[:, 0, :].reshape(1, 16384)
-    labels_all = notes_all[:, 1, :16].reshape(2048)
-    counted_all = notes_all[:, 1, 16:32].reshape(2048).astype(jnp.float32)
-    total_count = jnp.sum(counted_all)
-
-    local_ids = ids_all - vocab * shard_width
-    ids_high = local_ids >> 8
-    ids_low = local_ids & 255
     table_low = word_table.astype(LOW)
     table_levels = (
         jnp.pad(table_low, ((0, 0), (0, levels * SPAN_LOW - shard_width)))
@@ -1349,18 +1378,20 @@
         .transpose(1, 0, 2)
         .reshape(levels * table_rows, SPAN_LOW)
     )
-    found = pick_columns(table_levels, ids_high, ids_low, table_rows)
-    found, masters = lax.optimization_barrier((found, masters))
-    found = lax.all_to_all(found, AXES, 0, 0, tiled=True)
-
     table_blocks = (
         jnp.pad(table_low, ((0, 0), (0, 32 * HEAD_BLOCK - shard_width)))
         .reshape(table_rows, 32, HEAD_BLOCK)
         .transpose(1, 0, 2)
     )
-    table_head = lax.all_to_all(table_blocks, "dp", 0, 0, tiled=True).reshape(768, HEAD_BLOCK)
-
-    full = fetch(masters)
+    notes_all, found, table_head, gathered = start_step(
+        notes, table_levels, table_blocks, pack(masters), GATHER_PIECES, shard_width, 1
+    )
+    table_head = table_head.reshape(768, HEAD_BLOCK)
+    full = unpack(gathered)
+    labels_all = notes_all[:, 1, :16].reshape(2048)
+    counted_all = notes_all[:, 1, 16:32].reshape(2048).astype(jnp.float32)
+    total_count = jnp.sum(counted_all)
+
     vector = full["vector"].astype(jnp.float32)
     text_vec = vector[:10752].reshape(14, 768)
     layout_vec = vector[10752:13440].reshape(14, 192)
@@ -1505,24 +1536,18 @@
         ],
         "open_streams_back",
     )
-    d_text_blocks = jnp.broadcast_to(
-        d_embedded.reshape(32, 1, 24, 128), (32, 4, 24, 128)
-    ).reshape(128, 24, 128)
-    d_text_all = lax.all_to_all(d_text_blocks, AXES, 0, 0, tiled=True)
-    table_grad = (
-        spread_columns(d_text_all, ids_high, ids_low, levels)
-        .reshape(levels, table_rows, SPAN_LOW)
+    head_levels = (
+        table_head_grad.transpose(1, 0, 2)
+        .reshape(table_rows, 32 * HEAD_BLOCK)[:, : levels * SPAN_LOW]
+        .reshape(table_rows, levels, SPAN_LOW)
         .transpose(1, 0, 2)
-        .reshape(table_rows, levels * SPAN_LOW)[:, :shard_width]
-    )
-    table_grad = table_grad + table_head_grad.transpose(1, 0, 2).reshape(
-        table_rows, 32 * HEAD_BLOCK
-    )[:, :shard_width].astype(jnp.float32)
-
+        .reshape(levels * table_rows, SPAN_LOW)
+        .astype(f32)
+    )
     d_positions = lax.dynamic_update_slice_in_dim(
         jnp.zeros((640, 960), LOW), d_position.astype(LOW), vocab * 64, 0
     )
-    square, shards = reduce_weights(
+    table_grad, square, shards = reduce_weights(
         dict(
             query=d_query_w,
             key_value=d_kv_w,
@@ -1542,18 +1567,19 @@
                     d_head_vec.reshape(2304),
                 ]
             ).astype(LOW),
-        )
+        ),
+        d_embedded.reshape(32, 24, 128),
+        notes_all,
+        head_levels,
+        shard_width,
+    )
+    table_grad = (
+        table_grad.reshape(levels, table_rows, SPAN_LOW)
+        .transpose(1, 0, 2)
+        .reshape(table_rows, levels * SPAN_LOW)[:, :shard_width]
     )
     all_grads = [table_grad] + shards
-    norm_stats = jnp.concatenate(
-        [
-            jnp.zeros((16, 128), f32),
-            square + jnp.sum(table_grad * table_grad),
-            jnp.zeros((16, 128), f32),
-        ],
-        0,
-    )
-    grad_norm = jnp.sqrt(merge_stats(norm_stats, 7)[16, 0])
+    grad_norm = jnp.sqrt(square[0, 0])
     factor = jnp.minimum(1.0, CLIP / grad_norm)
     results = []
     for (master, momentum, average), grad in zip(triples, all_grads):

time: 459 us -> 402 us (0.88)
  starting transfers between devices: 48 us -> 13.3 us
  other arithmetic: 27.4 us -> 17.5 us
  waiting for transfers between devices: 11.3 us -> 1.43 us
    all_to_all x4 -> x0, starting transfers between devices: 34.8 us -> none  [the longest x1 11.1 us: on_device(): lax.all_to_all(jnp.broadcast_to(notes[None], (128,) + notes.shape), AXES,...]
    another operation x9 -> x5, local copies, waits for them, and re-layouts: 13.2 us -> 6.47 us  [finish_step(): views.append(array.reshape((high[1], mids[1], 4, 2, 2) + array.shape[1:]))]
    reshape x4 -> x8, local copies, waits for them, and re-layouts: 3.33 us -> 9.15 us  [the longest x2 2.24 us: unpack(): box = small[:, :16].reshape(128, 2, 8, 2, 128).transpose(3, 1, 0, 2, 4)]
    all_to_all x1, waiting for transfers between devices: 5.7 us -> 0.01 us  [on_device(): lax.all_to_all(partial.reshape(4, 16, 1280), 'vocab', 0, 0, tiled=True)]
    pallas_call x5 -> x2, Pallas kernels: 191 us -> 191 us  [the longest x1 99.7 us: finish_step(): pl.pallas_call(functools.partial(finish_kernel, sources, pieces, count, w...]
  transfers between devices with their start and end apart: 7 -> 3, of which waited for: 3 -> 1; matrix products, arithmetic and copies ran while one was open for 10% -> 5% of each run, Pallas kernels for 36% -> 2%
where the time goes in v2:
time: 402 us; the launch traced here: 399 us
  Pallas kernels  296 us (74%)
  local copies, waits for them, and re-layouts  41.6 us (10%)
  blocking collectives  25.4 us (6%)
  other arithmetic  17.5 us (4%)
  starting transfers between devices  13.3 us (3%)
    pallas_call x1, Pallas kernels, finish_step(): pl.pallas_call(functools.partial(finish_kernel, sources, pieces, count, w...  99.7 us
    pallas_call x1, Pallas kernels, start_step(): pl.pallas_call(functools.partial(start_kernel, pieces, count, width), out...  91.3 us
    pallas_call x1, Pallas kernels, head_step(): pl.pallas_call(kernel, out_shape=[jax.ShapeDtypeStruct((16, 768), jnp.flo...  58.3 us
    pallas_call x6, Pallas kernels, local_call(): pl.pallas_call(kernel, name=name, grid=(1,), out_shape=[jax.ShapeDtypeStr...  46.3 us
    all_gather x1, blocking collectives, on_device(): query_all = lax.all_gather(query, 'vocab', axis=0, tiled=True)  18.7 us
  transfers between devices with their start and end apart: 3, of which 1 were waited for; matrix products, arithmetic and copies ran while one was open for 5% of the time, Pallas kernels for 2%

profile of v2, /device:TPU:0, one launch (start us, length us, event | category | flops | bytes accessed | tf_op | source)
XLA Modules:
  0.0 398.6 jit_solution(17507697155805252127)
XLA Ops:
  4.9 91.3 %shard_map.535 = (s32[128,2,128]{2,1,0:T(2,128)S(1)}, bf16[128,24,128]{2,1,0:T(8,128)(2,1)S(1)}, bf16[32,24,512]{2,1,0:T(8,128)(2,1)S(1)}, bf16[2,4,4,2,2,48,768...) custom-call(s32[2,128]{1,0:T(2,128)S(1)} %add_add_fusion.notes_ref, ...), custom_call_target="tpu_custom_call" | custom-call | flops 60000002048 | bytes 200000000 | tf_op jit(solution)/shard_map/pallas_call | solution.py:951
  98.4 1.7 fusion.30
  102.6 3.1 slice.125
  105.7 1.8 reshape.285
  112.6 1.6 dynamic-slice_convert_fusion.position_ref
  114.9 5.8 %open_streams.1 = (f32[128,768]{1,0:T(8,128)}, f32[128,192]{1,0:T(8,128)}, bf16[128,768]{1,0:T(8,128)(2,1)}, bf16[128,768]{1,0:T(8,128)(2,1)}, bf16[128,768]{1,0...) custom-call(bf16[128,24,128]{2,1,0:T(8,128)(2,1)} %copy-done.2, ...), custom_call_target="tpu_custom_call" | custom-call | tf_op jit(solution)/shard_map/open_streams/pallas_call | solution.py:508
  120.6 18.7 %all_gather.6.query_ref = bf16[64,1024]{1,0:T(8,128)(2,1)} all-gather(bf16[16,1024]{1,0:T(8,128)(2,1)} %get-tuple-element.103), channel_id=1, replica_groups=mesh['dp'=32,'vocab'=4] {'vocab'}, dimensions={0}, use_global_device_ids=true | all-gather | bytes 163840 | tf_op jit(solution)/shard_map/all_gather | solution.py:1445
  139.3 3.2 partial_attention.1
  142.5 3.5 all-to-all-start
  146.0 1.8 slice.135
  149.4 1.8 reshape.295.head_ref
  155.2 10.4 %close_streams.1 = (f32[16,768]{1,0:T(8,128)}, f32[16,192]{1,0:T(8,128)}, f32[16,128]{1,0:T(8,128)}, f32[16,768]{1,0:T(8,128)}, f32[16,192]{1,0:T(8,128)}, /*ind...) custom-call(f32[4,16,1280]{2,1,0:T(8,128)} %copy-done.9, ...), custom_call_target="tpu_custom_call" | custom-call | tf_op jit(solution)/shard_map/close_streams/pallas_call | solution.py:508
  165.6 58.3 %shard_map.536 = (f32[16,768]{1,0:T(8,128)}, bf16[768,512]{1,0:T(8,128)(2,1)}, f32[8,128]{1,0:T(8,128)}) custom-call(bf16[16,768]{1,0:T(8,128)(2,1)} %get-tuple-element.111.refs_0_, bf16[768,512]{1,0:T(8,128)(2,1)} %bitcast.118, s32[1,2048]{1,0:T(1,128)} %sub.83.refs_2_, f32[1,2048]{1,0:T(1,128)} %broadcast_divide_fusion.refs_3_, f32[1,2048]{1,0:T(1,128)} %copy-done.29), custom_call_target="tpu_custom_call" | custom-call | tf_op jit(solution)/shard_map/pallas_call | solution.py:740
  223.9 15.5 %close_streams_back.1 = (f32[16,1280]{1,0:T(8,128)}, f32[16,768]{1,0:T(8,128)}, f32[16,192]{1,0:T(8,128)}, bf16[768,960]{1,0:T(8,128)(2,1)}, bf16[768,768]{1,0:T...) custom-call(f32[16,768]{1,0:T(8,128)} %get-tuple-element.114.grad_re, ...), custom_call_target="tpu_custom_call" | custom-call | tf_op jit(solution)/shard_map/close_streams_back/pallas_call | solution.py:508
  239.5 6.8 %all_gather.7.back_ref = f32[64,1280]{1,0:T(8,128)} all-gather(f32[16,1280]{1,0:T(8,128)} %get-tuple-element.126), channel_id=1, replica_groups=mesh['dp'=32,'vocab'=4] {'vocab'}, dimensions={0}, use_global_device_ids=true | all-gather | bytes 409600 | tf_op jit(solution)/shard_map/all_gather | solution.py:1506
  246.2 4.0 %attention_back.1 = (f32[64,1024]{1,0:T(8,128)}, bf16[128,768]{1,0:T(8,128)(2,1)}, bf16[128,768]{1,0:T(8,128)(2,1)}, bf16[128,192]{1,0:T(8,128)(2,1)}, bf16[128,192]{1,0:T(8,128)(2,1)}) custom-call(f32[64,1280]{1,0:T(8,128)} %all_gather.7.back_ref, bf16[64,1024]{1,0:T(8,128)(2,1)} %all_gather.6.query_ref, bf16[128,768]{1,0:T(8,128)(2,1)} %get-tuple-element.104.key_text, ...), custom_call_target="tpu_custom_call" | custom-call | tf_op jit(solution)/shard_map/attention_back/pallas_call | solution.py:508
  250.3 3.4 all-to-all-start.1
  254.5 1.7 reshape_reshape.43.refs_5_
  259.7 6.5 %all-to-all-start.2 = ((bf16[32,24,512]{2,1,0:T(8,128)(2,1)}), bf16[32,24,512]{2,1,0:T(8,128)(2,1)S(1)}, u32[]{:S(2)}, u32[]{:S(2)}) async-start(bf16[32,24,512]{2,1,0:T(8,128)(2,1)} %bitcast.32), calls=%async_computation.2 | async-start | bytes 1572864 | tf_op jit(solution)/shard_map/all_to_all | solution.py:1480
  266.2 7.4 %open_streams_back.1 = (bf16[768,768]{1,0:T(8,128)(2,1)}, bf16[1536,768]{1,0:T(8,128)(2,1)}, bf16[576,192]{1,0:T(8,128)(2,1)}, bf16[768,128]{1,0:T(8,128)(2,1)},...) custom-call(f32[4,16,1024]{2,1,0:T(8,128)} %copy-done.12, ...), custom_call_target="tpu_custom_call" | custom-call | tf_op jit(solution)/shard_map/open_streams_back/pallas_call | solution.py:508
  278.7 1.6 reshape_reshape.44.refs_6_
  284.4 99.7 %shard_map.537 = (f32[48,768]{1,0:T(8,128)}, f32[24,768]{1,0:T(8,128)}, f32[6,960]{1,0:T(8,128)}, f32[5,960]{1,0:T(8,128)}, f32[12,192]{1,0:T(8,128)}, /*index=5...) custom-call(bf16[1,1,4,2,2,48,768]{6,5,4,3,2,1,0:T(8,128)(2,1)} %bit, ...), custom_call_target="tpu_custom_call" | custom-call | flops 60000002048 | bytes 200000000 | tf_op jit(solution)/shard_map/pallas_call | solution.py:1221
  388.7 1.5 copy.176
  395.1 2.2 multiply_add_fusion
  (229 shorter events, 41.7 us)
Async XLA Ops:
  97.9 54.3 %copy-start.3 = (s32[128,2,128]{2,1,0:T(2,128)}, s32[128,2,128]{2,1,0:T(2,128)S(1)}, u32[]{:S(2)}) copy-start(s32[128,2,128]{2,1,0:T(2,128)S(1)} %get-tuple-element.113.refs_13_) | copy-start | bytes 393220
  142.5 11.9 %all-to-all-start = ((f32[4,16,1280]{2,1,0:T(8,128)}), f32[4,16,1280]{2,1,0:T(8,128)S(1)}, u32[]{:S(2)}, u32[]{:S(2)}) async-start(f32[4,16,1280]{2,1,0:T(8,128)} %bitcast.136), calls=%async_computation | async-start | bytes 655360 | tf_op jit(solution)/shard_map/all_to_all | solution.py:1447
  152.2 13.3 %copy-start.29 = (f32[1,2048]{1,0:T(1,128)}, f32[1,2048]{1,0:T(1,128)S(1)}, u32[]{:S(2)}) copy-start(f32[1,2048]{1,0:T(1,128)S(1)} %convert_element_type.111.refs_4_) | copy-start | bytes 24580
  239.4 14.3 %copy-start.33 = (f32[16,128]{1,0:T(8,128)S(1)}, f32[16,128]{1,0:T(8,128)}, u32[]{:S(2)}) copy-start(f32[16,128]{1,0:T(8,128)} %fusion.22.slot_ref) | copy-start | bytes 24580
  239.4 15.0 %copy-start.56 = (f32[3,768]{1,0:T(4,128)S(1)}, f32[3,768]{1,0:T(4,128)}, u32[]{:S(2)}) copy-start(f32[3,768]{1,0:T(4,128)} %get-tuple-element.153) | copy-start | bytes 27652
  239.5 15.0 %copy-start.8 = (bf16[768,960]{1,0:T(8,128)(2,1)S(1)}, bf16[768,960]{1,0:T(8,128)(2,1)}, u32[]{:S(2)}) copy-start(bf16[768,960]{1,0:T(8,128)(2,1)} %get-tuple-element.142) | copy-start | bytes 4423684
  250.3 9.4 %all-to-all-start.1 = ((f32[4,16,1024]{2,1,0:T(8,128)}), f32[4,16,1024]{2,1,0:T(8,128)S(1)}, u32[]{:S(2)}, u32[]{:S(2)}) async-start(f32[4,16,1024]{2,1,0:T(8,128)} %bitcast.142), calls=%async_computation.1 | async-start | bytes 524288 | tf_op jit(solution)/shard_map/all_to_all | solution.py:1519
  259.7 22.8 %all-to-all-start.2 = ((bf16[32,24,512]{2,1,0:T(8,128)(2,1)}), bf16[32,24,512]{2,1,0:T(8,128)(2,1)S(1)}, u32[]{:S(2)}, u32[]{:S(2)}) async-start(bf16[32,24,512]{2,1,0:T(8,128)(2,1)} %bitcast.32), calls=%async_computation.2 | async-start | bytes 1572864 | tf_op jit(solution)/shard_map/all_to_all | solution.py:1480
  284.3 101.8 %copy-start.39 = (f32[2,6,192]{2,0,1:T(2,128)S(1)}, f32[2,6,192]{2,0,1:T(2,128)}, u32[]{:S(2)}) copy-start(f32[2,6,192]{2,0,1:T(2,128)} %param.55) | copy-start | bytes 27652
  284.3 101.8 %copy-start.54 = (f32[2,6,192]{2,0,1:T(2,128)S(1)}, f32[2,6,192]{2,0,1:T(2,128)}, u32[]{:S(2)}) copy-start(f32[2,6,192]{2,0,1:T(2,128)} %param.57) | copy-start | bytes 27652
  284.3 101.8 %copy-start.55 = (f32[2,6,192]{2,0,1:T(2,128)S(1)}, f32[2,6,192]{2,0,1:T(2,128)}, u32[]{:S(2)}) copy-start(f32[2,6,192]{2,0,1:T(2,128)} %param.56) | copy-start | bytes 27652
  284.3 106.0 %copy-start.60 = (f32[123]{0:T(128)S(1)}, f32[123]{0:T(128)}, u32[]{:S(2)}) copy-start(f32[123]{0:T(128)} %param.61) | copy-start | bytes 1480
  284.3 106.0 %copy-start.61 = (f32[123]{0:T(128)S(1)}, f32[123]{0:T(128)}, u32[]{:S(2)}) copy-start(f32[123]{0:T(128)} %param.63) | copy-start | bytes 1480
  284.3 106.0 %copy-start.62 = (f32[123]{0:T(128)S(1)}, f32[123]{0:T(128)}, u32[]{:S(2)}) copy-start(f32[123]{0:T(128)} %param.62) | copy-start | bytes 1480
  284.3 106.6 %copy-start.26 = (f32[960,6]{0,1:T(8,128)S(1)}, f32[960,6]{0,1:T(8,128)}, u32[]{:S(2)}) copy-start(f32[960,6]{0,1:T(8,128)} %param.58) | copy-start | bytes 69124
  284.3 106.5 %copy-start.41 = (f32[960,6]{0,1:T(8,128)S(1)}, f32[960,6]{0,1:T(8,128)}, u32[]{:S(2)}) copy-start(f32[960,6]{0,1:T(8,128)} %param.60) | copy-start | bytes 69124
  284.3 106.5 %copy-start.42 = (f32[960,6]{0,1:T(8,128)S(1)}, f32[960,6]{0,1:T(8,128)}, u32[]{:S(2)}) copy-start(f32[960,6]{0,1:T(8,128)} %param.59) | copy-start | bytes 69124
  284.4 107.2 %copy-start.35 = (f32[192,12]{0,1:T(8,128)S(1)}, f32[192,12]{0,1:T(8,128)}, u32[]{:S(2)}) copy-start(f32[192,12]{0,1:T(8,128)} %param.52) | copy-start | bytes 27652
  284.4 107.2 %copy-start.47 = (f32[192,12]{0,1:T(8,128)S(1)}, f32[192,12]{0,1:T(8,128)}, u32[]{:S(2)}) copy-start(f32[192,12]{0,1:T(8,128)} %param.54) | copy-start | bytes 27652
  284.4 107.2 %copy-start.48 = (f32[192,12]{0,1:T(8,128)S(1)}, f32[192,12]{0,1:T(8,128)}, u32[]{:S(2)}) copy-start(f32[192,12]{0,1:T(8,128)} %param.53) | copy-start | bytes 27652
  284.4 107.8 %copy-start.30 = (f32[24,768]{1,0:T(8,128)S(1)}, f32[24,768]{1,0:T(8,128)}, u32[]{:S(2)}) copy-start(f32[24,768]{1,0:T(8,128)} %param.51) | copy-start | bytes 221188
  284.4 107.8 %copy-start.31 = (f32[24,768]{1,0:T(8,128)S(1)}, f32[24,768]{1,0:T(8,128)}, u32[]{:S(2)}) copy-start(f32[24,768]{1,0:T(8,128)} %param.50) | copy-start | bytes 221188
  284.4 109.3 %copy-start.49 = (f32[4,8,128]{2,1,0:T(8,128)S(1)}, f32[4,8,128]{2,1,0:T(8,128)}, u32[]{:S(2)}) copy-start(f32[4,8,128]{2,1,0:T(8,128)} %param.45) | copy-start | bytes 49156
  284.4 109.3 %copy-start.50 = (f32[4,8,128]{2,1,0:T(8,128)S(1)}, f32[4,8,128]{2,1,0:T(8,128)}, u32[]{:S(2)}) copy-start(f32[4,8,128]{2,1,0:T(8,128)} %param.44) | copy-start | bytes 49156
  (46 other events, 148.8 us)

commit v3 on v2

--- a/solution.py
+++ b/solution.py
@@ -243,8 +243,7 @@
     text_sum_ref, layout_sum_ref, spatial_ref, key_text, value_text, key_layout, value_layout,
     query_ref, slot_text, slot_layout,
 ):
-    found = found_ref[...].astype(jnp.float32).reshape(32, 4, 24, 128)
-    embedded = (found[:, 0] + found[:, 1] + found[:, 2] + found[:, 3]).reshape(768, 128).T
+    embedded = found_ref[...].astype(jnp.float32).reshape(768, 128).T
     place = position_ref[...]
     place = jnp.concatenate([place, place], 0)
     text_sum = embedded + place[:, :768]
@@ -784,8 +783,27 @@
     )(picked, table, labels, weights, counts)
 
 
-def device_at(number):
-    return number // 4, number % 4
+def greet_groups(place, extra):
+    barrier = pltpu.get_barrier_semaphore()
+    dp, vocab = device_of(place)
+
+    def signal(device):
+        pl.semaphore_signal(barrier, inc=1, device_id=device, device_id_type=MESH)
+
+    def group(step, carry):
+        signal(((dp + step) % 32, vocab))
+        return carry
+
+    lax.fori_loop(1, 32, group, 0)
+    for step in (1, 2, 3):
+        signal((dp, (vocab + step) % 4))
+    for peer in extra:
+        signal(device_of(peer))
+    pl.semaphore_wait(barrier, 34 + len(extra))
+
+
+def beyond(place):
+    return moved(place, "x", 2 * (place["x"] % 2) - 1)
 
 
 def start_kernel(
@@ -794,22 +812,13 @@
     ins, refs = refs[:count], refs[count:]
     notes_out, found_out, table_out = refs[:3]
     outs, refs = refs[3 : 3 + count], refs[3 + count :]
-    notes_all, found, note_sems, found_sems, table_sems = refs[:5]
-    plane_send, plane_recv, ring_send, ring_recv, pass_send, pass_recv = refs[5:]
+    notes_all, found, found_in, merged = refs[:4]
+    note_sems, spread_sems, found_sems, vocab_sems, table_sems = refs[4:9]
+    own_sem, ring_send, ring_recv, pass_send, pass_recv = refs[9:]
     place = my_place()
     sibling = moved(place, "c", 1)
-    me = lax.axis_index("dp") * 4 + lax.axis_index("vocab")
-    own_dp, own_vocab = device_at(me)
-    barrier = pltpu.get_barrier_semaphore()
-
-    def greet_one(step, carry):
-        pl.semaphore_signal(
-            barrier, inc=1, device_id=device_at((me + step) % 128), device_id_type=MESH
-        )
-        return carry
-
-    lax.fori_loop(1, 128, greet_one, 0)
-    pl.semaphore_wait(barrier, 127)
+    own_dp, own_vocab = device_of(place)
+    greet_groups(place, [beyond(place)])
 
     def to_device(src, dst, sems, device):
         return pltpu.make_async_remote_copy(
@@ -817,27 +826,74 @@
             device_id=device, device_id_type=MESH,
         )
 
-    planes = []
-    for piece, (number, lanes, order) in enumerate(pieces):
-        here = block_view(outs[number], place, "", lanes, place["c"])
-        src = ins[number].at[:, lanes_at(ins[number], lanes)]
-        pltpu.make_async_copy(src, here, plane_recv.at[piece]).start()
-        for a, b in PLANE_STEPS:
-            copy = remote(
-                src, here, plane_send.at[piece, 4 * a + b - 1], plane_recv.at[piece],
-                plane_peer(place, PLANES[order], a, b),
-            )
-            copy.start()
-            planes.append(copy)
-    own_note = pltpu.make_async_copy(notes_ref, notes_all.at[me], note_sems.at[1])
-    own_note.start()
-
-    def send_note(step, carry):
-        to_device(notes_ref, notes_all.at[me], note_sems, device_at((me + step) % 128)).start()
-        return carry
-
-    lax.fori_loop(1, 128, send_note, 0)
-
+    rings, passes = {}, []
+
+    def spot(number, origin, dims, lanes):
+        return block_view(outs[number], origin, dims, lanes, place["c"])
+
+    def send(phase, way, piece, src, dst, target):
+        copy = remote(
+            src, dst, ring_send.at[phase, way, piece], ring_recv.at[phase, way, piece], target
+        )
+        copy.start()
+        rings[(phase, way, piece)] = copy
+
+    def hand_over(phase, way, piece, where):
+        copy = remote(
+            where, where, pass_send.at[phase, way, piece], pass_recv.at[phase, way, piece], sibling
+        )
+        copy.start()
+        passes.append(copy)
+
+    def begin(phase, piece):
+        number, lanes, order = pieces[piece]
+        dim, dims = ORDERS[order][phase], ORDERS[order][:phase]
+        where = spot(number, place, dims, lanes)
+        src = ins[number].at[:, lanes_at(ins[number], lanes)] if phase == 0 else where
+        for way, step in ((0, 1), (1, -1)):
+            send(phase, way, piece, src, where, moved(place, dim, step))
+
+    def forward(phase):
+        for piece, (number, lanes, order) in enumerate(pieces):
+            dim, dims = ORDERS[order][phase], ORDERS[order][:phase]
+            parts = halves(lanes, piece)
+            for way, step in ((0, 1), (1, -1)):
+                rings[(phase, way, piece)].wait_recv()
+                origin = moved(place, dim, -step)
+                if parts[way] is not False:
+                    onward = spot(number, origin, dims, parts[way])
+                    send(phase, 2 + way, piece, onward, onward, moved(place, dim, step))
+                if phase == 2:
+                    hand_over(phase, way, piece, spot(number, origin, dims, lanes))
+
+    def conclude(phase):
+        for piece, (number, lanes, order) in enumerate(pieces):
+            dim, dims = ORDERS[order][phase], ORDERS[order][:phase]
+            parts = halves(lanes, piece)
+            for way in range(2):
+                if parts[way] is not False:
+                    rings[(phase, 2 + way, piece)].wait_recv()
+            if phase == 0:
+                begin(1, piece)
+            elif phase == 1:
+                begin(2, piece)
+                hand_over(1, 0, piece, spot(number, place, ORDERS[order][:2], lanes))
+            else:
+                hand_over(2, 2, piece, spot(number, moved(place, dim, 2), dims, lanes))
+
+    own_copies = []
+    for piece in range(len(pieces)):
+        begin(0, piece)
+    for number in range(count):
+        copy = pltpu.make_async_copy(
+            ins[number], spot(number, place, "", None), own_sem.at[number]
+        )
+        copy.start()
+        own_copies.append(copy)
+    own_notes = notes_all.at[own_dp, own_vocab]
+    pltpu.make_async_copy(notes_ref, own_notes, note_sems.at[1]).start()
+    for step in (1, 2, 3):
+        to_device(notes_ref, own_notes, note_sems, (own_dp, (own_vocab + step) % 4)).start()
     pltpu.make_async_copy(
         blocks_ref.at[own_dp], table_out.at[own_dp], table_sems.at[1]
     ).start()
@@ -851,12 +907,26 @@
 
     lax.fori_loop(1, 32, send_block, 0)
 
-    rows = found.shape[1]
+    group_notes = notes_all.at[own_dp]
+    pltpu.make_async_copy(group_notes, group_notes, note_sems.at[1]).wait()
+
+    def send_notes(step, carry):
+        to_device(
+            group_notes, group_notes, spread_sems, ((own_dp + step) % 32, own_vocab)
+        ).start()
+        return carry
+
+    lax.fori_loop(1, 32, send_notes, 0)
+    for copy in own_copies:
+        copy.wait()
+    forward(0)
+    rows = found.shape[2]
     levels = levels_ref.shape[0] // rows
 
     def pick(step, carry):
-        block = (step + me // 8) % 16
-        ids = jnp.concatenate([notes_all[block * 8 + n, 0:1, :] for n in range(8)], 1)
+        ids = jnp.concatenate(
+            [notes_all[step * 2 + n // 4, n % 4, 0:1, :] for n in range(8)], 1
+        )
         local = ids - own_vocab * width
         high = jnp.where((local >= 0) & (local < width), local >> 8, -1)
         low = local & 255
@@ -875,68 +945,57 @@
                 )
         total = total.astype(LOW)
         for n in range(8):
-            there = block * 8 + n
-            found[there] = total[:, 128 * n : 128 * n + 128]
-
-            @pl.when(there != me)
-            def _():
-                to_device(
-                    found.at[there], found_out.at[me], found_sems, device_at(there)
-                ).start()
-
+            found[step * 2 + n // 4, n % 4] = total[:, 128 * n : 128 * n + 128]
         return carry
 
-    rings, passes = {}, []
-
-    def spot(number, origin, dims, lanes):
-        return block_view(outs[number], origin, dims, lanes, place["c"])
-
-    def send(way, piece, src, target):
-        copy = remote(src, src, ring_send.at[way, piece], ring_recv.at[way, piece], target)
+    arrived = notes_all.at[pl.ds(0, 31)]
+    pltpu.make_async_copy(arrived, arrived, spread_sems.at[1]).wait()
+    conclude(0)
+    lax.fori_loop(0, 3, pick, 0)
+    forward(1)
+    lax.fori_loop(3, 6, pick, 0)
+    conclude(1)
+    lax.fori_loop(6, 16, pick, 0)
+    swaps = []
+    for step in (1, 2, 3):
+        there = (own_vocab + step) % 4
+        copy = pltpu.make_async_remote_copy(
+            src_ref=found.at[:, there], dst_ref=found_in.at[own_vocab],
+            send_sem=vocab_sems.at[0, step - 1], recv_sem=vocab_sems.at[1, step - 1],
+            device_id=(own_dp, there), device_id_type=MESH,
+        )
         copy.start()
-        rings[(way, piece)] = copy
-
-    def hand_over(way, piece, where):
-        copy = remote(where, where, pass_send.at[way, piece], pass_recv.at[way, piece], sibling)
-        copy.start()
-        passes.append(copy)
-
-    for piece, (number, lanes, order) in enumerate(pieces):
-        sheet = spot(number, place, PLANES[order], lanes)
-        pltpu.make_async_copy(sheet, sheet, plane_recv.at[piece]).wait()
-        for way, step in ((0, 1), (1, -1)):
-            send(way, piece, sheet, moved(place, LINES[order], step))
-        hand_over(2, piece, sheet)
-    pltpu.make_async_copy(notes_all, notes_all, note_sems.at[1]).wait()
-    lax.fori_loop(0, 8, pick, 0)
-    for piece, (number, lanes, order) in enumerate(pieces):
-        dim, dims = LINES[order], PLANES[order]
-        parts = halves(lanes, piece)
-        for way, step in ((0, 1), (1, -1)):
-            rings[(way, piece)].wait_recv()
-            origin = moved(place, dim, -step)
-            if parts[way] is not False:
-                send(2 + way, piece, spot(number, origin, dims, parts[way]), moved(place, dim, step))
-            hand_over(way, piece, spot(number, origin, dims, lanes))
-    lax.fori_loop(8, 16, pick, 0)
-    own_found = pltpu.make_async_copy(found.at[me], found_out.at[me], found_sems.at[1])
-    own_found.start()
-    for piece, (number, lanes, order) in enumerate(pieces):
-        parts = halves(lanes, piece)
-        for way in range(2):
-            if parts[way] is not False:
-                rings[(2 + way, piece)].wait_recv()
-        far = moved(place, LINES[order], 2)
-        hand_over(3, piece, spot(number, far, PLANES[order], lanes))
+        swaps.append(copy)
+    forward(2)
+    total = found[:, own_vocab]
+    for step in (1, 2, 3):
+        swaps[step - 1].wait_recv()
+        total = total + found_in[(own_vocab - step + 4) % 4]
+    merged[...] = total
+    pltpu.make_async_copy(merged.at[own_dp], found_out.at[own_dp], found_sems.at[1]).start()
+
+    def send_found(step, carry):
+        there = (own_dp + step) % 32
+        to_device(
+            merged.at[there], found_out.at[own_dp], found_sems, (there, own_vocab)
+        ).start()
+        return carry
+
+    lax.fori_loop(1, 32, send_found, 0)
+    conclude(2)
     notes_out[...] = notes_all[...]
     pltpu.make_async_copy(found_out, found_out, found_sems.at[1]).wait()
     pltpu.make_async_copy(table_out, table_out, table_sems.at[1]).wait()
-    for sems, ref, size in (
-        (note_sems, notes_all, 127), (found_sems, found, 127), (table_sems, blocks_ref, 31)
+    for sems, ref in (
+        (note_sems, notes_all.at[0, pl.ds(0, 3)]),
+        (spread_sems, arrived),
+        (found_sems, merged.at[pl.ds(0, 31)]),
+        (table_sems, blocks_ref.at[pl.ds(0, 31)]),
     ):
-        sent = ref.at[pl.ds(0, size)]
-        pltpu.make_async_copy(sent, sent, sems.at[0]).wait()
-    for copy in planes + list(rings.values()):
+        pltpu.make_async_copy(ref, ref, sems.at[0]).wait()
+    for copy in swaps:
+        copy.wait_send()
+    for copy in rings.values():
         copy.wait_send()
     for copy in passes:
         copy.wait()
@@ -951,25 +1010,28 @@
     notes_all, found, table, *outs = pl.pallas_call(
         functools.partial(start_kernel, pieces, count, width),
         out_shape=[
-            jax.ShapeDtypeStruct((128,) + notes.shape, jnp.int32),
-            jax.ShapeDtypeStruct((128, rows, 128), LOW),
+            jax.ShapeDtypeStruct((32, 4) + notes.shape, jnp.int32),
+            jax.ShapeDtypeStruct((32, rows, 128), LOW),
             jax.ShapeDtypeStruct(blocks.shape, LOW),
         ]
         + [jax.ShapeDtypeStruct((2, 4, 4, 2, 2) + a.shape, a.dtype) for a in arrays],
         in_specs=[local, local, anywhere] + [anywhere] * count,
         out_specs=[local, anywhere, anywhere] + [anywhere] * count,
         scratch_shapes=[
-            pltpu.VMEM((128,) + notes.shape, jnp.int32),
-            pltpu.VMEM((128, rows, 128), LOW),
+            pltpu.VMEM((32, 4) + notes.shape, jnp.int32),
+            pltpu.VMEM((32, 4, rows, 128), LOW),
+            pltpu.VMEM((4, 32, rows, 128), LOW),
+            pltpu.VMEM((32, rows, 128), LOW),
             sems((2,)),
             sems((2,)),
             sems((2,)),
-            sems((total, 15)),
-            sems((total,)),
-            sems((4, total)),
-            sems((4, total)),
-            sems((4, total)),
-            sems((4, total)),
+            sems((2, 3)),
+            sems((2,)),
+            sems((count,)),
+            sems((3, 4, total)),
+            sems((3, 4, total)),
+            sems((3, 3, total)),
+            sems((3, 3, total)),
         ],
         cost_estimate=LONG,
         compiler_params=pltpu.CompilerParams(
@@ -985,23 +1047,14 @@
     text_ref, notes_ref, head_ref, refs = refs[0], refs[1], refs[2], refs[3:]
     outs, table_ref, square_ref, refs = refs[:count], refs[count], refs[count + 1], refs[count + 2 :]
     accs, crosses, refs = refs[:count], refs[count : 2 * count], refs[2 * count :]
-    slots, planes, refs = refs[: 4 * total], refs[4 * total : 5 * total], refs[5 * total :]
+    slots, refs = refs[: 12 * total], refs[12 * total :]
     text_all, spread, near, far = refs[:4]
-    own_sem, core_sems, line_sems, plane_sems, text_sems, near_sems, far_sems = refs[4:]
+    own_sem, core_sems, ring_sems, text_sems, vocab_sems, near_sems, far_sems = refs[4:]
     place = my_place()
     sibling = moved(place, "c", 1)
-    me = lax.axis_index("dp") * 4 + lax.axis_index("vocab")
-    own_dp, own_vocab = device_at(me)
-    barrier = pltpu.get_barrier_semaphore()
-
-    def greet_one(step, carry):
-        pl.semaphore_signal(
-            barrier, inc=1, device_id=device_at((me + step) % 128), device_id_type=MESH
-        )
-        return carry
-
-    lax.fori_loop(1, 128, greet_one, 0)
-    pl.semaphore_wait(barrier, 127)
+    own_dp, own_vocab = device_of(place)
+    across = moved(moved(place, "x", 2), "c", 1)
+    greet_groups(place, [beyond(place), moved(beyond(place), "c", 1), across])
     started = []
 
     def go(src, dst, sems, index, target):
@@ -1052,53 +1105,90 @@
             first.setdefault(piece, []).append((cross, own))
             pair += 1
 
-    def text_copy(block, device):
-        return pltpu.make_async_remote_copy(
-            src_ref=text_ref.at[block], dst_ref=text_all.at[me], send_sem=text_sems.at[0],
-            recv_sem=text_sems.at[1], device_id=device, device_id_type=MESH,
+    own_text = text_all.at[own_dp, own_vocab]
+    pltpu.make_async_copy(text_ref.at[own_dp], own_text, text_sems.at[1]).start()
+
+    def send_text(step, carry):
+        there = (own_dp + step) % 32
+        pltpu.make_async_remote_copy(
+            src_ref=text_ref.at[there], dst_ref=own_text, send_sem=text_sems.at[0],
+            recv_sem=text_sems.at[1], device_id=(there, own_vocab), device_id_type=MESH,
+        ).start()
+        return carry
+
+    rings = {}
+
+    def slot(phase, way, piece):
+        return slots[(phase * 4 + way) * total + piece]
+
+    def send(phase, way, piece, src, step):
+        number, lanes, order = pieces[piece]
+        rings[(phase, way, piece)] = go(
+            src, slot(phase, way, piece), ring_sems, (phase, way, piece),
+            moved(place, ORDERS[order][phase], step),
         )
 
-    pltpu.make_async_copy(text_ref.at[own_dp], text_all.at[me], text_sems.at[1]).start()
-
-    def send_text(step, carry):
-        there = (me + step) % 128
-        text_copy(there // 4, device_at(there)).start()
-        return carry
-
-    rings = {}
-
-    def send_opposite(piece):
+    def begin(phase, piece):
         number, lanes, order = pieces[piece]
+        dim, rest = ORDERS[order][phase], ORDERS[order][phase + 1 :]
         parts = halves(lanes, piece)
-        there = moved(place, LINES[order], 2)
+        there = moved(place, dim, 2)
         for way, step in ((0, 1), (1, -1)):
             if parts[way] is not False:
-                rings[(way, piece)] = go(
-                    block_view(accs[number], there, PLANES[order], parts[way]),
-                    slots[way * total + piece], line_sems, (way, piece),
-                    moved(place, LINES[order], step),
-                )
-
+                send(phase, way, piece, block_view(accs[number], there, rest, parts[way]), step)
+
+    def pass_on(phase):
+        for piece, (number, lanes, order) in enumerate(pieces):
+            dim, rest = ORDERS[order][phase], ORDERS[order][phase + 1 :]
+            parts = halves(lanes, piece)
+            for way, step in ((0, 1), (1, -1)):
+                there = moved(place, dim, step)
+                if parts[way] is not False:
+                    rings[(phase, way, piece)].wait_recv()
+                    add(number, parts[way], there, rest, [(slot(phase, way, piece), None)])
+                send(phase, 2 + way, piece, block_view(accs[number], there, rest, lanes), step)
+
+    def take_in(phase):
+        for piece, (number, lanes, order) in enumerate(pieces):
+            rest = ORDERS[order][phase + 1 :]
+            for way in range(2):
+                rings[(phase, 2 + way, piece)].wait_recv()
+            others = [slot(phase, 2 + way, piece) for way in range(2)]
+            if phase < 2:
+                add(number, lanes, place, rest, [(other, None) for other in others])
+                begin(phase + 1, piece)
+            else:
+                where = (slice(None), lanes_at(accs[number], lanes))
+                value = accs[number][home + where].astype(jnp.float32)
+                for other in others:
+                    value = value + other[...].astype(jnp.float32)
+                outs[number][where] = value
+
+    home = (place["x"] // 2, place["y"], place["z"], place["x"] % 2)
     for piece, (number, lanes, order) in enumerate(pieces):
         for cross, own in first[piece]:
             own.wait()
             cross.wait_recv()
         run = (slice(None), lanes_at(accs[number], lanes))
         add(number, lanes, place, "xyz", [(crosses[number], run)])
-        send_opposite(piece)
+        begin(0, piece)
         if piece == 2:
-            lax.fori_loop(1, 128, send_text, 0)
-
-    rows = text_all.shape[1]
+            lax.fori_loop(1, 32, send_text, 0)
+
+    rows = text_all.shape[2]
     levels = head_ref.shape[0] // rows
     table_ref[...] = head_ref[...]
 
     def scatter(block, carry):
-        ids = jnp.concatenate([notes_ref[block * 8 + n, 0:1, :] for n in range(8)], 1)
+        ids = jnp.concatenate(
+            [notes_ref[block * 2 + n // 4, n % 4, 0:1, :] for n in range(8)], 1
+        )
         local = ids - own_vocab * width
         high = jnp.where((local >= 0) & (local < width), local >> 8, -1)
         hot = (lax.broadcasted_iota(jnp.int32, (SPAN_LOW, 1024), 0) == (local & 255)).astype(LOW)
-        grad = jnp.concatenate([text_all[block * 8 + n] for n in range(8)], 1).astype(jnp.float32)
+        grad = jnp.concatenate(
+            [text_all[block * 2 + n // 4, n % 4] for n in range(8)], 1
+        ).astype(jnp.float32)
         for level in range(0, levels, 2):
             spread[pl.ds(level * rows, 2 * rows), :] = jnp.concatenate(
                 [jnp.where(high == level + n, grad, 0.0) for n in range(2)], 0
@@ -1108,48 +1198,37 @@
             table_ref[pl.ds(start, group), :] += cols_product(spread[pl.ds(start, group), :], hot)
         return carry
 
-    for piece, (number, lanes, order) in enumerate(pieces):
-        parts = halves(lanes, piece)
-        for way, step in ((0, 1), (1, -1)):
-            there = moved(place, LINES[order], step)
-            if parts[way] is not False:
-                rings[(way, piece)].wait_recv()
-                add(number, parts[way], there, PLANES[order], [(slots[way * total + piece], None)])
-            rings[(2 + way, piece)] = go(
-                block_view(accs[number], there, PLANES[order], lanes),
-                slots[(2 + way) * total + piece], line_sems, (2 + way, piece), there,
-            )
-    whole = pltpu.make_async_copy(text_all, text_all, text_sems.at[1])
-    whole.wait()
-    lax.fori_loop(0, 10, scatter, 0)
-    for piece, (number, lanes, order) in enumerate(pieces):
-        for way in range(2):
-            rings[(2 + way, piece)].wait_recv()
-        add(
-            number, lanes, place, PLANES[order],
-            [(slots[(2 + way) * total + piece], None) for way in range(2)],
+    own_column = text_all.at[:, own_vocab]
+    pltpu.make_async_copy(own_column, own_column, text_sems.at[1]).wait()
+    swaps = []
+    for step in (1, 2, 3):
+        copy = pltpu.make_async_remote_copy(
+            src_ref=own_column, dst_ref=own_column, send_sem=vocab_sems.at[0, step - 1],
+            recv_sem=vocab_sems.at[1, step - 1], device_id=(own_dp, (own_vocab + step) % 4),
+            device_id_type=MESH,
         )
-        for a, b in PLANE_STEPS:
-            there = plane_peer(place, PLANES[order], a, b)
-            remote(
-                block_view(accs[number], there, "", lanes), planes[piece].at[4 * a + b - 1],
-                plane_sems.at[0, piece], plane_sems.at[1, piece], there,
-            ).start()
-    lax.fori_loop(10, 16, scatter, 0)
-    home = (place["x"] // 2, place["y"], place["z"], place["x"] % 2)
+        copy.start()
+        swaps.append(copy)
+    pass_on(0)
+    for copy in swaps:
+        copy.wait_recv()
+    lax.fori_loop(0, 7, scatter, 0)
+    take_in(0)
+    lax.fori_loop(7, 10, scatter, 0)
+    pass_on(1)
+    lax.fori_loop(10, 12, scatter, 0)
+    take_in(1)
+    lax.fori_loop(12, 14, scatter, 0)
+    pass_on(2)
+    lax.fori_loop(14, 16, scatter, 0)
+    take_in(2)
     square = jnp.zeros((1, 1), jnp.float32)
 
     def squared(value):
         return jnp.sum(jnp.sum(value * value, 1, keepdims=True), 0, keepdims=True)
 
-    for piece, (number, lanes, order) in enumerate(pieces):
-        pltpu.make_async_copy(planes[piece], planes[piece], plane_sems.at[1, piece]).wait()
-        where = (slice(None), lanes_at(accs[number], lanes))
-        value = accs[number][home + where].astype(jnp.float32)
-        for n in range(15):
-            value = value + planes[piece][n].astype(jnp.float32)
-        outs[number][where] = value
-        square = square + squared(value)
+    for out in outs:
+        square = square + squared(out[...])
     square = square + squared(table_ref[...])
 
     mine = place["x"] * 2 + place["c"]
@@ -1171,10 +1250,10 @@
     for copy in meets:
         copy.wait_recv()
     square_ref[...] = sum(far[n] for n in range(16))
-    for piece in range(total):
-        pltpu.make_async_copy(planes[piece], planes[piece], plane_sems.at[0, piece]).wait()
-    sent = text_all.at[pl.ds(0, 127)]
+    sent = text_ref.at[pl.ds(0, 31)]
     pltpu.make_async_copy(sent, sent, text_sems.at[0]).wait()
+    for copy in swaps:
+        copy.wait_send()
     for copy in started:
         copy.wait_send()
 
@@ -1192,28 +1271,27 @@
         parts = halves(lanes, piece)
         widths.append([shapes[number][1] if part is None else part for part in
                        [p if p in (None, False) else p[1] for p in (*parts, lanes, lanes)]])
-    for way in range(4):
-        for piece, (number, lanes, order) in enumerate(pieces):
-            wide = widths[piece][way]
-            if wide is False:
-                scratch.append(pltpu.VMEM((8, 128), LOW))
-            else:
-                rest = open_shape("".join(PLANES[order]))
-                scratch.append(pltpu.VMEM(rest + (shapes[number][0], wide), LOW))
-    for piece, (number, lanes, order) in enumerate(pieces):
-        scratch.append(pltpu.VMEM((15, shapes[number][0], widths[piece][2]), LOW))
+    for phase in range(3):
+        for way in range(4):
+            for piece, (number, lanes, order) in enumerate(pieces):
+                wide = widths[piece][way]
+                if wide is False:
+                    scratch.append(pltpu.VMEM((8, 128), LOW))
+                else:
+                    rest = open_shape(ORDERS[order][phase + 1 :])
+                    scratch.append(pltpu.VMEM(rest + (shapes[number][0], wide), LOW))
     rows = text.shape[1]
     sems = pltpu.SemaphoreType.DMA
     scratch += [
-        pltpu.VMEM((128, rows, 128), LOW),
+        pltpu.VMEM((32, 4, rows, 128), LOW),
         pltpu.VMEM((head_levels.shape[0], 1024), LOW),
         pltpu.VMEM((8, 8, 128), jnp.float32),
         pltpu.VMEM((16, 8, 128), jnp.float32),
         sems((pairs,)),
         sems((2, pairs)),
-        sems((2, 4, total)),
-        sems((2, total)),
+        sems((2, 3, 4, total)),
         sems((2,)),
+        sems((2, 3)),
         sems((2, 7)),
         sems((2, 15)),
     ]
@@ -1239,7 +1317,7 @@
     return [(number, (256 * k, 256), k) for k in range(3)]
 
 
-GATHER_PIECES = thirds(0) + thirds(1) + [(2, (0, 512), 0), (2, (512, 448), 2), (3, None, 1)]
+GATHER_PIECES = thirds(0) + thirds(1) + [(2, (0, 512), 0), (2, (512, 512), 1), (3, (0, 256), 2)]
 REDUCE_PIECES = (
     thirds(0)
     + thirds(1)
@@ -1262,22 +1340,22 @@
     small = jnp.concatenate(
         [
             jnp.concatenate([box[0], box[1]], 1),
-            jnp.pad(
-                jnp.concatenate(
-                    [
-                        layout.T,
-                        layout_down[0],
-                        layout_down[1],
-                        jnp.pad(vector, (0, 192 - vector.shape[0]))[None],
-                    ],
-                    0,
-                ),
-                ((0, 7), (0, 64)),
-            ),
+            filled(layout.T, 16, 256),
+            filled(layout_down[0], 8, 256),
+            filled(layout_down[1], 8, 256),
+            filled(vector[None], 8, 256),
         ],
         0,
     )
-    return [text.T, down, jnp.concatenate([head.T, position], 0), small]
+    wide = jnp.concatenate([filled(head.T, 8, 1024), filled(position, 8, 1024)], 0)
+    return [text.T, down, wide, small]
+
+
+def filled(values, rows, width):
+    lead = [(0, 0)] * (values.ndim - 2)
+    return jnp.pad(
+        values, lead + [(0, rows - values.shape[-2]), (0, width - values.shape[-1])]
+    )
 
 
 def unpack(gathered):
@@ -1286,13 +1364,13 @@
     return dict(
         text=text,
         down=down.reshape(3072, 768),
-        head=wide[:, :6].reshape(768, 960),
+        head=wide[:, :6, :960].reshape(768, 960),
         box=box.reshape(4096, 128),
         layout=small[:, 16:28, :192].reshape(1536, 192),
-        layout_down=small[:, 28:34, :192].reshape(768, 192),
-        box_proj=small[:, 34:40, :192].reshape(768, 192),
-        position=wide[:, 6:].reshape(640, 960),
-        vector=small[:, 40, :123].reshape(15744),
+        layout_down=small[:, 32:38, :192].reshape(768, 192),
+        box_proj=small[:, 40:46, :192].reshape(768, 192),
+        position=wide[:52, 8:13, :960].reshape(260, 960),
+        vector=small[:, 48, :123].reshape(15744),
     )
 
 
@@ -1388,8 +1466,9 @@
     )
     table_head = table_head.reshape(768, HEAD_BLOCK)
     full = unpack(gathered)
-    labels_all = notes_all[:, 1, :16].reshape(2048)
-    counted_all = notes_all[:, 1, 16:32].reshape(2048).astype(jnp.float32)
+    notes_rows = notes_all.reshape(128, 2, 128)
+    labels_all = notes_rows[:, 1, :16].reshape(2048)
+    counted_all = notes_rows[:, 1, 16:32].reshape(2048).astype(jnp.float32)
     total_count = jnp.sum(counted_all)
 
     vector = full["vector"].astype(jnp.float32)
@@ -1442,7 +1521,9 @@
         ],
         "open_streams",
     )
-    query_all = lax.all_gather(query, "vocab", axis=0, tiled=True)
+    query_all = lax.all_to_all(
+        jnp.broadcast_to(query[None], (4, 16, 1024)), "vocab", 0, 0, tiled=True
+    ).reshape(64, 1024)
     (partial,) = local_call(score_kernel, [query_all, *kv], [((64, 1280), f32)], "partial_attention")
     partial = lax.all_to_all(partial.reshape(4, 16, 1280), "vocab", 0, 0, tiled=True)
     weights_close = [out_w, up_w, full["down"], full["layout"], full["layout_down"]]
@@ -1503,7 +1584,9 @@
         ],
         "close_streams_back",
     )
-    back = lax.all_gather(back, "vocab", axis=0, tiled=True)
+    back = lax.all_to_all(
+        jnp.broadcast_to(back[None], (4, 16, 1280)), "vocab", 0, 0, tiled=True
+    ).reshape(64, 1280)
     d_query, *d_kv = local_call(
         score_back_kernel,
         [back, query_all, *kv],

time: 402 us -> 391 us (0.973)
  Pallas kernels: 296 us -> 280 us
  blocking collectives: 25.4 us -> 9.95 us
  starting transfers between devices: 13.3 us -> 28.5 us
  waiting for transfers between devices: 1.43 us -> 6.86 us
    all_gather x2 -> x0, blocking collectives: 25.4 us -> none  [the longest x1 18.7 us: on_device(): query_all = lax.all_gather(query, 'vocab', axis=0, tiled=True)]
    all_to_all x0 -> x1, starting transfers between devices: none -> 15.6 us  [on_device(): lax.all_to_all(jnp.broadcast_to(query[None], (4, 16, 1024)), 'vocab', 0,...]
    pallas_call x1, Pallas kernels: 91.3 us -> 79.1 us  [start_step(): pl.pallas_call(functools.partial(start_kernel, pieces, count, width), out...]
    all_to_all x0 -> x1, blocking collectives: none -> 9.95 us  [on_device(): lax.all_to_all(jnp.broadcast_to(back[None], (4, 16, 1280)), 'vocab', 0, 0...]
    all_to_all x1, waiting for transfers between devices: 0.01 us -> 5.45 us  [on_device(): lax.all_to_all(partial.reshape(4, 16, 1280), 'vocab', 0, 0, tiled=True)]
    unnamed x139 -> x142, local copies, waits for them, and re-layouts: 7.67 us -> 8.25 us
  transfers between devices with their start and end apart: 3 -> 4, of which waited for: 1 -> 2; matrix products, arithmetic and copies ran while one was open for 5% -> 6% of each run, Pallas kernels for 2% -> 2%
where the time goes in v3:
time: 391 us; the launch traced here: 387 us
  Pallas kernels  280 us (72%)
  local copies, waits for them, and re-layouts  40.9 us (10%)
  starting transfers between devices  28.5 us (7%)
  other arithmetic  17 us (4%)
  blocking collectives  9.95 us (3%)
  waiting for transfers between devices  6.86 us (2%)
    pallas_call x1, Pallas kernels, finish_step(): pl.pallas_call(functools.partial(finish_kernel, sources, pieces, count, w...  97 us
    pallas_call x1, Pallas kernels, start_step(): pl.pallas_call(functools.partial(start_kernel, pieces, count, width), out...  79.1 us
    pallas_call x1, Pallas kernels, head_step(): pl.pallas_call(kernel, out_shape=[jax.ShapeDtypeStruct((16, 768), jnp.flo...  57.7 us
    pallas_call x6, Pallas kernels, local_call(): pl.pallas_call(kernel, name=name, grid=(1,), out_shape=[jax.ShapeDtypeStr...  46.1 us
    all_to_all x1, starting transfers between devices, on_device(): lax.all_to_all(jnp.broadcast_to(query[None], (4, 16, 1024)), 'vocab', 0,...  15.6 us
    all_to_all x1, blocking collectives, on_device(): lax.all_to_all(jnp.broadcast_to(back[None], (4, 16, 1280)), 'vocab', 0, 0...  9.95 us
    unnamed x142, local copies, waits for them, and re-layouts  8.25 us
  transfers between devices with their start and end apart: 4, of which 2 were waited for; matrix products, arithmetic and copies ran while one was open for 6% of the time, Pallas kernels for 2%

profile of v3, /device:TPU:0, one launch (start us, length us, event | category | flops | bytes accessed | tf_op | source)
XLA Modules:
  0.0 386.9 jit_solution(7160099524578020736)
XLA Ops:
  4.9 79.1 %shard_map.535 = (s32[32,4,2,128]{3,2,1,0:T(2,128)S(1)}, bf16[32,24,128]{2,1,0:T(8,128)(2,1)S(1)}, bf16[32,24,512]{2,1,0:T(8,128)(2,1)S(1)}, bf16[2,4,4,2,2,48,7...) custom-call(s32[2,128]{1,0:T(2,128)S(1)} %add_add_fusion.notes_ref, ...), custom_call_target="tpu_custom_call" | custom-call | flops 60000002048 | bytes 200000000 | tf_op jit(solution)/shard_map/pallas_call | solution.py:1010
  85.3 1.5 fusion.21
  96.6 1.6 dynamic-slice_convert_fusion.position_ref
  98.9 5.6 %open_streams.1 = (f32[128,768]{1,0:T(8,128)}, f32[128,192]{1,0:T(8,128)}, bf16[128,768]{1,0:T(8,128)(2,1)}, bf16[128,768]{1,0:T(8,128)(2,1)}, bf16[128,768]{1,0...) custom-call(bf16[32,24,128]{2,1,0:T(8,128)(2,1)} %copy-done.2, ...), custom_call_target="tpu_custom_call" | custom-call | tf_op jit(solution)/shard_map/open_streams/pallas_call | solution.py:507
  104.5 1.4 broadcast_in_dim.39
  105.9 15.6 %all-to-all-start = ((bf16[4,16,1024]{2,1,0:T(8,128)(2,1)}), bf16[4,16,1024]{2,1,0:T(8,128)(2,1)S(1)}, u32[]{:S(2)}, u32[]{:S(2)}) async-start(bf16[4,16,1024]{2,1,0:T(8,128)(2,1)} %broadcast_in_dim.39), calls=%async_computation | async-start | bytes 262144 | tf_op jit(solution)/shard_map/all_to_all | solution.py:1524
  121.5 1.8 slice.135
  124.9 1.8 reshape.307.head_ref
  129.0 3.2 partial_attention.1
  132.3 3.5 all-to-all-start.1
  137.0 5.4 %all-to-all-done.1.parts_ref = f32[4,16,1280]{2,1,0:T(8,128)S(1)} async-done(((f32[4,16,1280]{2,1,0:T(8,128)}), f32[4,16,1280]{2,1,0:T(8,128)S(1)}, u32[]{:S(2)}, u32[]{:S(2)}) %all-to-all-start.1) | async-done | bytes 327712 | tf_op jit(solution)/shard_map/all_to_all | solution.py:1528
  143.2 10.4 %close_streams.1 = (f32[16,768]{1,0:T(8,128)}, f32[16,192]{1,0:T(8,128)}, f32[16,128]{1,0:T(8,128)}, f32[16,768]{1,0:T(8,128)}, f32[16,192]{1,0:T(8,128)}, /*ind...) custom-call(f32[4,16,1280]{2,1,0:T(8,128)} %copy-done.8, ...), custom_call_target="tpu_custom_call" | custom-call | tf_op jit(solution)/shard_map/close_streams/pallas_call | solution.py:507
  153.5 57.7 %shard_map.536 = (f32[16,768]{1,0:T(8,128)}, bf16[768,512]{1,0:T(8,128)(2,1)}, f32[8,128]{1,0:T(8,128)}) custom-call(bf16[16,768]{1,0:T(8,128)(2,1)} %get-tuple-element.111.refs_0_, bf16[768,512]{1,0:T(8,128)(2,1)} %bitcast.129, s32[1,2048]{1,0:T(1,128)} %sub.83.refs_2_, f32[1,2048]{1,0:T(1,128)} %broadcast_divide_fusion.refs_3_, f32[1,2048]{1,0:T(1,128)} %copy-done.29), custom_call_target="tpu_custom_call" | custom-call | tf_op jit(solution)/shard_map/pallas_call | solution.py:739
  211.2 15.5 %close_streams_back.1 = (f32[16,1280]{1,0:T(8,128)}, f32[16,768]{1,0:T(8,128)}, f32[16,192]{1,0:T(8,128)}, bf16[768,960]{1,0:T(8,128)(2,1)}, bf16[768,768]{1,0:T...) custom-call(f32[16,768]{1,0:T(8,128)} %get-tuple-element.114.grad_re, ...), custom_call_target="tpu_custom_call" | custom-call | tf_op jit(solution)/shard_map/close_streams_back/pallas_call | solution.py:507
  227.7 9.9 %all_to_all.25 = f32[4,16,1280]{2,1,0:T(8,128)} all-to-all(f32[4,16,1280]{2,1,0:T(8,128)S(1)} %broadcast_in_dim.40), channel_id=1, replica_groups=mesh['dp'=32,'vocab'=4] {'vocab'}, dimensions={0} | all-to-all | bytes 655360 | tf_op jit(solution)/shard_map/all_to_all | solution.py:1587
  237.6 4.0 %attention_back.1 = (f32[64,1024]{1,0:T(8,128)}, bf16[128,768]{1,0:T(8,128)(2,1)}, bf16[128,768]{1,0:T(8,128)(2,1)}, bf16[128,192]{1,0:T(8,128)(2,1)}, bf16[128,192]{1,0:T(8,128)(2,1)}) custom-call(f32[64,1280]{1,0:T(8,128)} %bitcast.148, bf16[64,1024]{1,0:T(8,128)(2,1)} %bitcast.153, bf16[128,768]{1,0:T(8,128)(2,1)} %get-tuple-element.104.key_text, ...), custom_call_target="tpu_custom_call" | custom-call | tf_op jit(solution)/shard_map/attention_back/pallas_call | solution.py:507
  241.7 3.4 all-to-all-start.3
  245.9 1.6 reshape_reshape.43.refs_5_
  251.1 6.1 %all-to-all-start.4 = ((bf16[32,24,512]{2,1,0:T(8,128)(2,1)}), bf16[32,24,512]{2,1,0:T(8,128)(2,1)S(1)}, u32[]{:S(2)}, u32[]{:S(2)}) async-start(bf16[32,24,512]{2,1,0:T(8,128)(2,1)} %bitcast.36), calls=%async_computation.4 | async-start | bytes 1572864 | tf_op jit(solution)/shard_map/all_to_all | solution.py:1561
  257.3 7.4 %open_streams_back.1 = (bf16[768,768]{1,0:T(8,128)(2,1)}, bf16[1536,768]{1,0:T(8,128)(2,1)}, bf16[576,192]{1,0:T(8,128)(2,1)}, bf16[768,128]{1,0:T(8,128)(2,1)},...) custom-call(f32[4,16,1024]{2,1,0:T(8,128)} %copy-done.12, ...), custom_call_target="tpu_custom_call" | custom-call | tf_op jit(solution)/shard_map/open_streams_back/pallas_call | solution.py:507
  269.7 1.6 reshape_reshape.44.refs_6_
  275.4 97.0 %shard_map.537 = (f32[48,768]{1,0:T(8,128)}, f32[24,768]{1,0:T(8,128)}, f32[6,960]{1,0:T(8,128)}, f32[5,960]{1,0:T(8,128)}, f32[12,192]{1,0:T(8,128)}, /*index=5...) custom-call(bf16[1,1,4,2,2,48,768]{6,5,4,3,2,1,0:T(8,128)(2,1)} %bit, ...), custom_call_target="tpu_custom_call" | custom-call | flops 60000002048 | bytes 200000000 | tf_op jit(solution)/shard_map/pallas_call | solution.py:1299
  377.0 1.5 copy.188
  383.4 2.2 multiply_add_fusion
  (235 shorter events, 44.3 us)
Async XLA Ops:
  84.9 41.8 %copy-start.3 = (s32[32,4,2,128]{3,2,1,0:T(2,128)}, s32[32,4,2,128]{3,2,1,0:T(2,128)S(1)}, u32[]{:S(2)}) copy-start(s32[32,4,2,128]{3,2,1,0:T(2,128)S(1)} %get-tuple-element.113.refs_13_) | copy-start | bytes 393220
  105.9 22.5 %all-to-all-start = ((bf16[4,16,1024]{2,1,0:T(8,128)(2,1)}), bf16[4,16,1024]{2,1,0:T(8,128)(2,1)S(1)}, u32[]{:S(2)}, u32[]{:S(2)}) async-start(bf16[4,16,1024]{2,1,0:T(8,128)(2,1)} %broadcast_in_dim.39), calls=%async_computation | async-start | bytes 262144 | tf_op jit(solution)/shard_map/all_to_all | solution.py:1524
  127.0 26.5 %copy-start.29 = (f32[1,2048]{1,0:T(1,128)}, f32[1,2048]{1,0:T(1,128)S(1)}, u32[]{:S(2)}) copy-start(f32[1,2048]{1,0:T(1,128)S(1)} %convert_element_type.118.refs_4_) | copy-start | bytes 24580
  132.3 10.2 %all-to-all-start.1 = ((f32[4,16,1280]{2,1,0:T(8,128)}), f32[4,16,1280]{2,1,0:T(8,128)S(1)}, u32[]{:S(2)}, u32[]{:S(2)}) async-start(f32[4,16,1280]{2,1,0:T(8,128)} %bitcast.149), calls=%async_computation.1 | async-start | bytes 655360 | tf_op jit(solution)/shard_map/all_to_all | solution.py:1528
  226.7 18.4 %copy-start.33 = (f32[16,128]{1,0:T(8,128)S(1)}, f32[16,128]{1,0:T(8,128)}, u32[]{:S(2)}) copy-start(f32[16,128]{1,0:T(8,128)} %fusion.13.slot_ref) | copy-start | bytes 24580
  226.8 19.1 %copy-start.56 = (f32[3,768]{1,0:T(4,128)S(1)}, f32[3,768]{1,0:T(4,128)}, u32[]{:S(2)}) copy-start(f32[3,768]{1,0:T(4,128)} %get-tuple-element.153) | copy-start | bytes 27652
  241.7 9.4 %all-to-all-start.3 = ((f32[4,16,1024]{2,1,0:T(8,128)}), f32[4,16,1024]{2,1,0:T(8,128)S(1)}, u32[]{:S(2)}, u32[]{:S(2)}) async-start(f32[4,16,1024]{2,1,0:T(8,128)} %bitcast.159), calls=%async_computation.3 | async-start | bytes 524288 | tf_op jit(solution)/shard_map/all_to_all | solution.py:1602
  251.1 22.4 %all-to-all-start.4 = ((bf16[32,24,512]{2,1,0:T(8,128)(2,1)}), bf16[32,24,512]{2,1,0:T(8,128)(2,1)S(1)}, u32[]{:S(2)}, u32[]{:S(2)}) async-start(bf16[32,24,512]{2,1,0:T(8,128)(2,1)} %bitcast.36), calls=%async_computation.4 | async-start | bytes 1572864 | tf_op jit(solution)/shard_map/all_to_all | solution.py:1561
  275.3 99.1 %copy-start.39 = (f32[2,6,192]{2,0,1:T(2,128)S(1)}, f32[2,6,192]{2,0,1:T(2,128)}, u32[]{:S(2)}) copy-start(f32[2,6,192]{2,0,1:T(2,128)} %param.55) | copy-start | bytes 27652
  275.3 99.1 %copy-start.54 = (f32[2,6,192]{2,0,1:T(2,128)S(1)}, f32[2,6,192]{2,0,1:T(2,128)}, u32[]{:S(2)}) copy-start(f32[2,6,192]{2,0,1:T(2,128)} %param.57) | copy-start | bytes 27652
  275.3 99.1 %copy-start.55 = (f32[2,6,192]{2,0,1:T(2,128)S(1)}, f32[2,6,192]{2,0,1:T(2,128)}, u32[]{:S(2)}) copy-start(f32[2,6,192]{2,0,1:T(2,128)} %param.56) | copy-start | bytes 27652
  275.3 103.4 %copy-start.60 = (f32[123]{0:T(128)S(1)}, f32[123]{0:T(128)}, u32[]{:S(2)}) copy-start(f32[123]{0:T(128)} %param.61) | copy-start | bytes 1480
  275.3 103.4 %copy-start.61 = (f32[123]{0:T(128)S(1)}, f32[123]{0:T(128)}, u32[]{:S(2)}) copy-start(f32[123]{0:T(128)} %param.63) | copy-start | bytes 1480
  275.3 103.4 %copy-start.62 = (f32[123]{0:T(128)S(1)}, f32[123]{0:T(128)}, u32[]{:S(2)}) copy-start(f32[123]{0:T(128)} %param.62) | copy-start | bytes 1480
  275.3 103.9 %copy-start.26 = (f32[960,6]{0,1:T(8,128)S(1)}, f32[960,6]{0,1:T(8,128)}, u32[]{:S(2)}) copy-start(f32[960,6]{0,1:T(8,128)} %param.58) | copy-start | bytes 69124
  275.3 103.9 %copy-start.41 = (f32[960,6]{0,1:T(8,128)S(1)}, f32[960,6]{0,1:T(8,128)}, u32[]{:S(2)}) copy-start(f32[960,6]{0,1:T(8,128)} %param.60) | copy-start | bytes 69124
  275.3 103.9 %copy-start.42 = (f32[960,6]{0,1:T(8,128)S(1)}, f32[960,6]{0,1:T(8,128)}, u32[]{:S(2)}) copy-start(f32[960,6]{0,1:T(8,128)} %param.59) | copy-start | bytes 69124
  275.3 104.5 %copy-start.35 = (f32[192,12]{0,1:T(8,128)S(1)}, f32[192,12]{0,1:T(8,128)}, u32[]{:S(2)}) copy-start(f32[192,12]{0,1:T(8,128)} %param.52) | copy-start | bytes 27652
  275.4 104.5 %copy-start.47 = (f32[192,12]{0,1:T(8,128)S(1)}, f32[192,12]{0,1:T(8,128)}, u32[]{:S(2)}) copy-start(f32[192,12]{0,1:T(8,128)} %param.54) | copy-start | bytes 27652
  275.4 104.5 %copy-start.48 = (f32[192,12]{0,1:T(8,128)S(1)}, f32[192,12]{0,1:T(8,128)}, u32[]{:S(2)}) copy-start(f32[192,12]{0,1:T(8,128)} %param.53) | copy-start | bytes 27652
  275.4 105.1 %copy-start.30 = (f32[24,768]{1,0:T(8,128)S(1)}, f32[24,768]{1,0:T(8,128)}, u32[]{:S(2)}) copy-start(f32[24,768]{1,0:T(8,128)} %param.51) | copy-start | bytes 221188
  275.4 105.1 %copy-start.31 = (f32[24,768]{1,0:T(8,128)S(1)}, f32[24,768]{1,0:T(8,128)}, u32[]{:S(2)}) copy-start(f32[24,768]{1,0:T(8,128)} %param.50) | copy-start | bytes 221188
  275.4 106.7 %copy-start.49 = (f32[4,8,128]{2,1,0:T(8,128)S(1)}, f32[4,8,128]{2,1,0:T(8,128)}, u32[]{:S(2)}) copy-start(f32[4,8,128]{2,1,0:T(8,128)} %param.45) | copy-start | bytes 49156
  275.4 106.7 %copy-start.50 = (f32[4,8,128]{2,1,0:T(8,128)S(1)}, f32[4,8,128]{2,1,0:T(8,128)}, u32[]{:S(2)}) copy-start(f32[4,8,128]{2,1,0:T(8,128)} %param.44) | copy-start | bytes 49156
  (47 other events, 165.1 us)

commit v4 on v3

--- a/solution.py
+++ b/solution.py
@@ -1584,9 +1584,7 @@
         ],
         "close_streams_back",
     )
-    back = lax.all_to_all(
-        jnp.broadcast_to(back[None], (4, 16, 1280)), "vocab", 0, 0, tiled=True
-    ).reshape(64, 1280)
+    back = lax.all_gather(back, "vocab", axis=0, tiled=True)
     d_query, *d_kv = local_call(
         score_back_kernel,
         [back, query_all, *kv],

time: 391 us -> 387 us (0.990)
    all_to_all x1 -> x0, blocking collectives: 9.95 us -> none  [on_device(): lax.all_to_all(jnp.broadcast_to(back[None], (4, 16, 1280)), 'vocab', 0, 0...]
    all_gather x0 -> x1, blocking collectives: none -> 6.76 us  [on_device(): back = lax.all_gather(back, 'vocab', axis=0, tiled=True)]
where the time goes in v4:
time: 387 us; the launch traced here: 383 us
  Pallas kernels  280 us (72%)
  local copies, waits for them, and re-layouts  40 us (10%)
  starting transfers between devices  28.9 us (7%)
  other arithmetic  17 us (4%)
  waiting for transfers between devices  6.86 us (2%)
  blocking collectives  6.76 us (2%)
    pallas_call x1, Pallas kernels, finish_step(): pl.pallas_call(functools.partial(finish_kernel, sources, pieces, count, w...  97 us
    pallas_call x1, Pallas kernels, start_step(): pl.pallas_call(functools.partial(start_kernel, pieces, count, width), out...  79.1 us
    pallas_call x1, Pallas kernels, head_step(): pl.pallas_call(kernel, out_shape=[jax.ShapeDtypeStruct((16, 768), jnp.flo...  57.7 us
    pallas_call x6, Pallas kernels, local_call(): pl.pallas_call(kernel, name=name, grid=(1,), out_shape=[jax.ShapeDtypeStr...  46.1 us
    all_to_all x1, starting transfers between devices, on_device(): lax.all_to_all(jnp.broadcast_to(query[None], (4, 16, 1024)), 'vocab', 0,...  15.6 us
    unnamed x142, local copies, waits for them, and re-layouts  8.25 us
  transfers between devices with their start and end apart: 4, of which 2 were waited for; matrix products, arithmetic and copies ran while one was open for 6% of the time, Pallas kernels for 2%

profile of v4, /device:TPU:0, one launch (start us, length us, event | category | flops | bytes accessed | tf_op | source)
XLA Modules:
  0.0 383.1 jit_solution(11533870569450021498)
XLA Ops:
  4.9 79.1 %shard_map.535 = (s32[32,4,2,128]{3,2,1,0:T(2,128)S(1)}, bf16[32,24,128]{2,1,0:T(8,128)(2,1)S(1)}, bf16[32,24,512]{2,1,0:T(8,128)(2,1)S(1)}, bf16[2,4,4,2,2,48,7...) custom-call(s32[2,128]{1,0:T(2,128)S(1)} %add_add_fusion.notes_ref, ...), custom_call_target="tpu_custom_call" | custom-call | flops 60000002048 | bytes 200000000 | tf_op jit(solution)/shard_map/pallas_call | solution.py:1010
  85.3 1.5 fusion.21
  96.6 1.6 dynamic-slice_convert_fusion.position_ref
  98.9 5.6 %open_streams.1 = (f32[128,768]{1,0:T(8,128)}, f32[128,192]{1,0:T(8,128)}, bf16[128,768]{1,0:T(8,128)(2,1)}, bf16[128,768]{1,0:T(8,128)(2,1)}, bf16[128,768]{1,0...) custom-call(bf16[32,24,128]{2,1,0:T(8,128)(2,1)} %copy-done.2, ...), custom_call_target="tpu_custom_call" | custom-call | tf_op jit(solution)/shard_map/open_streams/pallas_call | solution.py:507
  104.5 1.4 broadcast_in_dim.33
  105.9 15.6 %all-to-all-start = ((bf16[4,16,1024]{2,1,0:T(8,128)(2,1)}), bf16[4,16,1024]{2,1,0:T(8,128)(2,1)S(1)}, u32[]{:S(2)}, u32[]{:S(2)}) async-start(bf16[4,16,1024]{2,1,0:T(8,128)(2,1)} %broadcast_in_dim.33), calls=%async_computation | async-start | bytes 262144 | tf_op jit(solution)/shard_map/all_to_all | solution.py:1524
  121.5 1.8 slice.135
  124.9 1.8 reshape.303.head_ref
  129.0 3.2 partial_attention.1
  132.3 3.5 all-to-all-start.1
  137.0 5.4 %all-to-all-done.1.parts_ref = f32[4,16,1280]{2,1,0:T(8,128)S(1)} async-done(((f32[4,16,1280]{2,1,0:T(8,128)}), f32[4,16,1280]{2,1,0:T(8,128)S(1)}, u32[]{:S(2)}, u32[]{:S(2)}) %all-to-all-start.1) | async-done | bytes 327712 | tf_op jit(solution)/shard_map/all_to_all | solution.py:1528
  143.2 10.4 %close_streams.1 = (f32[16,768]{1,0:T(8,128)}, f32[16,192]{1,0:T(8,128)}, f32[16,128]{1,0:T(8,128)}, f32[16,768]{1,0:T(8,128)}, f32[16,192]{1,0:T(8,128)}, /*ind...) custom-call(f32[4,16,1280]{2,1,0:T(8,128)} %copy-done.8, ...), custom_call_target="tpu_custom_call" | custom-call | tf_op jit(solution)/shard_map/close_streams/pallas_call | solution.py:507
  153.5 57.7 %shard_map.536 = (f32[16,768]{1,0:T(8,128)}, bf16[768,512]{1,0:T(8,128)(2,1)}, f32[8,128]{1,0:T(8,128)}) custom-call(bf16[16,768]{1,0:T(8,128)(2,1)} %get-tuple-element.111.refs_0_, bf16[768,512]{1,0:T(8,128)(2,1)} %bitcast.128, s32[1,2048]{1,0:T(1,128)} %sub.83.refs_2_, f32[1,2048]{1,0:T(1,128)} %broadcast_divide_fusion.refs_3_, f32[1,2048]{1,0:T(1,128)} %copy-done.29), custom_call_target="tpu_custom_call" | custom-call | tf_op jit(solution)/shard_map/pallas_call | solution.py:739
  211.2 15.5 %close_streams_back.1 = (f32[16,1280]{1,0:T(8,128)}, f32[16,768]{1,0:T(8,128)}, f32[16,192]{1,0:T(8,128)}, bf16[768,960]{1,0:T(8,128)(2,1)}, bf16[768,768]{1,0:T...) custom-call(f32[16,768]{1,0:T(8,128)} %get-tuple-element.114.grad_re, ...), custom_call_target="tpu_custom_call" | custom-call | tf_op jit(solution)/shard_map/close_streams_back/pallas_call | solution.py:507
  226.8 6.8 %all_gather.3.back_ref = f32[64,1280]{1,0:T(8,128)} all-gather(f32[16,1280]{1,0:T(8,128)} %get-tuple-element.126), channel_id=1, replica_groups=mesh['dp'=32,'vocab'=4] {'vocab'}, dimensions={0}, use_global_device_ids=true | all-gather | bytes 409600 | tf_op jit(solution)/shard_map/all_gather | solution.py:1587
  233.5 4.0 %attention_back.1 = (f32[64,1024]{1,0:T(8,128)}, bf16[128,768]{1,0:T(8,128)(2,1)}, bf16[128,768]{1,0:T(8,128)(2,1)}, bf16[128,192]{1,0:T(8,128)(2,1)}, bf16[128,192]{1,0:T(8,128)(2,1)}) custom-call(f32[64,1280]{1,0:T(8,128)} %all_gather.3.back_ref, bf16[64,1024]{1,0:T(8,128)(2,1)} %bitcast.151, bf16[128,768]{1,0:T(8,128)(2,1)} %get-tuple-element.104.key_text, ...), custom_call_target="tpu_custom_call" | custom-call | tf_op jit(solution)/shard_map/attention_back/pallas_call | solution.py:507
  237.6 3.4 all-to-all-start.2
  241.8 1.6 reshape_reshape.43.refs_5_
  247.0 6.4 %all-to-all-start.3 = ((bf16[32,24,512]{2,1,0:T(8,128)(2,1)}), bf16[32,24,512]{2,1,0:T(8,128)(2,1)S(1)}, u32[]{:S(2)}, u32[]{:S(2)}) async-start(bf16[32,24,512]{2,1,0:T(8,128)(2,1)} %bitcast.35), calls=%async_computation.3 | async-start | bytes 1572864 | tf_op jit(solution)/shard_map/all_to_all | solution.py:1561
  253.5 7.4 %open_streams_back.1 = (bf16[768,768]{1,0:T(8,128)(2,1)}, bf16[1536,768]{1,0:T(8,128)(2,1)}, bf16[576,192]{1,0:T(8,128)(2,1)}, bf16[768,128]{1,0:T(8,128)(2,1)},...) custom-call(f32[4,16,1024]{2,1,0:T(8,128)} %copy-done.12, ...), custom_call_target="tpu_custom_call" | custom-call | tf_op jit(solution)/shard_map/open_streams_back/pallas_call | solution.py:507
  266.0 1.6 reshape_reshape.44.refs_6_
  271.6 97.0 %shard_map.537 = (f32[48,768]{1,0:T(8,128)}, f32[24,768]{1,0:T(8,128)}, f32[6,960]{1,0:T(8,128)}, f32[5,960]{1,0:T(8,128)}, f32[12,192]{1,0:T(8,128)}, /*index=5...) custom-call(bf16[1,1,4,2,2,48,768]{6,5,4,3,2,1,0:T(8,128)(2,1)} %bit, ...), custom_call_target="tpu_custom_call" | custom-call | flops 60000002048 | bytes 200000000 | tf_op jit(solution)/shard_map/pallas_call | solution.py:1299
  373.3 1.5 copy.188
  379.6 2.2 multiply_add_fusion
  (234 shorter events, 43.4 us)
Async XLA Ops:
  84.9 41.8 %copy-start.3 = (s32[32,4,2,128]{3,2,1,0:T(2,128)}, s32[32,4,2,128]{3,2,1,0:T(2,128)S(1)}, u32[]{:S(2)}) copy-start(s32[32,4,2,128]{3,2,1,0:T(2,128)S(1)} %get-tuple-element.113.refs_13_) | copy-start | bytes 393220
  105.9 22.5 %all-to-all-start = ((bf16[4,16,1024]{2,1,0:T(8,128)(2,1)}), bf16[4,16,1024]{2,1,0:T(8,128)(2,1)S(1)}, u32[]{:S(2)}, u32[]{:S(2)}) async-start(bf16[4,16,1024]{2,1,0:T(8,128)(2,1)} %broadcast_in_dim.33), calls=%async_computation | async-start | bytes 262144 | tf_op jit(solution)/shard_map/all_to_all | solution.py:1524
  127.0 26.5 %copy-start.29 = (f32[1,2048]{1,0:T(1,128)}, f32[1,2048]{1,0:T(1,128)S(1)}, u32[]{:S(2)}) copy-start(f32[1,2048]{1,0:T(1,128)S(1)} %convert_element_type.118.refs_4_) | copy-start | bytes 24580
  132.3 10.2 %all-to-all-start.1 = ((f32[4,16,1280]{2,1,0:T(8,128)}), f32[4,16,1280]{2,1,0:T(8,128)S(1)}, u32[]{:S(2)}, u32[]{:S(2)}) async-start(f32[4,16,1280]{2,1,0:T(8,128)} %bitcast.147), calls=%async_computation.1 | async-start | bytes 655360 | tf_op jit(solution)/shard_map/all_to_all | solution.py:1528
  226.8 15.0 %copy-start.56 = (f32[3,768]{1,0:T(4,128)S(1)}, f32[3,768]{1,0:T(4,128)}, u32[]{:S(2)}) copy-start(f32[3,768]{1,0:T(4,128)} %get-tuple-element.153) | copy-start | bytes 27652
  226.8 15.0 %copy-start.7 = (bf16[768,960]{1,0:T(8,128)(2,1)S(1)}, bf16[768,960]{1,0:T(8,128)(2,1)}, u32[]{:S(2)}) copy-start(bf16[768,960]{1,0:T(8,128)(2,1)} %get-tuple-element.142) | copy-start | bytes 4423684
  237.6 9.4 %all-to-all-start.2 = ((f32[4,16,1024]{2,1,0:T(8,128)}), f32[4,16,1024]{2,1,0:T(8,128)S(1)}, u32[]{:S(2)}, u32[]{:S(2)}) async-start(f32[4,16,1024]{2,1,0:T(8,128)} %bitcast.157), calls=%async_computation.2 | async-start | bytes 524288 | tf_op jit(solution)/shard_map/all_to_all | solution.py:1600
  247.0 22.7 %all-to-all-start.3 = ((bf16[32,24,512]{2,1,0:T(8,128)(2,1)}), bf16[32,24,512]{2,1,0:T(8,128)(2,1)S(1)}, u32[]{:S(2)}, u32[]{:S(2)}) async-start(bf16[32,24,512]{2,1,0:T(8,128)(2,1)} %bitcast.35), calls=%async_computation.3 | async-start | bytes 1572864 | tf_op jit(solution)/shard_map/all_to_all | solution.py:1561
  271.5 99.1 %copy-start.39 = (f32[2,6,192]{2,0,1:T(2,128)S(1)}, f32[2,6,192]{2,0,1:T(2,128)}, u32[]{:S(2)}) copy-start(f32[2,6,192]{2,0,1:T(2,128)} %param.55) | copy-start | bytes 27652
  271.5 99.1 %copy-start.54 = (f32[2,6,192]{2,0,1:T(2,128)S(1)}, f32[2,6,192]{2,0,1:T(2,128)}, u32[]{:S(2)}) copy-start(f32[2,6,192]{2,0,1:T(2,128)} %param.57) | copy-start | bytes 27652
  271.5 99.1 %copy-start.55 = (f32[2,6,192]{2,0,1:T(2,128)S(1)}, f32[2,6,192]{2,0,1:T(2,128)}, u32[]{:S(2)}) copy-start(f32[2,6,192]{2,0,1:T(2,128)} %param.56) | copy-start | bytes 27652
  271.5 103.4 %copy-start.60 = (f32[123]{0:T(128)S(1)}, f32[123]{0:T(128)}, u32[]{:S(2)}) copy-start(f32[123]{0:T(128)} %param.61) | copy-start | bytes 1480
  271.5 103.4 %copy-start.61 = (f32[123]{0:T(128)S(1)}, f32[123]{0:T(128)}, u32[]{:S(2)}) copy-start(f32[123]{0:T(128)} %param.63) | copy-start | bytes 1480
  271.5 103.4 %copy-start.62 = (f32[123]{0:T(128)S(1)}, f32[123]{0:T(128)}, u32[]{:S(2)}) copy-start(f32[123]{0:T(128)} %param.62) | copy-start | bytes 1480
  271.5 103.9 %copy-start.26 = (f32[960,6]{0,1:T(8,128)S(1)}, f32[960,6]{0,1:T(8,128)}, u32[]{:S(2)}) copy-start(f32[960,6]{0,1:T(8,128)} %param.58) | copy-start | bytes 69124
  271.5 103.9 %copy-start.41 = (f32[960,6]{0,1:T(8,128)S(1)}, f32[960,6]{0,1:T(8,128)}, u32[]{:S(2)}) copy-start(f32[960,6]{0,1:T(8,128)} %param.60) | copy-start | bytes 69124
  271.5 103.9 %copy-start.42 = (f32[960,6]{0,1:T(8,128)S(1)}, f32[960,6]{0,1:T(8,128)}, u32[]{:S(2)}) copy-start(f32[960,6]{0,1:T(8,128)} %param.59) | copy-start | bytes 69124
  271.6 104.5 %copy-start.35 = (f32[192,12]{0,1:T(8,128)S(1)}, f32[192,12]{0,1:T(8,128)}, u32[]{:S(2)}) copy-start(f32[192,12]{0,1:T(8,128)} %param.52) | copy-start | bytes 27652
  271.6 104.5 %copy-start.47 = (f32[192,12]{0,1:T(8,128)S(1)}, f32[192,12]{0,1:T(8,128)}, u32[]{:S(2)}) copy-start(f32[192,12]{0,1:T(8,128)} %param.54) | copy-start | bytes 27652
  271.6 104.5 %copy-start.48 = (f32[192,12]{0,1:T(8,128)S(1)}, f32[192,12]{0,1:T(8,128)}, u32[]{:S(2)}) copy-start(f32[192,12]{0,1:T(8,128)} %param.53) | copy-start | bytes 27652
  271.6 105.1 %copy-start.30 = (f32[24,768]{1,0:T(8,128)S(1)}, f32[24,768]{1,0:T(8,128)}, u32[]{:S(2)}) copy-start(f32[24,768]{1,0:T(8,128)} %param.51) | copy-start | bytes 221188
  271.6 105.1 %copy-start.31 = (f32[24,768]{1,0:T(8,128)S(1)}, f32[24,768]{1,0:T(8,128)}, u32[]{:S(2)}) copy-start(f32[24,768]{1,0:T(8,128)} %param.50) | copy-start | bytes 221188
  271.6 106.7 %copy-start.49 = (f32[4,8,128]{2,1,0:T(8,128)S(1)}, f32[4,8,128]{2,1,0:T(8,128)}, u32[]{:S(2)}) copy-start(f32[4,8,128]{2,1,0:T(8,128)} %param.45) | copy-start | bytes 49156
  271.6 106.7 %copy-start.50 = (f32[4,8,128]{2,1,0:T(8,128)S(1)}, f32[4,8,128]{2,1,0:T(8,128)}, u32[]{:S(2)}) copy-start(f32[4,8,128]{2,1,0:T(8,128)} %param.44) | copy-start | bytes 49156
  (47 other events, 161.5 us)
